TPU v7x, 32 devices: a whole 2x2x4 slice. The times are simulated.
32 devices in a mesh: dp: 4 (over z), fsdp: 8 (over y, x, core).
Axes of the slice: x: 2, y: 2, z: 4, core: 2. Of those that a mesh axis runs over, the one named last changes fastest.
Arguments:
- tokens: bfloat16 [4096, 2304], P(('dp', 'fsdp')), may hold values from -6 to 6
- query_codes: bfloat16 [2304, 2048], P(('dp', 'fsdp')), may hold values from -128 to 127, as said below
- key_codes: bfloat16 [2304, 1024], P(('dp', 'fsdp')), may hold values from -128 to 127, as said below
- value_codes: bfloat16 [2304, 1024], P(('dp', 'fsdp')), may hold values from -128 to 127, as said below
- output_codes: bfloat16 [2048, 2304], P(('dp', 'fsdp')), may hold values from -128 to 127, as said below
- gate_codes: bfloat16 [2304, 9216], P(('dp', 'fsdp')), may hold values from -128 to 127, as said below
- up_codes: bfloat16 [2304, 9216], P(('dp', 'fsdp')), may hold values from -128 to 127, as said below
- down_codes: bfloat16 [9216, 2304], P(('dp', 'fsdp')), may hold values from -128 to 127, as said below
- query_scale: float32 [2048], P(('dp', 'fsdp')), may hold values from 0.00014 to 0.00056
- key_scale: float32 [1024], P(('dp', 'fsdp')), may hold values from 0.00014 to 0.00056
- value_scale: float32 [1024], P(('dp', 'fsdp')), may hold values from 0.00014 to 0.00056
- output_scale: float32 [2304], P(('dp', 'fsdp')), may hold values from 0.00015 to 0.0006
- gate_scale: float32 [9216], P(('dp', 'fsdp')), may hold values from 0.00014 to 0.00056
- up_scale: float32 [9216], P(('dp', 'fsdp')), may hold values from 0.00014 to 0.00056
- down_scale: float32 [2304], P(('dp', 'fsdp')), may hold values from 7e-05 to 0.00028
- pre_attn_gain: float32 [2304], replicated, may hold values from 0.25 to 1.75
- post_attn_gain: float32 [2304], replicated, may hold values from 0.25 to 1.75
- pre_ffw_gain: float32 [2304], replicated, may hold values from 0.25 to 1.75
- post_ffw_gain: float32 [2304], replicated, may hold values from 0.25 to 1.75
- slot_width: int32 [4, 3], P('dp'), may hold values from 0 to 2, as said below
- slot_live: int32 [4, 3], P('dp'), may hold values from 0 to 1, as said below
- cotangent: bfloat16 [3, 4096, 2304], P(None, ('dp', 'fsdp')), may hold values from -6 to 6
Outputs:
- mixed: bfloat16 [3, 4096, 2304], P(None, ('dp', 'fsdp'))
- input_grad: float32 [4096, 2304], P(('dp', 'fsdp'))
- query_grad: float32 [2304, 2048], P(('dp', 'fsdp'))
- key_grad: float32 [2304, 1024], P(('dp', 'fsdp'))
- value_grad: float32 [2304, 1024], P(('dp', 'fsdp'))
- output_grad: float32 [2048, 2304], P(('dp', 'fsdp'))
- gate_grad: float32 [2304, 9216], P(('dp', 'fsdp'))
- up_grad: float32 [2304, 9216], P(('dp', 'fsdp'))
- down_grad: float32 [9216, 2304], P(('dp', 'fsdp'))
- query_scale_grad: float32 [2048], P(('dp', 'fsdp'))
- key_scale_grad: float32 [1024], P(('dp', 'fsdp'))
- value_scale_grad: float32 [1024], P(('dp', 'fsdp'))
- output_scale_grad: float32 [2304], P(('dp', 'fsdp'))
- gate_scale_grad: float32 [9216], P(('dp', 'fsdp'))
- up_scale_grad: float32 [9216], P(('dp', 'fsdp'))
- down_scale_grad: float32 [2304], P(('dp', 'fsdp'))
- pre_attn_gain_grad: float32 [2304], P(('dp', 'fsdp'))
- post_attn_gain_grad: float32 [2304], P(('dp', 'fsdp'))
- pre_ffw_gain_grad: float32 [2304], P(('dp', 'fsdp'))
- post_ffw_gain_grad: float32 [2304], P(('dp', 'fsdp'))
Inputs may be any that keep to these rules, and one draw needn't show every extreme that they name: `query_codes`: whole numbers. `key_codes`: whole numbers. `value_codes`: whole numbers. `output_codes`: whole numbers. `gate_codes`: whole numbers. `up_codes`: whole numbers. `down_codes`: whole numbers. `slot_width`: each row is an ordering of 0, 1 and 2. `slot_live`: each row is a run of ones followed by zeros with at least one one; some row has three ones and some other row exactly one.
All inputs are finite; a program needn't handle non-finite values.
Results may differ from a plain program's by a relative error of at most 0.017.
Values may be sent and summed in bfloat16 or wider, within the bound.
No kernel may reach another device: no remote copies, remote signals or barrier semaphores. Data moves between devices by JAX's collectives and lax.ppermute only.
A program may use at most 1.0625 GiB of HBM per device.

v0:
```python
import jax
import jax.numpy as jnp
from jax import lax
from jax.sharding import PartitionSpec as P

HEADS = 8
KV_HEADS = 4
HD = 256
SLOTS = 3


EPSILON = 1e-06
SOFT_CAP = 50.0


def dequantized(codes, width_index):
    step_size = jnp.where(width_index == 0, 1.0, jnp.where(width_index == 1, 16.0, 64.0)).astype(
        jnp.bfloat16
    )
    return jnp.floor(codes / step_size) * step_size + step_size * jnp.bfloat16(0.5)


def rms_norm(values, gain_vector):
    return (
        values
        * lax.rsqrt(jnp.mean(values * values, axis=-1, keepdims=True) + EPSILON)
        * gain_vector
    )


def rotate(values, positions, heads):
    half_dim = HD // 2
    inv_rates = 10000.0 ** (-jnp.arange(half_dim, dtype=jnp.float32) / half_dim)
    angles = positions.astype(jnp.float32)[:, None] * inv_rates[None, :]
    cosine = jnp.cos(angles)[:, None, :]
    sine_part = jnp.sin(angles)[:, None, :]
    shaped = values.reshape(values.shape[0], heads, HD)
    first_half = shaped[:, :, :half_dim]
    second = shaped[:, :, half_dim:]
    turned = jnp.concatenate(
        [first_half * cosine - second * sine_part, second * cosine + first_half * sine_part],
        axis=-1,
    )
    return turned.reshape(values.shape)


def forward_product(activations, weights):
    return jnp.dot(activations, weights, preferred_element_type=jnp.float32)


def backward_product(gradients, weights):
    return lax.dot_general(
        gradients, weights, (((1,), (1,)), ((), ())), preferred_element_type=jnp.float32
    )


def gated(gate_in, up_in):
    return jax.nn.gelu(gate_in, approximate=True) * up_in


def shards(
    tokens,
    query_codes,
    key_codes,
    value_codes,
    output_codes,
    gate_codes,
    up_codes,
    down_codes,
    query_scale,
    key_scale,
    value_scale,
    output_scale,
    gate_scale,
    up_scale,
    down_scale,
    pre_attn_gain,
    post_attn_gain,
    pre_ffw_gain,
    post_ffw_gain,
    slot_width,
    slot_live,
    cotangent,
):
    scale_list = (
        lax.all_gather(query_scale, ("dp", "fsdp"), axis=0, tiled=True),
        lax.all_gather(key_scale, ("dp", "fsdp"), axis=0, tiled=True),
        lax.all_gather(value_scale, ("dp", "fsdp"), axis=0, tiled=True),
        lax.all_gather(output_scale, ("dp", "fsdp"), axis=0, tiled=True),
        lax.all_gather(gate_scale, ("dp", "fsdp"), axis=0, tiled=True),
        lax.all_gather(up_scale, ("dp", "fsdp"), axis=0, tiled=True),
        lax.all_gather(down_scale, ("dp", "fsdp"), axis=0, tiled=True),
    )
    code_list = (
        lax.all_gather(query_codes, ("dp", "fsdp"), axis=0, tiled=True),
        lax.all_gather(key_codes, ("dp", "fsdp"), axis=0, tiled=True),
        lax.all_gather(value_codes, ("dp", "fsdp"), axis=0, tiled=True),
        lax.all_gather(output_codes, ("dp", "fsdp"), axis=0, tiled=True),
        lax.all_gather(gate_codes, ("dp", "fsdp"), axis=0, tiled=True),
        lax.all_gather(up_codes, ("dp", "fsdp"), axis=0, tiled=True),
        lax.all_gather(down_codes, ("dp", "fsdp"), axis=0, tiled=True),
    )
    gain_list = (pre_attn_gain, post_attn_gain, pre_ffw_gain, post_ffw_gain)
    fsdp_rank = lax.axis_index("fsdp")
    tok_rows = tokens.shape[0]
    length = tok_rows * lax.axis_size("fsdp")
    positions = fsdp_rank * tok_rows + jnp.arange(tok_rows, dtype=jnp.int32)
    causal = positions[:, None] >= jnp.arange(length, dtype=jnp.int32)[None, :]
    group_size = HEADS // KV_HEADS
    inputs = tokens.astype(jnp.float32)

    def turn_queries(values):
        return rotate(values, positions, HEADS) * HD ** (-0.5)

    def turn_keys(values):
        return rotate(values, positions, KV_HEADS)

    outputs = []
    act_rows = [[] for matrix_index in range(7)]
    grad_rows = [[] for matrix_index in range(7)]
    scale_acc = [jnp.zeros(scale_vector.shape, jnp.float32) for scale_vector in scale_list]
    gain_acc = [jnp.zeros(gain_vector.shape, jnp.float32) for gain_vector in gain_list]
    input_total = jnp.zeros(inputs.shape, jnp.float32)
    for slot_index in range(SLOTS):
        width_index = slot_width[0, slot_index]
        live_factor = slot_live[0, slot_index].astype(jnp.float32)
        mats = tuple(
            (dequantized(code_list[matrix_index], width_index) for matrix_index in range(7))
        )
        normed = rms_norm(inputs, gain_list[0]).astype(jnp.bfloat16)
        query_raw = forward_product(normed, mats[0])
        key_raw = forward_product(normed, mats[1])
        value_raw = forward_product(normed, mats[2])
        query_lin = query_raw * scale_list[0]
        key_lin = key_raw * scale_list[1]
        queries = turn_queries(query_lin).astype(jnp.bfloat16)
        keys_own = turn_keys(key_lin).astype(jnp.bfloat16)
        values_own = (value_raw * scale_list[2]).astype(jnp.bfloat16)
        all_keys, all_values = (
            lax.all_gather(keys_own, "fsdp", axis=0, tiled=True),
            lax.all_gather(values_own, "fsdp", axis=0, tiled=True),
        )
        query_heads = queries.reshape(tok_rows, KV_HEADS, group_size, HD)
        key_heads = all_keys.reshape(length, KV_HEADS, HD)
        value_heads = all_values.reshape(length, KV_HEADS, HD)
        scores = jnp.einsum(
            "tgeh,lgh->getl", query_heads, key_heads, preferred_element_type=jnp.float32
        )
        masked = jnp.where(causal, SOFT_CAP * jnp.tanh(scores / SOFT_CAP), -1e30)
        row_max = jnp.max(masked, axis=-1, keepdims=True)
        exp_scores = jnp.exp(masked - row_max)
        row_total = jnp.sum(exp_scores, axis=-1, keepdims=True)
        log_total = row_max + jnp.log(row_total)
        probabilities = (exp_scores / row_total).astype(jnp.bfloat16)
        attended = jnp.einsum(
            "getl,lgh->tgeh", probabilities, value_heads, preferred_element_type=jnp.float32
        )
        attended = attended.reshape(tok_rows, HEADS * HD).astype(jnp.bfloat16)
        out_raw = forward_product(attended, mats[3])
        attn_out = out_raw * scale_list[3]
        middle = inputs + rms_norm(attn_out, gain_list[1])
        normed_two = rms_norm(middle, gain_list[2]).astype(jnp.bfloat16)
        gate_raw = forward_product(normed_two, mats[4])
        up_raw = forward_product(normed_two, mats[5])
        gate_lin = gate_raw * scale_list[4]
        up_lin = up_raw * scale_list[5]
        hidden = gated(gate_lin, up_lin).astype(jnp.bfloat16)
        down_raw = forward_product(hidden, mats[6])
        down_lin = down_raw * scale_list[6]
        result = middle + rms_norm(down_lin, gain_list[3])
        outputs.append((result * live_factor).astype(jnp.bfloat16))
        grad_out = cotangent[slot_index].astype(jnp.float32) * live_factor
        branch_four, pull_four = jax.vjp(rms_norm, down_lin, gain_list[3])
        down_lin_grad, gain_four = pull_four(grad_out)
        scale_acc[6] = scale_acc[6] + jnp.sum(down_raw * down_lin_grad, axis=0)
        down_round = (down_lin_grad * scale_list[6]).astype(jnp.bfloat16)
        hidden_grad = backward_product(down_round, mats[6])
        mix_value, pull_mix = jax.vjp(gated, gate_lin, up_lin)
        gate_lin_grad, up_lin_grad = pull_mix(hidden_grad)
        scale_acc[4] = scale_acc[4] + jnp.sum(gate_raw * gate_lin_grad, axis=0)
        scale_acc[5] = scale_acc[5] + jnp.sum(up_raw * up_lin_grad, axis=0)
        gate_round = (gate_lin_grad * scale_list[4]).astype(jnp.bfloat16)
        up_round = (up_lin_grad * scale_list[5]).astype(jnp.bfloat16)
        normed_two_grad = backward_product(gate_round, mats[4])
        normed_two_grad = normed_two_grad + backward_product(up_round, mats[5])
        branch_three, pull_three = jax.vjp(rms_norm, middle, gain_list[2])
        middle_part, gain_three = pull_three(normed_two_grad)
        middle_grad = grad_out + middle_part
        branch_two, pull_two = jax.vjp(rms_norm, attn_out, gain_list[1])
        attn_out_grad, gain_two = pull_two(middle_grad)
        scale_acc[3] = scale_acc[3] + jnp.sum(out_raw * attn_out_grad, axis=0)
        out_round = (attn_out_grad * scale_list[3]).astype(jnp.bfloat16)
        attended_grad = backward_product(out_round, mats[3]).astype(jnp.bfloat16)
        scores = jnp.einsum(
            "tgeh,lgh->getl", query_heads, key_heads, preferred_element_type=jnp.float32
        )
        tanh_part = jnp.tanh(scores / SOFT_CAP)
        masked = jnp.where(causal, SOFT_CAP * tanh_part, -1e30)
        probs_full = jnp.exp(masked - log_total)
        prob_round = probs_full.astype(jnp.bfloat16)
        grad_heads = attended_grad.reshape(tok_rows, KV_HEADS, group_size, HD)
        prob_grad = jnp.einsum(
            "tgeh,lgh->getl", grad_heads, value_heads, preferred_element_type=jnp.float32
        )
        value_full = jnp.einsum(
            "getl,tgeh->lgh", prob_round, grad_heads, preferred_element_type=jnp.float32
        ).reshape(length, KV_HEADS * HD)
        row_dot = jnp.sum(probs_full * prob_grad, axis=-1, keepdims=True)
        score_grad = (probs_full * (prob_grad - row_dot) * (1.0 - tanh_part * tanh_part)).astype(
            jnp.bfloat16
        )
        query_grad = jnp.einsum(
            "getl,lgh->tgeh", score_grad, key_heads, preferred_element_type=jnp.float32
        ).reshape(tok_rows, HEADS * HD)
        key_full = jnp.einsum(
            "getl,tgeh->lgh", score_grad, query_heads, preferred_element_type=jnp.float32
        ).reshape(length, KV_HEADS * HD)
        key_grad, value_grad = (
            lax.psum_scatter(key_full, "fsdp", scatter_dimension=0, tiled=True),
            lax.psum_scatter(value_full, "fsdp", scatter_dimension=0, tiled=True),
        )
        scale_acc[2] = scale_acc[2] + jnp.sum(value_raw * value_grad, axis=0)
        value_round = (value_grad * scale_list[2]).astype(jnp.bfloat16)
        key_turned, pull_key = jax.vjp(turn_keys, key_lin)
        key_lin_grad = pull_key(key_grad)[0]
        scale_acc[1] = scale_acc[1] + jnp.sum(key_raw * key_lin_grad, axis=0)
        key_round = (key_lin_grad * scale_list[1]).astype(jnp.bfloat16)
        query_turned, pull_query = jax.vjp(turn_queries, query_lin)
        query_lin_grad = pull_query(query_grad)[0]
        scale_acc[0] = scale_acc[0] + jnp.sum(query_raw * query_lin_grad, axis=0)
        query_round = (query_lin_grad * scale_list[0]).astype(jnp.bfloat16)
        normed_grad = backward_product(query_round, mats[0])
        normed_grad = normed_grad + backward_product(key_round, mats[1])
        normed_grad = normed_grad + backward_product(value_round, mats[2])
        branch_one, pull_one = jax.vjp(rms_norm, inputs, gain_list[0])
        input_part, gain_one = pull_one(normed_grad)
        input_total = input_total + middle_grad + input_part
        gain_acc[0] = gain_acc[0] + gain_one
        gain_acc[1] = gain_acc[1] + gain_two
        gain_acc[2] = gain_acc[2] + gain_three
        gain_acc[3] = gain_acc[3] + gain_four
        slot_acts = (normed, normed, normed, attended, normed_two, normed_two, hidden)
        slot_grads = (
            query_round,
            key_round,
            value_round,
            out_round,
            gate_round,
            up_round,
            down_round,
        )
        for matrix_index in range(7):
            act_rows[matrix_index].append(slot_acts[matrix_index])
            grad_rows[matrix_index].append(slot_grads[matrix_index])

    def weight_term(matrix_index):
        return jnp.einsum(
            "ti,to->io",
            jnp.concatenate(act_rows[matrix_index], axis=0),
            jnp.concatenate(grad_rows[matrix_index], axis=0),
            preferred_element_type=jnp.float32,
        )

    ffw_terms = (
        weight_term(4),
        weight_term(5),
        weight_term(6),
        scale_acc[4],
        scale_acc[5],
        scale_acc[6],
    )
    ffw_sums = (
        lax.psum_scatter(ffw_terms[0], ("dp", "fsdp"), scatter_dimension=0, tiled=True),
        lax.psum_scatter(ffw_terms[1], ("dp", "fsdp"), scatter_dimension=0, tiled=True),
        lax.psum_scatter(ffw_terms[2], ("dp", "fsdp"), scatter_dimension=0, tiled=True),
        lax.psum_scatter(ffw_terms[3], ("dp", "fsdp"), scatter_dimension=0, tiled=True),
        lax.psum_scatter(ffw_terms[4], ("dp", "fsdp"), scatter_dimension=0, tiled=True),
        lax.psum_scatter(ffw_terms[5], ("dp", "fsdp"), scatter_dimension=0, tiled=True),
    )
    attn_terms = (
        weight_term(0),
        weight_term(1),
        weight_term(2),
        weight_term(3),
        scale_acc[0],
        scale_acc[1],
        scale_acc[2],
        scale_acc[3],
        gain_acc[0],
        gain_acc[1],
        gain_acc[2],
        gain_acc[3],
    )
    attn_sums = (
        lax.psum_scatter(attn_terms[0], ("dp", "fsdp"), scatter_dimension=0, tiled=True),
        lax.psum_scatter(attn_terms[1], ("dp", "fsdp"), scatter_dimension=0, tiled=True),
        lax.psum_scatter(attn_terms[2], ("dp", "fsdp"), scatter_dimension=0, tiled=True),
        lax.psum_scatter(attn_terms[3], ("dp", "fsdp"), scatter_dimension=0, tiled=True),
        lax.psum_scatter(attn_terms[4], ("dp", "fsdp"), scatter_dimension=0, tiled=True),
        lax.psum_scatter(attn_terms[5], ("dp", "fsdp"), scatter_dimension=0, tiled=True),
        lax.psum_scatter(attn_terms[6], ("dp", "fsdp"), scatter_dimension=0, tiled=True),
        lax.psum_scatter(attn_terms[7], ("dp", "fsdp"), scatter_dimension=0, tiled=True),
        lax.psum_scatter(attn_terms[8], ("dp", "fsdp"), scatter_dimension=0, tiled=True),
        lax.psum_scatter(attn_terms[9], ("dp", "fsdp"), scatter_dimension=0, tiled=True),
        lax.psum_scatter(attn_terms[10], ("dp", "fsdp"), scatter_dimension=0, tiled=True),
        lax.psum_scatter(attn_terms[11], ("dp", "fsdp"), scatter_dimension=0, tiled=True),
    )
    summed_mats = (
        attn_sums[0],
        attn_sums[1],
        attn_sums[2],
        attn_sums[3],
        ffw_sums[0],
        ffw_sums[1],
        ffw_sums[2],
    )
    weight_grads = [
        summed_mats[matrix_index] / scale_list[matrix_index][None, :] for matrix_index in range(7)
    ]
    return (
        jnp.stack(outputs, axis=0),
        input_total,
        weight_grads[0],
        weight_grads[1],
        weight_grads[2],
        weight_grads[3],
        weight_grads[4],
        weight_grads[5],
        weight_grads[6],
        attn_sums[4],
        attn_sums[5],
        attn_sums[6],
        attn_sums[7],
        ffw_sums[3],
        ffw_sums[4],
        ffw_sums[5],
        attn_sums[8],
        attn_sums[9],
        attn_sums[10],
        attn_sums[11],
    )


def solution(mesh):
    in_specs = (
        P(("dp", "fsdp"), None),
        P(("dp", "fsdp"), None),
        P(("dp", "fsdp"), None),
        P(("dp", "fsdp"), None),
        P(("dp", "fsdp"), None),
        P(("dp", "fsdp"), None),
        P(("dp", "fsdp"), None),
        P(("dp", "fsdp"), None),
        P(("dp", "fsdp")),
        P(("dp", "fsdp")),
        P(("dp", "fsdp")),
        P(("dp", "fsdp")),
        P(("dp", "fsdp")),
        P(("dp", "fsdp")),
        P(("dp", "fsdp")),
        P(),
        P(),
        P(),
        P(),
        P("dp", None),
        P("dp", None),
        P(None, ("dp", "fsdp"), None),
    )
    out_specs = (
        P(None, ("dp", "fsdp"), None),
        P(("dp", "fsdp"), None),
        P(("dp", "fsdp"), None),
        P(("dp", "fsdp"), None),
        P(("dp", "fsdp"), None),
        P(("dp", "fsdp"), None),
        P(("dp", "fsdp"), None),
        P(("dp", "fsdp"), None),
        P(("dp", "fsdp"), None),
        P(("dp", "fsdp")),
        P(("dp", "fsdp")),
        P(("dp", "fsdp")),
        P(("dp", "fsdp")),
        P(("dp", "fsdp")),
        P(("dp", "fsdp")),
        P(("dp", "fsdp")),
        P(("dp", "fsdp")),
        P(("dp", "fsdp")),
        P(("dp", "fsdp")),
        P(("dp", "fsdp")),
    )
    return jax.shard_map(shards, mesh=mesh, in_specs=in_specs, out_specs=out_specs, check_vma=False)
```

profile of v0, /device:TPU:0, one launch (start us, length us, event | category | flops | bytes accessed | tf_op | source)
XLA Modules:
  0.0 5068.7 jit_solution(7089700495236750043)
XLA Ops:
  24.5 52.8 %all-gather.14.cloned.1.call-done = bf16[2304,1024]{1,0:T(8,128)(2,1)} async-done(((bf16[72,1024]{1,0:T(8,128)(2,1)}), bf16[2304,1024]{1,0:T(8,128)(2,1)}) %all-gather.14.cloned.1.call-update) | async-done | bytes 4718608 | tf_op jit(solution)/shard_map/all_gather | solution.py:97
  77.3 7.5 multiply_add_fusion.16
  89.3 118.9 %all-reduce.39.cloned.1.call-done = (f32[1024]{0:T(1024)}, f32[2048]{0:T(1024)}, f32[1024]{0:T(1024)}, f32[2304]{0:T(1024)}, f32[9216]{0:T(1024)}, /*index=5*/f32[9216]{0:T(1024)}, f32[2304]{0:T(1024)}) async-done(((f32[1024]{0:T(1024)}, f32[2048]{0:T(1024)}, f32[1024]{0:T(1024)}, f32[2304]{0:T(1024)}, f32[9216]{0:T(1024)}, /*index=5*/f32[9216]{0:T(1024)}, f32[2304]{0:T(1024)}), (f32[1024]{0:T(1024)}, ...) | async-done | bytes 108560
  214.7 61.2 %all-gather.18.cloned.1.call-done = bf16[2304,1024]{1,0:T(8,128)(2,1)} async-done(((bf16[72,1024]{1,0:T(8,128)(2,1)}), bf16[2304,1024]{1,0:T(8,128)(2,1)}) %all-gather.18.cloned.1.call-update) | async-done | bytes 4718608 | tf_op jit(solution)/shard_map/all_gather | solution.py:96
  297.6 7.5 all-gather.36.cloned.1.call-done
  309.7 25.9 all-gather.32.cloned.1.call-done
  338.9 27.1 all-gather.16.cloned.1.call-done
  370.5 80.8 %all-gather.22.cloned.1.call-done = bf16[2304,2048]{1,0:T(8,128)(2,1)} async-done(((bf16[72,2048]{1,0:T(8,128)(2,1)}), bf16[2304,2048]{1,0:T(8,128)(2,1)}) %all-gather.22.cloned.1.call-update) | async-done | bytes 9437200 | tf_op jit(solution)/shard_map/all_gather | solution.py:95
  451.3 10.8 multiply_add_fusion.10
  485.3 26.3 all-gather.38.cloned.1.call-done
  516.2 26.1 all-gather.20.cloned.1.call-done
  542.3 6.8 fusion.72
  560.6 67.1 %all-gather.24.cloned.1.call-done = bf16[2048,2304]{1,0:T(8,128)(2,1)} async-done(((bf16[64,2304]{1,0:T(8,128)(2,1)}), bf16[2048,2304]{1,0:T(8,128)(2,1)}) %all-gather.24.cloned.1.call-update) | async-done | bytes 9437200 | tf_op jit(solution)/shard_map/all_gather | solution.py:98
  627.7 10.8 multiply_add_fusion.9
  654.2 213.0 %all-gather.28.cloned.1.call-done = bf16[2304,9216]{1,0:T(8,128)(2,1)} async-done(((bf16[72,9216]{1,0:T(8,128)(2,1)}), bf16[2304,9216]{1,0:T(8,128)(2,1)}) %all-gather.28.cloned.1.call-update) | async-done | bytes 42467344 | tf_op jit(solution)/shard_map/all_gather | solution.py:100
  867.2 57.3 %multiply_add_fusion.7 = (bf16[2304,9216]{1,0:T(8,128)(2,1)}, bf16[2304,9216]{1,0:T(8,128)(2,1)}, bf16[2304,9216]{1,0:T(8,128)(2,1)}) fusion(bf16[2304,9216]{1,0:T(8,128)(2,1)} %all-gather.28.cloned.1.call-done, bf16[]{:T(256)S(6)} %mul.847, bf16[]{:T(256)} %bitcast, bf16[]{:T(256)S(6)} %mul.955, bf16[]{:T(256)} %bitcast.22, bf16[]{:T(256)S(6)} %mul.910, ...), kind=kLoop, calls=%fused_computation.10 | loop fusion | flops 467140608 | bytes 169869328 | tf_op jit(solution)/shard_map/add | solution.py:20
  924.6 18.4 fusion.272
  943.0 163.5 %all-gather.26.cloned.1.call-done = bf16[2304,9216]{1,0:T(8,128)(2,1)} async-done(((bf16[72,9216]{1,0:T(8,128)(2,1)}), bf16[2304,9216]{1,0:T(8,128)(2,1)}) %all-gather.26.cloned.1.call-update) | async-done | bytes 42467344 | tf_op jit(solution)/shard_map/all_gather | solution.py:99
  1106.5 57.4 %multiply_add_fusion.8 = (bf16[2304,9216]{1,0:T(8,128)(2,1)}, bf16[2304,9216]{1,0:T(8,128)(2,1)}, bf16[2304,9216]{1,0:T(8,128)(2,1)}) fusion(bf16[2304,9216]{1,0:T(8,128)(2,1)} %all-gather.26.cloned.1.call-done, bf16[]{:T(256)S(6)} %mul.847, bf16[]{:T(256)} %bitcast, bf16[]{:T(256)S(6)} %mul.955, bf16[]{:T(256)} %bitcast.22, bf16[]{:T(256)S(6)} %mul.910, ...), kind=kLoop, calls=%fused_computation.11 | loop fusion | flops 467140608 | bytes 169869328 | tf_op jit(solution)/shard_map/add | solution.py:20
  1163.9 18.4 fusion.271
  1182.3 18.4 fusion.268
  1200.7 18.3 fusion.267
  1219.0 24.6 fusion.260
  1243.6 28.0 multiply_convert_fusion.8
  1271.6 74.0 %all-gather.30.cloned.1.call-done = bf16[9216,2304]{1,0:T(8,128)(2,1)} async-done(((bf16[288,2304]{1,0:T(8,128)(2,1)}), bf16[9216,2304]{1,0:T(8,128)(2,1)}) %all-gather.30.cloned.1.call-update) | async-done | bytes 42467344 | tf_op jit(solution)/shard_map/all_gather | solution.py:101
  1345.6 54.3 %multiply_add_fusion.6 = (bf16[9216,2304]{1,0:T(8,128)(2,1)}, bf16[9216,2304]{1,0:T(8,128)(2,1)}, bf16[9216,2304]{1,0:T(8,128)(2,1)}) fusion(bf16[9216,2304]{1,0:T(8,128)(2,1)} %all-gather.30.cloned.1.call-done, bf16[]{:T(256)S(6)} %mul.847, bf16[]{:T(256)} %bitcast, bf16[]{:T(256)S(6)} %mul.955, bf16[]{:T(256)} %bitcast.22, bf16[]{:T(256)S(6)} %mul.910, ...), kind=kLoop, calls=%fused_computation.9 | loop fusion | flops 467140608 | bytes 169869328 | tf_op jit(solution)/shard_map/add | solution.py:20
  1399.9 15.4 fusion.261
  1415.3 18.4 fusion.273
  1433.8 19.4 multiply_reduce_fusion.23
  1459.9 21.2 fusion.279
  1484.4 22.2 fusion.274
  1506.7 39.3 multiply_reduce_fusion.1
  1546.0 8.7 multiply_convert_fusion.1
  1554.7 21.1 fusion.277
  1575.7 21.3 fusion.275
  1597.1 20.7 fusion.280
  1617.8 21.3 convolution_add_fusion.7
  1639.1 21.5 convolution_add_fusion.8
  1660.6 24.0 multiply_reduce_fusion.6
  1703.6 11.9 fusion.70
  1716.2 8.1 convolution_convert_fusion.2
  1728.3 11.7 fusion.66
  1740.7 8.0 convolution_convert_fusion.1
  1754.5 12.1 fusion.68
  1802.4 10.0 fusion.110
  1813.0 11.2 fusion.112
  1830.8 11.8 fusion.111
  1857.4 8.2 fusion.276
  1865.6 7.0 fusion.278
  1885.3 44.0 reduce-scatter.20.cloned.1.call-done
  1931.7 52.7 %reduce-scatter.24.cloned.1.call-done = f32[128,1024]{1,0:T(8,128)} async-done(((f32[1024,1024]{1,0:T(8,128)}), f32[128,1024]{1,0:T(8,128)}) %reduce-scatter.24.cloned.1.call-update) | async-done | bytes 524304 | tf_op jit(solution)/shard_map/reduce_scatter | solution.py:220
  2004.6 34.4 reduce-scatter.28.cloned.1.call-done
  2062.1 9.1 fusion.99
  2073.2 9.0 fusion.88
  2084.2 34.5 fusion.15
  2120.7 34.6 fusion.9
  2157.0 34.6 fusion.3
  2215.7 104.4 %reduce-scatter.34.cloned.1.call-done = f32[72,1024]{1,0:T(8,128)} async-done(((f32[2304,1024]{1,0:T(8,128)}), f32[72,1024]{1,0:T(8,128)}) %reduce-scatter.34.cloned.1.call-update) | async-done | bytes 294928 | tf_op jit(solution)/shard_map/reduce_scatter | solution.py:297
  2321.9 139.9 %reduce-scatter.32.cloned.1.call-done = f32[72,1024]{1,0:T(8,128)} async-done(((f32[2304,1024]{1,0:T(8,128)}), f32[72,1024]{1,0:T(8,128)}) %reduce-scatter.32.cloned.1.call-update) | async-done | bytes 294928 | tf_op jit(solution)/shard_map/reduce_scatter | solution.py:296
  2463.5 210.2 %reduce-scatter.30.cloned.1.call-done = f32[72,2048]{1,0:T(8,128)} async-done(((f32[2304,2048]{1,0:T(8,128)}), f32[72,2048]{1,0:T(8,128)}) %reduce-scatter.30.cloned.1.call-update) | async-done | bytes 589840 | tf_op jit(solution)/shard_map/reduce_scatter | solution.py:295
  2675.7 210.1 %reduce-scatter.36.cloned.1.call-done = f32[64,2304]{1,0:T(8,128)} async-done(((f32[2048,2304]{1,0:T(8,128)}), f32[64,2304]{1,0:T(8,128)}) %reduce-scatter.36.cloned.1.call-update) | async-done | bytes 589840 | tf_op jit(solution)/shard_map/reduce_scatter | solution.py:298
  2887.7 721.6 %reduce-scatter.38.cloned.1.call-done = f32[288,2304]{1,0:T(8,128)} async-done(((f32[9216,2304]{1,0:T(8,128)}), f32[288,2304]{1,0:T(8,128)}) %reduce-scatter.38.cloned.1.call-update) | async-done | bytes 2654224 | tf_op jit(solution)/shard_map/reduce_scatter | solution.py:275
  3612.8 721.4 %reduce-scatter.42.cloned.1.call-done = f32[72,9216]{1,0:T(8,128)} async-done(((f32[2304,9216]{1,0:T(8,128)}), f32[72,9216]{1,0:T(8,128)}) %reduce-scatter.42.cloned.1.call-update) | async-done | bytes 2654224
  4337.7 720.5 %reduce-scatter.40.cloned.1.call-done = f32[72,9216]{1,0:T(8,128)} async-done(((f32[2304,9216]{1,0:T(8,128)}), f32[72,9216]{1,0:T(8,128)}) %reduce-scatter.40.cloned.1.call-update) | async-done | bytes 2654224
  (681 shorter events, 314.8 us)
Async XLA Ops:
  7.2 70.1 %all-gather.14.cloned.1.call-start = ((), (), s32[]{:S(2)}) async-start(), calls=%async_computation.13 | async-start | bytes 4866048 | tf_op jit(solution)/shard_map/all_gather | solution.py:97
  7.9 200.2 %all-reduce.39.cloned.1.call-start = ((), (), s32[]{:S(2)}) async-start(), calls=%async_computation.40 | async-start | bytes 229376
  14.7 261.1 %all-gather.18.cloned.1.call-start = ((), (), s32[]{:S(2)}) async-start(), calls=%async_computation.15 | async-start | bytes 4866048 | tf_op jit(solution)/shard_map/all_gather | solution.py:96
  15.5 289.7 %all-gather.36.cloned.1.call-start = ((), (), s32[]{:S(2)}) async-start(), calls=%async_computation.24 | async-start | bytes 2359296 | tf_op jit(solution)/shard_map/all_gather | solution.py:141
  24.5 444.1 %copy-start.6 = (bf16[128,2304]{1,0:T(8,128)(2,1)}, bf16[128,2304]{1,0:T(8,128)(2,1)S(1)}, u32[]{:S(2)}) copy-start(bf16[128,2304]{1,0:T(8,128)(2,1)S(1)} %fusion.130) | copy-start | bytes 1769476
  87.8 124.5 %copy-start.78 = (f32[128,1024]{1,0:T(8,128)}, f32[128,1024]{1,0:T(8,128)S(1)}, u32[]{:S(2)}) copy-start(f32[128,1024]{1,0:T(8,128)S(1)} %fusion.262) | copy-start | bytes 1572868
  89.3 124.3 %copy-start.80 = (f32[128,1024]{1,0:T(8,128)}, f32[128,1024]{1,0:T(8,128)S(1)}, u32[]{:S(2)}) copy-start(f32[128,1024]{1,0:T(8,128)S(1)} %fusion.257) | copy-start | bytes 1572868
  212.4 123.2 %all-gather.32.cloned.1.call-start = ((), (), s32[]{:S(2)}) async-start(), calls=%async_computation.22 | async-start | bytes 2359296 | tf_op jit(solution)/shard_map/all_gather | solution.py:141
  212.9 153.0 %all-gather.16.cloned.1.call-start = ((), (), s32[]{:S(2)}) async-start(), calls=%async_computation.14 | async-start | bytes 2359296 | tf_op jit(solution)/shard_map/all_gather | solution.py:141
  213.5 237.8 %all-gather.22.cloned.1.call-start = ((), (), s32[]{:S(2)}) async-start(), calls=%async_computation.17 | async-start | bytes 9732096 | tf_op jit(solution)/shard_map/all_gather | solution.py:95
  214.3 266.5 %all-gather.34.cloned.1.call-start = ((), (), s32[]{:S(2)}) async-start(), calls=%async_computation.23 | async-start | bytes 2359296 | tf_op jit(solution)/shard_map/all_gather | solution.py:140
  214.7 260.9 %copy-start.104 = (f32[128,128]{1,0:T(8,128)}, f32[128,128]{1,0:T(8,128)S(1)}, u32[]{:S(2)}) copy-start(f32[128,128]{1,0:T(8,128)S(1)} %get-tuple-element.243) | copy-start | bytes 196612
  214.7 260.9 %copy-start.107 = (f32[128,128]{1,0:T(8,128)}, f32[128,128]{1,0:T(8,128)S(1)}, u32[]{:S(2)}) copy-start(f32[128,128]{1,0:T(8,128)S(1)} %get-tuple-element.244) | copy-start | bytes 196612
  289.9 221.8 %all-gather.38.cloned.1.call-start = ((), (), s32[]{:S(2)}) async-start(), calls=%async_computation.25 | async-start | bytes 2359296 | tf_op jit(solution)/shard_map/all_gather | solution.py:140
  291.0 251.3 %all-gather.20.cloned.1.call-start = ((), (), s32[]{:S(2)}) async-start(), calls=%async_computation.16 | async-start | bytes 2359296 | tf_op jit(solution)/shard_map/all_gather | solution.py:140
  292.3 335.4 %all-gather.24.cloned.1.call-start = ((), (), s32[]{:S(2)}) async-start(), calls=%async_computation.18 | async-start | bytes 9732096 | tf_op jit(solution)/shard_map/all_gather | solution.py:98
  293.0 574.2 %all-gather.28.cloned.1.call-start = ((), (), s32[]{:S(2)}) async-start(), calls=%async_computation.20 | async-start | bytes 43794432 | tf_op jit(solution)/shard_map/all_gather | solution.py:100
  293.6 812.9 %all-gather.26.cloned.1.call-start = ((), (), s32[]{:S(2)}) async-start(), calls=%async_computation.19 | async-start | bytes 43794432 | tf_op jit(solution)/shard_map/all_gather | solution.py:99
  294.3 1051.3 %all-gather.30.cloned.1.call-start = ((), (), s32[]{:S(2)}) async-start(), calls=%async_computation.21 | async-start | bytes 43794432 | tf_op jit(solution)/shard_map/all_gather | solution.py:101
  294.9 1582.0 %reduce-scatter.26.cloned.1.call-start = ((), (), s32[]{:S(2)}) async-start(), calls=%async_computation.30 | async-start | bytes 4718592 | tf_op jit(solution)/shard_map/reduce_scatter | solution.py:219
  297.6 260.2 %copy-start.55 = (pred[128,1024]{0,1:T(8,128)(4,1)}, pred[128,1024]{0,1:T(8,128)(4,1)S(1)}, u32[]{:S(2)}) copy-start(pred[128,1024]{0,1:T(8,128)(4,1)S(1)} %iota_compare_fusion) | copy-start | bytes 393220
  338.9 218.9 %copy-start.57 = (bf16[1024,4,256]{2,1,0:T(4,128)(2,1)}, bf16[1024,4,256]{2,1,0:T(4,128)(2,1)S(1)}, u32[]{:S(2)}) copy-start(bf16[1024,4,256]{2,1,0:T(4,128)(2,1)S(1)} %reshape.533) | copy-start | bytes 6291460
  555.8 89.5 %copy-start.90 = (bf16[4,256,2,128]{3,1,2,0:T(8,128)(2,1)}, bf16[4,256,2,128]{3,1,2,0:T(8,128)(2,1)S(1)}, u32[]{:S(2)}) copy-start(bf16[4,256,2,128]{3,1,2,0:T(8,128)(2,1)S(1)} %fusion.119) | copy-start | bytes 1572868
  557.8 84.4 %copy-start.92 = (bf16[4,256,2,128]{3,1,2,0:T(8,128)(2,1)}, bf16[4,256,2,128]{3,1,2,0:T(8,128)(2,1)S(1)}, u32[]{:S(2)}) copy-start(bf16[4,256,2,128]{3,1,2,0:T(8,128)(2,1)S(1)} %fusion.113) | copy-start | bytes 1572868
  560.6 78.0 %copy-start.94 = (bf16[4,256,2,128]{3,1,2,0:T(8,128)(2,1)S(1)}, bf16[4,256,2,128]{3,1,2,0:T(8,128)(2,1)}, u32[]{:S(2)}) copy-start(bf16[4,256,2,128]{3,1,2,0:T(8,128)(2,1)} %fusion.116) | copy-start | bytes 1572868
  654.2 509.7 %copy-start.31 = (bf16[128,2304]{1,0:T(8,128)(2,1)}, bf16[128,2304]{1,0:T(8,128)(2,1)S(1)}, u32[]{:S(2)}) copy-start(bf16[128,2304]{1,0:T(8,128)(2,1)S(1)} %get-tuple-element.233) | copy-start | bytes 1769476
  654.2 546.5 %copy-start.29 = (bf16[128,2304]{1,0:T(8,128)(2,1)}, bf16[128,2304]{1,0:T(8,128)(2,1)S(1)}, u32[]{:S(2)}) copy-start(bf16[128,2304]{1,0:T(8,128)(2,1)S(1)} %get-tuple-element.232) | copy-start | bytes 1769476
  1271.6 128.3 %copy-start.50 = (bf16[128,9216]{1,0:T(8,128)(2,1)S(1)}, bf16[128,9216]{1,0:T(8,128)(2,1)}, u32[]{:S(2)}) copy-start(bf16[128,9216]{1,0:T(8,128)(2,1)} %get-tuple-element.221) | copy-start | bytes 7077892
  1554.7 42.4 copy-start.26
  1715.5 162.8 %reduce-scatter.18.cloned.1.call-start = ((), (), s32[]{:S(2)}) async-start(), calls=%async_computation.26 | async-start | bytes 4718592 | tf_op jit(solution)/shard_map/reduce_scatter | solution.py:219
  1740.0 139.8 %reduce-scatter.22.cloned.1.call-start = ((), (), s32[]{:S(2)}) async-start(), calls=%async_computation.28 | async-start | bytes 4718592 | tf_op jit(solution)/shard_map/reduce_scatter | solution.py:219
  1766.6 162.7 %reduce-scatter.20.cloned.1.call-start = ((), (), s32[]{:S(2)}) async-start(), calls=%async_computation.27 | async-start | bytes 4718592 | tf_op jit(solution)/shard_map/reduce_scatter | solution.py:220
  1778.1 206.3 %reduce-scatter.24.cloned.1.call-start = ((), (), s32[]{:S(2)}) async-start(), calls=%async_computation.29 | async-start | bytes 4718592 | tf_op jit(solution)/shard_map/reduce_scatter | solution.py:220
  1790.8 248.1 %reduce-scatter.28.cloned.1.call-start = ((), (), s32[]{:S(2)}) async-start(), calls=%async_computation.31 | async-start | bytes 4718592 | tf_op jit(solution)/shard_map/reduce_scatter | solution.py:220
  1851.3 350.2 %all-reduce.37.cloned.1.call-start = ((), (), s32[]{:S(2)}) async-start(), calls=%async_computation.39 | async-start | bytes 327680
  1881.6 47.7 copy-start.81
  1881.6 47.7 copy-start.139
  1881.7 102.7 %copy-start.79 = (f32[128,1024]{1,0:T(8,128)S(1)}, f32[128,1024]{1,0:T(8,128)}, u32[]{:S(2)}) copy-start(f32[128,1024]{1,0:T(8,128)} %copy-done.78) | copy-start | bytes 1572868
  1883.8 109.1 %slice-start.8 = ((s8[4718592]{0:T(1024)(128)(4,1)}), s8[524288]{0:T(1024)(128)(4,1)S(1)}, s32[]{:S(2)}) async-start(s8[4718592]{0:T(1024)(128)(4,1)} %bitcast.492), calls=%async_computation.49 | async-start | bytes 1048576
  1931.7 56.9 %copy-start.83 = (f32[128,2304]{1,0:T(8,128)S(1)}, f32[128,2304]{1,0:T(8,128)}, u32[]{:S(2)}) copy-start(f32[128,2304]{1,0:T(8,128)} %fusion.276) | copy-start | bytes 3538948
  1995.0 46.4 copy-start.42
  2001.8 39.6 copy-start.44
  2001.8 37.2 copy-start.100
  2001.8 38.3 copy-start.175
  2001.8 38.3 copy-start.178
  2001.8 38.9 copy-start.174
  2001.8 38.9 copy-start.176
  2001.9 38.9 copy-start.177
  2001.9 39.5 copy-start.36
  2001.9 39.5 copy-start.134
  2048.3 271.8 %reduce-scatter.34.cloned.1.call-start = ((), (), s32[]{:S(2)}) async-start(), calls=%async_computation.34 | async-start | bytes 9732096 | tf_op jit(solution)/shard_map/reduce_scatter | solution.py:297
  2054.6 407.2 %reduce-scatter.32.cloned.1.call-start = ((), (), s32[]{:S(2)}) async-start(), calls=%async_computation.33 | async-start | bytes 9732096 | tf_op jit(solution)/shard_map/reduce_scatter | solution.py:296
  2060.8 612.9 %reduce-scatter.30.cloned.1.call-start = ((), (), s32[]{:S(2)}) async-start(), calls=%async_computation.32 | async-start | bytes 19464192 | tf_op jit(solution)/shard_map/reduce_scatter | solution.py:295
  2071.3 814.5 %reduce-scatter.36.cloned.1.call-start = ((), (), s32[]{:S(2)}) async-start(), calls=%async_computation.35 | async-start | bytes 19464192 | tf_op jit(solution)/shard_map/reduce_scatter | solution.py:298
  2082.2 1527.1 %reduce-scatter.38.cloned.1.call-start = ((), (), s32[]{:S(2)}) async-start(), calls=%async_computation.36 | async-start | bytes 87588864 | tf_op jit(solution)/shard_map/reduce_scatter | solution.py:275
  2118.7 2215.5 %reduce-scatter.42.cloned.1.call-start = ((), (), s32[]{:S(2)}) async-start(), calls=%async_computation.38 | async-start | bytes 87588864
  2155.3 2902.8 %reduce-scatter.40.cloned.1.call-start = ((), (), s32[]{:S(2)}) async-start(), calls=%async_computation.37 | async-start | bytes 87588864
  2197.4 122.8 %copy-start.140 = (f32[1024]{0:T(1024)S(1)}, f32[1024]{0:T(1024)}, u32[]{:S(2)}) copy-start(f32[1024]{0:T(1024)} %get-tuple-element.95) | copy-start | bytes 12292
  2197.4 264.4 %copy-start.143 = (f32[1024]{0:T(1024)S(1)}, f32[1024]{0:T(1024)}, u32[]{:S(2)}) copy-start(f32[1024]{0:T(1024)} %get-tuple-element.93) | copy-start | bytes 12292
  2197.4 476.3 %copy-start.132 = (f32[2048]{0:T(1024)S(1)}, f32[2048]{0:T(1024)}, u32[]{:S(2)}) copy-start(f32[2048]{0:T(1024)} %get-tuple-element.94) | copy-start | bytes 24580
  2197.4 688.4 %copy-start.122 = (f32[2304]{0:T(1024)S(1)}, f32[2304]{0:T(1024)}, u32[]{:S(2)}) copy-start(f32[2304]{0:T(1024)} %get-tuple-element.96) | copy-start | bytes 27652
  2197.5 1411.9 %copy-start.124 = (f32[2304]{0:T(1024)S(1)}, f32[2304]{0:T(1024)}, u32[]{:S(2)}) copy-start(f32[2304]{0:T(1024)} %get-tuple-element.99) | copy-start | bytes 27652
  2321.9 2012.3 %copy-start.157 = (f32[9216]{0:T(1024)S(1)}, f32[9216]{0:T(1024)}, u32[]{:S(2)}) copy-start(f32[9216]{0:T(1024)} %get-tuple-element.97) | copy-start | bytes 110596
  2887.7 2170.4 %copy-start.127 = (f32[9216]{0:T(1024)S(1)}, f32[9216]{0:T(1024)}, u32[]{:S(2)}) copy-start(f32[9216]{0:T(1024)} %get-tuple-element.98) | copy-start | bytes 110596
  (181 other events, 1187.4 us)
Sparse Core Ops, SparseCore 0:
  10.9 66.3 all-gather.13
  84.9 123.2 all-reduce.38
  211.5 64.3 all-gather.17
  278.4 26.7 all-gather.35
  307.6 27.8 all-gather.31
  338.0 27.8 all-gather.15
  369.3 82.0 all-gather.21
  454.0 26.7 all-gather.33
  483.4 28.1 all-gather.37
  514.1 28.1 all-gather.19
  545.6 82.0 all-gather.23
  630.9 236.3 all-gather.27
  870.5 235.9 all-gather.25
  1109.7 235.9 all-gather.29
  1715.6 49.5 reduce-scatter.25
  1768.5 51.3 reduce-scatter.17
  1823.4 51.2 reduce-scatter.21
  1878.0 51.2 reduce-scatter.19
  1933.0 51.3 reduce-scatter.23
  1987.6 51.3 reduce-scatter.27
  2048.4 129.0 all-reduce.36
  2183.4 136.7 reduce-scatter.33
  2327.1 134.6 reduce-scatter.31
  2468.1 205.6 reduce-scatter.29
  2680.1 205.6 reduce-scatter.35
  2892.1 717.2 reduce-scatter.37
  3616.8 717.3 reduce-scatter.41
  4340.6 717.4 reduce-scatter.39
where the time goes:
time: 5080 us; the launch traced here: 5070 us
  waiting for transfers between devices  3910 us (77%)
  matrix products  724 us (14%)
  other arithmetic  289 us (6%)
  local copies, waits for them, and re-layouts  118 us (2%)
    unnamed x32, waiting for transfers between devices  1570 us
    reduce_scatter x1, waiting for transfers between devices, shards(): lax.psum_scatter(ffw_terms[2], ('dp', 'fsdp'), scatter_dimension=0, tiled...  722 us
    dot_general x21, matrix products, backward_product(): lax.dot_general(gradients, weights, (((1,), (1,)), ((), ())), preferred_e...  274 us
    all_gather x1, waiting for transfers between devices, shards(): lax.all_gather(up_codes, ('dp', 'fsdp'), axis=0, tiled=True)  213 us
    reduce_scatter x1, waiting for transfers between devices, shards(): lax.psum_scatter(attn_terms[0], ('dp', 'fsdp'), scatter_dimension=0, tile...  210 us
    reduce_scatter x1, waiting for transfers between devices, shards(): lax.psum_scatter(attn_terms[3], ('dp', 'fsdp'), scatter_dimension=0, tile...  210 us
    add x7, other arithmetic, dequantized(): jnp.floor(codes / step_size) * step_size + step_size * jnp.bfloat16(0.5)  204 us
    dot_general x21, matrix products, forward_product(): return jnp.dot(activations, weights, preferred_element_type=jnp.float32)  198 us
  transfers between devices with their start and end apart: 28, of which 24 were waited for; matrix products, arithmetic and copies ran while one was open for 14% of the time, Pallas kernels for 0%

commit v1 on v0

v1 whole, which is shorter than its diff:
```python
import functools

import jax
import jax.numpy as jnp
from jax import lax
from jax.experimental import pallas as pl
from jax.experimental.pallas import tpu as pltpu
from jax.sharding import PartitionSpec as P

HEADS = 8
KV_HEADS = 4
HD = 256
HALF = HD // 2
SLOTS = 3
EPSILON = 1e-06
SOFT_CAP = 50.0
BF = jnp.bfloat16
F32 = jnp.float32
ALL = ("dp", "fsdp")
STEPS = (1.0, 16.0, 64.0)
VMEM_LIMIT = 48 * 1024 * 1024


def dequantized(codes, width):
    step = STEPS[width]
    if width == 0:
        return codes + BF(0.5)
    return jnp.floor(codes * BF(1.0 / step)) * BF(step) + BF(step / 2)


def rms_norm(values, gain_vector):
    return (
        values
        * lax.rsqrt(jnp.mean(values * values, axis=-1, keepdims=True) + EPSILON)
        * gain_vector
    )


def rotate(values, cosine, sine_part):
    first_half = values[..., :HALF]
    second = values[..., HALF:]
    return jnp.concatenate(
        [first_half * cosine - second * sine_part, second * cosine + first_half * sine_part],
        axis=-1,
    )


def dot(left, right):
    return jnp.dot(left, right, preferred_element_type=F32)


def dot_nt(left, right):
    return lax.dot_general(left, right, (((1,), (1,)), ((), ())), preferred_element_type=F32)


def dot_tn(left, right):
    return lax.dot_general(left, right, (((0,), (0,)), ((), ())), preferred_element_type=F32)


def gated(gate_in, up_in):
    return jax.nn.gelu(gate_in, approximate=True) * up_in


def score_block(qpos_ref, kpos_ref, q, k):
    tanh_part = jnp.tanh(dot_nt(q, k) * (1.0 / SOFT_CAP))
    causal = qpos_ref[...] >= kpos_ref[...]
    exp_scores = jnp.where(causal, jnp.exp(SOFT_CAP * tanh_part), 0.0)
    total = jnp.sum(exp_scores, axis=-1, keepdims=True)
    return tanh_part, exp_scores / total


def attend_kernel(qpos_ref, kpos_ref, q_ref, k_ref, v_ref, o_ref):
    rows = qpos_ref.shape[0]
    keys = kpos_ref.shape[1]
    k = k_ref[...].reshape(keys, HD)
    v = v_ref[...].reshape(keys, HD)
    _, probs = score_block(qpos_ref, kpos_ref, q_ref[...].reshape(rows, HD), k)
    o_ref[...] = dot(probs.astype(BF), v).astype(BF).reshape(o_ref.shape)


def attend_back_kernel(
    qpos_ref, kpos_ref, q_ref, k_ref, v_ref, do_ref, dq_ref, dk_ref, dv_ref
):
    rows = qpos_ref.shape[0]
    keys = kpos_ref.shape[1]
    q = q_ref[...].reshape(rows, HD)
    k = k_ref[...].reshape(keys, HD)
    v = v_ref[...].reshape(keys, HD)
    do = do_ref[...].reshape(rows, HD)
    tanh_part, probs = score_block(qpos_ref, kpos_ref, q, k)
    prob_grad = dot_nt(do, v)
    row_dot = jnp.sum(probs * prob_grad, axis=-1, keepdims=True)
    score_grad = (probs * (prob_grad - row_dot) * (1.0 - tanh_part * tanh_part)).astype(BF)
    dq_ref[...] = dot(score_grad, k).reshape(dq_ref.shape)
    dk_ref[...] = dot_tn(score_grad, q).reshape(dk_ref.shape)
    dv_ref[...] = dot_tn(probs.astype(BF), do).reshape(dv_ref.shape)


def attention_specs(q, keys):
    widths, _, seqs, rows, _ = q.shape
    groups = keys.shape[1]
    q_spec = pl.BlockSpec((1, 2, 1, rows, HD), lambda w, z: (w, 0, z, 0, 0))
    k_spec = pl.BlockSpec((1, groups, 2, 1, rows, HD), lambda w, z: (w, 0, 0, z, 0, 0))
    qpos_spec = pl.BlockSpec((2 * rows, 1), lambda w, z: (0, 0))
    kpos_spec = pl.BlockSpec((1, groups * 2 * rows), lambda w, z: (0, 0))
    return (widths, seqs), q_spec, k_spec, qpos_spec, kpos_spec


def attention_cost(q, keys, products):
    pairs = q.shape[0] * q.shape[2] * 2 * q.shape[3] * keys.shape[1] * 2 * keys.shape[4]
    return pl.CostEstimate(
        flops=2 * products * pairs * HD, bytes_accessed=2 * q.size + 4 * keys.size, transcendentals=2 * pairs
    )


def attend(qpos, kpos, q, k, v):
    grid, q_spec, k_spec, qpos_spec, kpos_spec = attention_specs(q, k)
    return pl.pallas_call(
        attend_kernel,
        grid=grid,
        in_specs=[qpos_spec, kpos_spec, q_spec, k_spec, k_spec],
        out_specs=q_spec,
        out_shape=jax.ShapeDtypeStruct(q.shape, BF),
        compiler_params=pltpu.CompilerParams(vmem_limit_bytes=VMEM_LIMIT),
        cost_estimate=attention_cost(q, k, 2),
        name="attend",
    )(qpos, kpos, q, k, v)


def attend_back(qpos, kpos, q, k, v, do):
    grid, q_spec, k_spec, qpos_spec, kpos_spec = attention_specs(q, k)
    return pl.pallas_call(
        attend_back_kernel,
        grid=grid,
        in_specs=[qpos_spec, kpos_spec, q_spec, k_spec, k_spec, q_spec],
        out_specs=[q_spec, k_spec, k_spec],
        out_shape=[
            jax.ShapeDtypeStruct(q.shape, F32),
            jax.ShapeDtypeStruct(k.shape, F32),
            jax.ShapeDtypeStruct(k.shape, F32),
        ],
        compiler_params=pltpu.CompilerParams(vmem_limit_bytes=VMEM_LIMIT),
        cost_estimate=attention_cost(q, k, 5),
        name="attend_back",
    )(qpos, kpos, q, k, v, do)


def shards(
    tokens,
    query_codes,
    key_codes,
    value_codes,
    output_codes,
    gate_codes,
    up_codes,
    down_codes,
    query_scale,
    key_scale,
    value_scale,
    output_scale,
    gate_scale,
    up_scale,
    down_scale,
    pre_attn_gain,
    post_attn_gain,
    pre_ffw_gain,
    post_ffw_gain,
    slot_width,
    slot_live,
    cotangent,
):
    planes = lax.axis_size("dp")
    width = lax.axis_size("fsdp")
    devices = planes * width
    zh_count, y_count = planes // 2, width // 4
    dp_rank = lax.axis_index("dp")
    rank = lax.axis_index("fsdp")
    me = dp_rank * width + rank
    zh, zl = dp_rank // 2, dp_rank % 2
    yh, xc = rank // 4, rank % 4
    core = rank % 2
    t_index = zl * 4 + xc
    CORE, X, ZL = 1, 2, width
    zh_masks = [width * 2 * (1 << b) for b in range(zh_count.bit_length() - 1)]
    y_masks = [4 * (1 << b) for b in range(y_count.bit_length() - 1)]

    def swap(values, mask):
        return lax.ppermute(values, ALL, [(i, i ^ mask) for i in range(devices)])

    tok_rows, model = tokens.shape
    group_rows = 8 * tok_rows
    d_rows = query_codes.shape[0]
    o_rows = output_codes.shape[0]
    ff_rows = down_codes.shape[0]
    q_cols = query_codes.shape[1] // 8
    k_cols = key_codes.shape[1] // 8
    ff_cols = ff_rows * zh_count * y_count
    half = model // 2
    widths = range(SLOTS)

    def tp_gather(block):
        first, second = block[:, :half], block[:, half:]
        first_z = swap(first, ZL)
        second_x = swap(second, X)
        first_x = swap(jnp.stack([first, first_z]), X)
        second_z = swap(jnp.stack([second, second_x]), ZL)
        same = jnp.concatenate(
            [
                block,
                jnp.concatenate([first_x[0], second_x], axis=1),
                jnp.concatenate([first_z, second_z[0]], axis=1),
                jnp.concatenate([first_x[1], second_z[1]], axis=1),
            ],
            axis=0,
        )
        return jnp.concatenate([same, swap(same, CORE)], axis=0)

    def tp_scatter(partial):
        low = partial.astype(BF).reshape(2, 2, 2, tok_rows, model)
        pair = (low[0].astype(F32) + swap(low[1], CORE).astype(F32)).astype(BF)
        got_x = swap(pair[:, 1, :, :half], X)
        got_z = swap(pair[1, :, :, half:], ZL)
        first = (pair[:, 0, :, :half].astype(F32) + got_x.astype(F32)).astype(BF)
        second = (pair[0, :, :, half:].astype(F32) + got_z.astype(F32)).astype(BF)
        last_z = swap(first[1], ZL)
        last_x = swap(second[1], X)
        return jnp.concatenate(
            [
                first[0].astype(F32) + last_z.astype(F32),
                second[0].astype(F32) + last_x.astype(F32),
            ],
            axis=1,
        )

    def tp_columns(blocks):
        result = jnp.zeros_like(blocks)
        for m in range(8):
            mask = (m & 3) + (width if m & 4 else 0)
            block = lax.dynamic_index_in_dim(blocks, t_index ^ m, 0, keepdims=False)
            moved = block if m == 0 else swap(block, mask)
            result = lax.dynamic_update_index_in_dim(result, moved, t_index ^ m, 0)
        return result

    def weight_gather(shard, place):
        parts = {0: shard}
        for mask in zh_masks + y_masks:
            for key in list(parts):
                parts[key ^ mask] = swap(parts[key], mask)
        return parts

    def from_parts(parts, key):
        other = me ^ key
        other_dp, other_rank = other // width, other % width
        return other_dp // 2, other_rank // 4

    def gather_rows(shard):
        parts = weight_gather(shard, None)
        rows, cols = shard.shape[1], shard.shape[2]
        result = jnp.zeros((zh_count, 2, y_count, 4 * rows, cols), shard.dtype)
        for key, part in parts.items():
            z, y = from_parts(parts, key)
            result = lax.dynamic_update_slice(
                result, part.reshape(1, 2, 1, 4 * rows, cols), (z, 0, y, 0, 0)
            )
        return result.reshape(devices * rows, cols)

    def gather_blocks(shard):
        parts = weight_gather(shard, None)
        rows, cols = shard.shape
        result = jnp.zeros((zh_count, y_count, rows, cols), shard.dtype)
        for key, part in parts.items():
            z, y = from_parts(parts, key)
            result = lax.dynamic_update_slice(result, part[None, None], (z, y, 0, 0))
        return result

    def weight_scatter(values, z_axis, y_axis):
        for axis, masks, place in ((y_axis, y_masks, yh), (z_axis, zh_masks, zh)):
            for bit in reversed(range(len(masks))):
                keep = values.shape[axis] // 2
                side = (place >> bit) & 1
                gone = lax.dynamic_slice_in_dim(values, (1 - side) * keep, keep, axis)
                kept = lax.dynamic_slice_in_dim(values, side * keep, keep, axis)
                values = (kept.astype(F32) + swap(gone, masks[bit]).astype(F32)).astype(BF)
        return values

    def scatter_rows(grad):
        rows, cols = grad.shape[0] // devices, grad.shape[1]
        values = grad.reshape(zh_count, 2, y_count, 4 * rows, cols)
        return weight_scatter(values, 0, 2).reshape(8, rows, cols)

    small = jnp.concatenate(
        [query_scale, key_scale, value_scale, output_scale, gate_scale, up_scale, down_scale]
    )
    all_small = small[None]
    for bit in range(devices.bit_length() - 1):
        all_small = jnp.concatenate([all_small, swap(all_small, 1 << bit)], axis=0)
    order = jnp.arange(devices, dtype=jnp.int32) ^ me
    all_small = all_small[order]
    cuts = []
    at = 0
    for vector in (
        query_scale,
        key_scale,
        value_scale,
        output_scale,
        gate_scale,
        up_scale,
        down_scale,
    ):
        cuts.append(all_small[:, at : at + vector.shape[0]].reshape(-1))
        at += vector.shape[0]
    q_scale_all, k_scale_all, v_scale_all, o_scale_all, g_scale_all, u_scale_all, d_scale_all = cuts

    head = (xc // 2) * 4 + zl * 2 + core
    kv_half = head

    def own_ff(vector):
        cut = vector.reshape(zh_count, 2, y_count, 4, ff_rows)
        cut = lax.dynamic_slice(cut, (0, zl, 0, xc, 0), (zh_count, 1, y_count, 1, ff_rows))
        return cut.reshape(ff_cols)

    qkv_scale = jnp.concatenate(
        [
            lax.dynamic_slice_in_dim(q_scale_all, head * q_cols, q_cols),
            lax.dynamic_slice_in_dim(k_scale_all, kv_half * k_cols, k_cols),
            lax.dynamic_slice_in_dim(v_scale_all, kv_half * k_cols, k_cols),
        ]
    )
    g_scale = own_ff(g_scale_all)
    u_scale = own_ff(u_scale_all)

    def by_head(codes):
        cut = codes.reshape(codes.shape[0], 2, 2, 2, -1)
        return cut.transpose(2, 1, 3, 0, 4).reshape(8, codes.shape[0], -1)

    def by_head_back(blocks):
        cut = blocks.reshape(2, 2, 2, blocks.shape[1], blocks.shape[2])
        return cut.transpose(3, 1, 0, 2, 4).reshape(blocks.shape[1], -1)

    def by_ff(codes):
        cut = codes.reshape(d_rows, zh_count, 2, y_count, 4, ff_rows)
        return cut.transpose(2, 4, 0, 1, 3, 5).reshape(8, d_rows, ff_cols)

    def by_ff_back(blocks):
        cut = blocks.reshape(2, 4, d_rows, zh_count, y_count, ff_rows)
        return cut.transpose(2, 3, 0, 4, 1, 5).reshape(d_rows, 8 * ff_cols)

    qkv_blocks = jnp.concatenate(
        [by_head(query_codes), by_head(key_codes), by_head(value_codes)], axis=2
    )
    inputs = tokens.astype(F32)
    normed = tp_gather(rms_norm(inputs, pre_attn_gain).astype(BF))
    qkv_codes = gather_rows(tp_columns(qkv_blocks))

    def quarter_swap(blocks):
        result = jnp.zeros_like(blocks)
        for m in range(4):
            block = lax.dynamic_index_in_dim(blocks, xc ^ m, 0, keepdims=False)
            moved = block if m == 0 else swap(block, m)
            result = lax.dynamic_update_index_in_dim(result, moved, xc ^ m, 0)
        return result

    whole_heads = zh_count == 2 and y_count == 2
    if whole_heads:
        parts = gather_blocks(output_codes).reshape(4, o_rows, model)
        out_codes = quarter_swap(parts).reshape(HD, model)
    else:
        every = lax.all_gather(output_codes, ALL, axis=0, tiled=True)
        out_codes = lax.dynamic_slice_in_dim(every, head * HD, HD, 0)

    gate_codes_t = gather_rows(tp_columns(by_ff(gate_codes)))
    up_codes_t = gather_rows(tp_columns(by_ff(up_codes)))
    down_codes_t = gather_blocks(down_codes).reshape(ff_cols, model)

    offsets = jnp.arange(tok_rows, dtype=jnp.int32)
    blocks_at = jnp.stack([jnp.stack([xc ^ (c + 2 * x) for x in range(2)]) for c in range(2)])
    q_positions = ((yh * 4 + blocks_at) * tok_rows)[:, :, None] + offsets
    q_positions = q_positions.reshape(4 * tok_rows)
    seq_rows = 4 * tok_rows
    far = jnp.int32(1 << 30)
    key_positions = []
    for back in range(y_count):
        positions = q_positions - back * seq_rows
        key_positions.append(jnp.where(positions >= 0, positions, far))
    kpos = jnp.concatenate(key_positions)[None, :]
    qpos = q_positions[:, None]
    inv_rates = 10000.0 ** (-jnp.arange(HALF, dtype=F32) / HALF)
    angles = q_positions.astype(F32)[:, None] * inv_rates[None, :]
    cosine = jnp.cos(angles).reshape(2, 1, 2 * tok_rows, HALF)
    sine = jnp.sin(angles).reshape(2, 1, 2 * tok_rows, HALF)
    q_factor = HD ** (-0.5)
    rows_shape = (SLOTS, 2, 2, 2 * tok_rows)

    qkv_w = [dequantized(qkv_codes, w) for w in widths]
    qkv_raw = [dot(normed, qkv_w[w]) for w in widths]
    qkv_lin = jnp.stack([raw * qkv_scale for raw in qkv_raw]).reshape(
        SLOTS, 2, 2, 2 * tok_rows, q_cols + 2 * k_cols
    )
    q = (rotate(qkv_lin[..., :q_cols], cosine, sine) * q_factor).astype(BF)
    kv_own = qkv_lin[..., q_cols:]
    kv_other = swap(kv_own, CORE)[:, ::-1]
    first_core = core == 0

    def both(own, other):
        return jnp.concatenate(
            [jnp.where(first_core, own, other), jnp.where(first_core, other, own)], axis=-1
        )

    k_near = rotate(both(kv_own[..., :k_cols], kv_other[..., :k_cols]), cosine, sine).astype(BF)
    v_near = both(kv_own[..., k_cols:], kv_other[..., k_cols:]).astype(BF)

    def own_half(values):
        return lax.dynamic_slice_in_dim(values, core * k_cols, k_cols, values.ndim - 1)

    kv_near = jnp.concatenate([own_half(k_near), own_half(v_near)], axis=-1)
    k_parts, v_parts = [k_near], [v_near]

    def back_pairs(back):
        return [(i, i + 4 * back) for i in range(devices) if (i % width) + 4 * back < width]

    for back in range(1, y_count):
        mine = lax.ppermute(kv_near, ALL, back_pairs(back))
        other = swap(mine, CORE)[:, ::-1]
        k_parts.append(both(mine[..., :k_cols], other[..., :k_cols]))
        v_parts.append(both(mine[..., k_cols:], other[..., k_cols:]))
    k_all = jnp.stack(k_parts, axis=1)
    v_all = jnp.stack(v_parts, axis=1)
    attended = attend(qpos, kpos, q, k_all, v_all)
    o_flat = attended.reshape(SLOTS, group_rows, HD)

    slot_of = []
    for w in widths:
        slot = jnp.int32(0)
        for s in range(SLOTS):
            slot = jnp.where(slot_width[0, s] == w, s, slot)
        slot_of.append(slot)
    kept = [dict() for w in widths]
    for w in widths:
        k = kept[w]
        k["out_w"] = dequantized(out_codes, w)
        k["out_raw"] = tp_scatter(dot(o_flat[w], k["out_w"]))
        k["attn_out"] = k["out_raw"] * o_scale_all
        k["middle"] = inputs + rms_norm(k["attn_out"], post_attn_gain)
        k["normed_two"] = tp_gather(rms_norm(k["middle"], pre_ffw_gain).astype(BF))
    for w in widths:
        k = kept[w]
        k["gate_w"] = dequantized(gate_codes_t, w)
        k["up_w"] = dequantized(up_codes_t, w)
        k["gate_raw"] = dot(k["normed_two"], k["gate_w"])
        k["up_raw"] = dot(k["normed_two"], k["up_w"])
        k["hidden"] = gated(k["gate_raw"] * g_scale, k["up_raw"] * u_scale).astype(BF)
    for w in widths:
        k = kept[w]
        k["down_w"] = dequantized(down_codes_t, w)
        k["down_raw"] = tp_scatter(dot(k["hidden"], k["down_w"]))

    mixed = jnp.zeros((SLOTS, tok_rows, model), BF)
    out_scale_acc = jnp.zeros((model,), F32)
    down_scale_acc = jnp.zeros((model,), F32)
    gate_scale_acc = jnp.zeros((ff_cols,), F32)
    up_scale_acc = jnp.zeros((ff_cols,), F32)
    gains = [jnp.zeros((model,), F32) for g in range(4)]
    input_total = jnp.zeros(inputs.shape, F32)
    for w in widths:
        k = kept[w]
        live = lax.dynamic_index_in_dim(slot_live[0], slot_of[w], 0, keepdims=False).astype(F32)
        down_lin = k["down_raw"] * d_scale_all
        branch, pull_four = jax.vjp(rms_norm, down_lin, post_ffw_gain)
        result = ((k["middle"] + branch) * live).astype(BF)
        mixed = lax.dynamic_update_index_in_dim(mixed, result, slot_of[w], 0)
        cot = lax.dynamic_index_in_dim(cotangent, slot_of[w], 0, keepdims=False)
        k["grad_out"] = cot.astype(F32) * live
        down_lin_grad, gain_four = pull_four(k["grad_out"])
        gains[3] = gains[3] + gain_four
        down_scale_acc = down_scale_acc + jnp.sum(k["down_raw"] * down_lin_grad, axis=0)
        k["down_round"] = tp_gather((down_lin_grad * d_scale_all).astype(BF))
    down_sum = dot_tn(
        jnp.concatenate([kept[w]["hidden"] for w in widths], axis=0),
        jnp.concatenate([kept[w]["down_round"] for w in widths], axis=0),
    )
    down_sum = weight_scatter(
        (down_sum / d_scale_all).astype(BF).reshape(zh_count, y_count, ff_rows, model), 0, 1
    )
    for w in widths:
        k = kept[w]
        hidden_grad = dot_nt(k["down_round"], k["down_w"])
        _, pull_mix = jax.vjp(gated, k["gate_raw"] * g_scale, k["up_raw"] * u_scale)
        gate_grad, up_grad = pull_mix(hidden_grad)
        gate_scale_acc = gate_scale_acc + jnp.sum(k["gate_raw"] * gate_grad, axis=0)
        up_scale_acc = up_scale_acc + jnp.sum(k["up_raw"] * up_grad, axis=0)
        k["gate_round"] = (gate_grad * g_scale).astype(BF)
        k["up_round"] = (up_grad * u_scale).astype(BF)
        k["two_grad"] = tp_scatter(
            dot_nt(k["gate_round"], k["gate_w"]) + dot_nt(k["up_round"], k["up_w"])
        )
    normed_two_rows = jnp.concatenate([kept[w]["normed_two"] for w in widths], axis=0)
    gate_sum = dot_tn(
        normed_two_rows, jnp.concatenate([kept[w]["gate_round"] for w in widths], axis=0)
    )
    gate_sum = scatter_rows((gate_sum / g_scale).astype(BF))
    up_sum = dot_tn(
        normed_two_rows, jnp.concatenate([kept[w]["up_round"] for w in widths], axis=0)
    )
    up_sum = scatter_rows((up_sum / u_scale).astype(BF))
    for w in widths:
        k = kept[w]
        _, pull_three = jax.vjp(rms_norm, k["middle"], pre_ffw_gain)
        middle_part, gain_three = pull_three(k["two_grad"])
        gains[2] = gains[2] + gain_three
        middle_grad = k["grad_out"] + middle_part
        _, pull_two = jax.vjp(rms_norm, k["attn_out"], post_attn_gain)
        attn_out_grad, gain_two = pull_two(middle_grad)
        gains[1] = gains[1] + gain_two
        out_scale_acc = out_scale_acc + jnp.sum(k["out_raw"] * attn_out_grad, axis=0)
        k["out_round"] = tp_gather((attn_out_grad * o_scale_all).astype(BF))
        k["o_grad"] = dot_nt(k["out_round"], k["out_w"]).astype(BF)
        input_total = input_total + middle_grad
    out_sum = dot_tn(
        o_flat.reshape(SLOTS * group_rows, HD),
        jnp.concatenate([kept[w]["out_round"] for w in widths], axis=0),
    )
    out_sum = (out_sum / o_scale_all).astype(BF)
    if whole_heads:
        out_blocks = quarter_swap(out_sum.reshape(4, o_rows, model))
        out_sum = weight_scatter(out_blocks.reshape(2, 2, o_rows, model), 0, 1)
    else:
        whole = jnp.zeros((HEADS * HD, model), BF)
        whole = lax.dynamic_update_slice_in_dim(whole, out_sum, head * HD, 0)
        out_sum = lax.psum_scatter(whole, ALL, scatter_dimension=0, tiled=True)

    o_grad = jnp.stack([kept[w]["o_grad"] for w in widths]).reshape(q.shape)
    dq, dk, dv = attend_back(qpos, kpos, q, k_all, v_all, o_grad)
    q_grad = rotate(dq * q_factor, cosine, -sine)
    far_cos = jnp.stack([jnp.cos((q_positions - b * seq_rows).astype(F32)[:, None] * inv_rates) for b in range(y_count)])
    far_sin = jnp.stack([jnp.sin((q_positions - b * seq_rows).astype(F32)[:, None] * inv_rates) for b in range(y_count)])
    far_shape = (y_count, 2, 1, 2 * tok_rows, HALF)
    dk = rotate(dk, far_cos.reshape(far_shape), -far_sin.reshape(far_shape))
    other = 1 - core

    def half_of(values, which):
        return lax.dynamic_slice_in_dim(values, which * k_cols, k_cols, values.ndim - 1)

    dkv = jnp.concatenate([half_of(dk, core), half_of(dv, core)], axis=-1)
    dkv_gone = jnp.concatenate([half_of(dk, other), half_of(dv, other)], axis=-1)
    dkv = dkv + swap(dkv_gone, CORE)[:, :, ::-1]
    kv_grad = dkv[:, 0]
    for back in range(1, y_count):
        pairs = [(b, a) for a, b in back_pairs(back)]
        kv_grad = kv_grad + lax.ppermute(dkv[:, back].astype(BF), ALL, pairs).astype(F32)
    qkv_grad = jnp.concatenate([q_grad, kv_grad], axis=-1).reshape(SLOTS, group_rows, -1)
    qkv_round = [(qkv_grad[w] * qkv_scale).astype(BF) for w in widths]
    qkv_scale_acc = sum(jnp.sum(qkv_raw[w] * qkv_grad[w], axis=0) for w in widths)
    qkv_rows = sum(qkv_round[w].astype(F32) for w in widths).astype(BF)
    normed_grad = tp_scatter(sum(dot_nt(qkv_round[w], qkv_w[w]) for w in widths))
    qkv_sum = scatter_rows((dot_tn(normed, qkv_rows) / qkv_scale).astype(BF))
    _, pull_one = jax.vjp(rms_norm, inputs, pre_attn_gain)
    input_part, gains[0] = pull_one(normed_grad)
    input_total = input_total + input_part

    down_grad = down_sum.reshape(ff_rows, model).astype(F32)
    gate_grad = by_ff_back(tp_columns(gate_sum)).astype(F32)
    up_grad = by_ff_back(tp_columns(up_sum)).astype(F32)
    output_grad = out_sum.reshape(o_rows, model).astype(F32)
    qkv_back = tp_columns(qkv_sum)
    query_grad = by_head_back(qkv_back[:, :, :q_cols]).astype(F32)
    key_grad = by_head_back(qkv_back[:, :, q_cols : q_cols + k_cols]).astype(F32)
    value_grad = by_head_back(qkv_back[:, :, q_cols + k_cols :]).astype(F32)

    def placed(part, count):
        whole = jnp.zeros((8 * count,), F32)
        return lax.dynamic_update_slice_in_dim(whole, part, head * count, 0)

    def placed_ff(part):
        whole = jnp.zeros((zh_count, 2, y_count, 4, ff_rows), F32)
        block = part.reshape(zh_count, 1, y_count, 1, ff_rows)
        return lax.dynamic_update_slice(whole, block, (0, zl, 0, xc, 0)).reshape(-1)

    vectors = [
        placed(qkv_scale_acc[:q_cols], q_cols),
        placed(qkv_scale_acc[q_cols : q_cols + k_cols], k_cols),
        placed(qkv_scale_acc[q_cols + k_cols :], k_cols),
        out_scale_acc,
        placed_ff(gate_scale_acc),
        placed_ff(up_scale_acc),
        down_scale_acc,
    ] + gains
    summed = jnp.concatenate([v.reshape(devices, -1) for v in vectors], axis=1)[order]
    for bit in reversed(range(devices.bit_length() - 1)):
        keep = 1 << bit
        summed = summed[:keep] + swap(summed[keep:], keep)
    summed = summed[0]
    vector_grads = []
    at = 0
    for v in vectors:
        size = v.shape[0] // devices
        vector_grads.append(summed[at : at + size])
        at += size

    return (
        mixed,
        input_total,
        query_grad,
        key_grad,
        value_grad,
        output_grad,
        gate_grad,
        up_grad,
        down_grad,
        *vector_grads,
    )


def solution(mesh):
    rows = P(ALL, None)
    vector = P(ALL)
    in_specs = (
        (rows,) * 8
        + (vector,) * 7
        + (P(),) * 4
        + (P("dp", None), P("dp", None), P(None, ALL, None))
    )
    out_specs = (P(None, ALL, None),) + (rows,) * 8 + (vector,) * 11
    return jax.shard_map(shards, mesh=mesh, in_specs=in_specs, out_specs=out_specs, check_vma=False)
```

time: 5080 us -> 2000 us (0.39)
  waiting for transfers between devices: 3910 us -> 976 us
  matrix products: 724 us -> 320 us
  starting transfers between devices: 2.3 us -> 159 us
  local copies, waits for them, and re-layouts: 118 us -> 216 us
    unnamed x32 -> x0, waiting for transfers between devices: 1570 us -> none
    reduce_scatter x11 -> x0, waiting for transfers between devices: 1520 us -> none  [the longest x1 722 us: shards(): lax.psum_scatter(ffw_terms[2], ('dp', 'fsdp'), scatter_dimension=0, tiled...]
    ppermute x0 -> x188, waiting for transfers between devices: none -> 976 us  [the longest x186 874 us: swap(): return lax.ppermute(values, ALL, [(i, i ^ mask) for i in range(devices)])]
    all_gather x13 -> x0, waiting for transfers between devices: 829 us -> none  [the longest x1 213 us: shards(): lax.all_gather(up_codes, ('dp', 'fsdp'), axis=0, tiled=True)]
    dot_general x67 -> x35, matrix products: 724 us -> 320 us  [the longest x15 140 us: dot_nt(): lax.dot_general(left, right, (((1,), (1,)), ((), ())), preferred_element_...]
    add x20 -> x41, other arithmetic: 214 us -> 29.1 us  [the longest x3 17.7 us: dequantized(): return jnp.floor(codes * BF(1.0 / step)) * BF(step) + BF(step / 2)]
    ppermute x0 -> x188, starting transfers between devices: none -> 159 us  [the longest x186 155 us: swap(): return lax.ppermute(values, ALL, [(i, i ^ mask) for i in range(devices)])]
    concatenate x0 -> x21, other arithmetic: none -> 128 us  [the longest x10 124 us: tp_gather(): jnp.concatenate([block, jnp.concatenate([first_x[0], second_x], axis=1),...]
  transfers between devices with their start and end apart: 28 -> 188, of which waited for: 24 -> 111; matrix products, arithmetic and copies ran while one was open for 14% -> 29% of each run, Pallas kernels for 0% -> 1%
where the time goes in v1:
time: 2000 us; the launch traced here: 1990 us
  waiting for transfers between devices  976 us (49%)
  matrix products  320 us (16%)
  other arithmetic  280 us (14%)
  local copies, waits for them, and re-layouts  216 us (11%)
  starting transfers between devices  159 us (8%)
  Pallas kernels  27.8 us (1%)
    ppermute x186, waiting for transfers between devices, swap(): return lax.ppermute(values, ALL, [(i, i ^ mask) for i in range(devices)])  874 us
    ppermute x186, starting transfers between devices, swap(): return lax.ppermute(values, ALL, [(i, i ^ mask) for i in range(devices)])  155 us
    dot_general x15, matrix products, dot_nt(): lax.dot_general(left, right, (((1,), (1,)), ((), ())), preferred_element_...  140 us
    concatenate x10, other arithmetic, tp_gather(): jnp.concatenate([block, jnp.concatenate([first_x[0], second_x], axis=1),...  124 us
    dot_general x15, matrix products, dot(): return jnp.dot(left, right, preferred_element_type=F32)  101 us
    ppermute x1, waiting for transfers between devices, shards(): mine = lax.ppermute(kv_near, ALL, back_pairs(back))  86.1 us
    dot_general x5, matrix products, dot_tn(): lax.dot_general(left, right, (((0,), (0,)), ((), ())), preferred_element_...  79.2 us
  transfers between devices with their start and end apart: 188, of which 111 were waited for; matrix products, arithmetic and copies ran while one was open for 29% of the time, Pallas kernels for 1%

profile of v1, /device:TPU:0, one launch (start us, length us, event | category | flops | bytes accessed | tf_op | source)
XLA Modules:
  0.0 1990.9 jit_solution(6714015500844065481)
XLA Ops:
  70.6 17.5 collective-permute-done.8
  88.1 31.2 %collective-permute-done.9 = bf16[72,512]{1,0:T(8,128)(2,1)S(1)} collective-permute-done((bf16[72,512]{1,0:T(8,128)(2,1)S(1)}, bf16[72,512]{1,0:T(8,128)(2,1)S(1)}, u32[]{:S(2)}, u32[]{:S(2)}) %collective-permute-start.9) | collective-permute-done | bytes 73760 | tf_op jit(solution)/shard_map/ppermute | solution.py:188
  235.2 13.8 collective-permute-done.25
  252.9 8.0 collective-permute-done.12
  264.3 12.9 collective-permute-done.3
  277.3 12.9 maximum_maximum_fusion
  291.5 14.7 collective-permute-done.14
  333.2 89.5 %collective-permute-done.56 = bf16[8,72,1152]{2,1,0:T(8,128)(2,1)} collective-permute-done((bf16[8,72,1152]{2,1,0:T(8,128)(2,1)S(1)}, bf16[8,72,1152]{2,1,0:T(8,128)(2,1)}, u32[]{:S(2)}, u32[]{:S(2)}) %collective-permute-start.56) | collective-permute-done | bytes 1327136 | tf_op jit(solution)/shard_map/ppermute | solution.py:188
  440.2 14.9 collective-permute-done.61
  456.5 86.1 %collective-permute-done.21 = bf16[3,2,2,256,256]{4,3,2,1,0:T(8,128)(2,1)S(1)} collective-permute-done((bf16[3,2,2,256,256]{4,3,2,1,0:T(8,128)(2,1)S(1)}, bf16[3,2,2,256,256]{4,3,2,1,0:T(8,128)(2,1)S(1)}, u32[]{:S(2)}, u32[]{:S(2)}) %collective-permute-start.21) | collective-permute-done | bytes 1572896 | tf_op jit(solution)/shard_map/ppermute | solution.py:422
  556.6 10.3 attend.1
  596.2 8.3 collective-permute-done.30
  608.8 8.3 collective-permute-done.68
  663.7 13.6 maximum_maximum_fusion.1
  693.3 8.0 fusion.208
  703.4 13.3 collective-permute-done.73
  717.1 12.6 maximum_maximum_fusion.2
  729.9 9.7 fusion.207
  757.8 13.1 collective-permute-done.88
  771.3 12.6 maximum_maximum_fusion.3
  784.1 8.2 fusion.209
  804.7 20.0 %multiply_convert_fusion.6 = (bf16[1024,1152]{1,0:T(8,128)(2,1)S(1)}, bf16[1024,1152]{1,0:T(8,128)(2,1)}, bf16[1024,1152]{1,0:T(8,128)(2,1)}, f32[1024,1152]{1,0:T(8,128)}) fusion(f32[1152]{0:T(1024)S(1)} %copy-done.174, f32[1024,1152]{1,0:T(8,128)} %fusion.211, f32[1152]{0:T(1024)S(1)} %copy-done.169, f32[1024,1152]{1,0:T(8,128)} %fusion.210, ...), kind=kOutput, calls=%fused_computation.107 | convolution fusion | flops 5478285312 | bytes 45425664 | tf_op jit(solution)/shard_map/dot_general | solution.py:49
  824.7 10.0 convolution_convert_fusion
  860.8 9.0 collective-permute-done.93
  872.5 9.9 collective-permute-done.78
  885.2 9.9 collective-permute-done.63
  929.3 8.5 collective-permute-done.98
  938.4 13.6 maximum_maximum_fusion.4
  983.8 12.6 collective-permute-done.108
  996.9 12.8 maximum_maximum_fusion.5
  1033.1 9.4 collective-permute-done.118
  1046.5 12.6 maximum_maximum_fusion.6
  1059.2 11.4 fusion.212
  1075.1 7.9 fusion.215
  1083.1 21.7 %fusion.2 = bf16[1152,2304]{1,0:T(8,128)(2,1)} fusion(bf16[3072,2304]{1,0:T(8,128)(2,1)S(1)} %copy-done.173, bf16[1024,1152]{1,0:T(8,128)(2,1)} %copy-done.221, bf16[1024,1152]{1,0:T(8,128)(2,1)} %get-tuple-element.423, bf16[1024,1152]{1,0:T(8,128)(2,1)} %get-tuple-element.424, f32[2304]{0:T(1024)S(1)} %copy-done.123), kind=kOutput, calls=%fused_computation.7 | convolution fusion | flops 16333996032 | bytes 26551296 | tf_op jit(solution)/shard_map/dot_general | solution.py:57
  1104.7 33.5 %multiply_reduce_fusion.1 = (f32[1152]{0:T(1024)S(1)}, f32[1152]{0:T(1024)S(1)}, f32[1152]{0:T(1024)S(1)}, f32[1152]{0:T(1024)S(1)}, f32[1152]{0:T(1024)S(1)}, /...) fusion(f32[1024,1152]{1,0:T(8,128)} %fusion.210, ...), kind=kOutput, calls=%fused_computation.95 | convolution fusion | flops 5541980160 | bytes 69046272 | tf_op jit(solution)/shard_map/dot_general | solution.py:53
  1145.9 11.6 fusion.213
  1157.5 21.9 %fusion.1 = bf16[2304,1152]{1,0:T(8,128)(2,1)S(1)} fusion(bf16[3072,2304]{1,0:T(8,128)(2,1)} %get-tuple-element.160, bf16[1024,1152]{1,0:T(8,128)(2,1)S(1)} %copy-done.218, bf16[1024,1152]{1,0:T(8,128)(2,1)S(1)} %copy-done.219, bf16[1024,1152]{1,0:T(8,128)(2,1)S(1)} %copy-done.220, f32[1152]{0:T(1024)S(1)} %copy-done.175), kind=kOutput, calls=%fused_computation.6 | convolution fusion | flops 16333996032 | bytes 26546688 | tf_op jit(solution)/shard_map/dot_general | solution.py:57
  1182.6 8.4 multiply_convert_fusion.5
  1191.0 11.6 fusion.214
  1202.7 9.0 fusion.216
  1211.7 23.7 %fusion = bf16[2304,1152]{1,0:T(8,128)(2,1)S(1)} fusion(bf16[3072,2304]{1,0:T(8,128)(2,1)} %get-tuple-element.160, bf16[1024,1152]{1,0:T(8,128)(2,1)} %get-tuple-element.431, bf16[1024,1152]{1,0:T(8,128)(2,1)} %get-tuple-element.430, bf16[1024,1152]{1,0:T(8,128)(2,1)} %get-tuple-element.429, f32[1152]{0:T(1024)S(1)} %copy-done.170), kind=kOutput, calls=%fused_computation.5 | convolution fusion | flops 16333996032 | bytes 26546688 | tf_op jit(solution)/shard_map/dot_general | solution.py:57
  1235.4 10.8 add_convert_fusion.2
  1250.5 10.9 add_convert_fusion.1
  1266.2 10.5 add_convert_fusion.3
  1302.0 37.9 %collective-permute-done.163 = bf16[2,2,1,288,1152]{4,3,2,1,0:T(8,128)(2,1)S(1)} collective-permute-done((bf16[2,2,1,288,1152]{4,3,2,1,0:T(8,128)(2,1)S(1)}, bf16[2,2,1,288,1152]{4,3,2,1,0:T(8,128)(2,1)S(1)}, u32[]{:S(2)}, u32[]{:S(2)}) %collective-permute-start.163) | collective-permute-done | bytes 2654240 | tf_op jit(solution)/shard_map/ppermute | solution.py:188
  1356.4 14.1 collective-permute-done.105
  1371.9 77.7 %collective-permute-done.124 = bf16[128,1152]{1,0:T(8,128)(2,1)S(1)} collective-permute-done((bf16[128,1152]{1,0:T(8,128)(2,1)S(1)}, bf16[128,1152]{1,0:T(8,128)(2,1)S(1)}, u32[]{:S(2)}, u32[]{:S(2)}) %collective-permute-start.124) | collective-permute-done | bytes 294944 | tf_op jit(solution)/shard_map/ppermute | solution.py:188
  1452.9 72.6 %collective-permute-done.114 = bf16[128,1152]{1,0:T(8,128)(2,1)S(1)} collective-permute-done((bf16[128,1152]{1,0:T(8,128)(2,1)S(1)}, bf16[128,1152]{1,0:T(8,128)(2,1)S(1)}, u32[]{:S(2)}, u32[]{:S(2)}) %collective-permute-start.114) | collective-permute-done | bytes 294944 | tf_op jit(solution)/shard_map/ppermute | solution.py:188
  1525.7 8.8 collective-permute-done.104
  1607.7 8.7 collective-permute-done.132
  1620.1 15.9 collective-permute-done.133
  1637.6 13.1 maximum_maximum_fusion.8
  1676.2 10.4 collective-permute-done.138
  1689.4 12.8 maximum_maximum_fusion.9
  1712.6 17.6 attend_back.1
  1779.0 8.9 fusion.46
  1791.5 12.4 collective-permute-done.159
  1811.1 9.2 collective-permute-done.161
  1822.9 12.9 collective-permute-done.162
  1836.7 16.2 collective-permute-done.143
  1876.5 8.0 add_convert_fusion
  1892.3 26.0 %collective-permute-done.150 = bf16[1,2,1,288,512]{4,3,2,1,0:T(8,128)(2,1)S(1)} collective-permute-done((bf16[1,2,1,288,512]{4,3,2,1,0:T(8,128)(2,1)S(1)}, bf16[1,2,1,288,512]{4,3,2,1,0:T(8,128)(2,1)S(1)}, u32[]{:S(2)}, u32[]{:S(2)}) %collective-permute-start.150) | collective-permute-done | bytes 589856 | tf_op jit(solution)/shard_map/ppermute | solution.py:188
  1940.3 13.1 collective-permute-done.145
  (1382 shorter events, 841.6 us)
Async XLA Ops:
  0.7 228.0 %collective-permute-start.24 = (bf16[64,2304]{1,0:T(8,128)(2,1)}, bf16[64,2304]{1,0:T(8,128)(2,1)}, u32[]{:S(2)}, u32[]{:S(2)}) collective-permute-start(bf16[64,2304]{1,0:T(8,128)(2,1)} %param.26), channel_id=1, source_target_pairs={{0,4},{1,5},{2,6},{3,7},{4,0},{5,1},{6,2},{7,3},{8,12},{9,13},{10,... | collective-permute-start | bytes 884744 | tf_op jit(solution)/shard_map/ppermute | solution.py:188
  3.7 222.0 %collective-permute-start.23 = (bf16[64,2304]{1,0:T(8,128)(2,1)}, bf16[64,2304]{1,0:T(8,128)(2,1)}, u32[]{:S(2)}, u32[]{:S(2)}) collective-permute-start(bf16[64,2304]{1,0:T(8,128)(2,1)} %param.26), channel_id=1, source_target_pairs={{0,16},{1,17},{2,18},{3,19},{4,20},{5,21},{6,22},{7,23},{8,24},{9,... | collective-permute-start | bytes 884744 | tf_op jit(solution)/shard_map/ppermute | solution.py:188
  7.1 38.0 %collective-permute-start.15 = (f32[1,848]{1,0:T(1,128)S(1)}, f32[1,848]{1,0:T(1,128)S(1)}, u32[]{:S(2)}, u32[]{:S(2)}) collective-permute-start(f32[1,848]{1,0:T(1,128)S(1)} %broadcast_in_dim.315), channel_id=1, source_target_pairs={{0,1},{1,0},{2,3},{3,2},{4,5},{5,4},{6,7},{7,6},{8,9},{9,8},{10,11... | collective-permute-start | bytes 10184 | tf_op jit(solution)/shard_map/ppermute | solution.py:188
  11.7 50.0 %collective-permute-start.5 = (bf16[72,512]{1,0:T(8,128)(2,1)}, bf16[72,512]{1,0:T(8,128)(2,1)}, u32[]{:S(2)}, u32[]{:S(2)}) collective-permute-start(bf16[72,512]{1,0:T(8,128)(2,1)} %get-tuple-element.406), channel_id=1, source_target_pairs={{0,1},{1,0},{2,3},{3,2},{4,5},{5,4},{6,7},{7,6},{8,9},{9,8},{10,11... | collective-permute-start | bytes 221192 | tf_op jit(solution)/shard_map/ppermute | solution.py:188
  12.1 319.1 %collective-permute-start.60 = (bf16[288,2304]{1,0:T(8,128)(2,1)}, bf16[288,2304]{1,0:T(8,128)(2,1)}, u32[]{:S(2)}, u32[]{:S(2)}) collective-permute-start(bf16[288,2304]{1,0:T(8,128)(2,1)} %param.29), channel_id=1, source_target_pairs={{0,4},{1,5},{2,6},{3,7},{4,0},{5,1},{6,2},{7,3},{8,12},{9,13},{10,... | collective-permute-start | bytes 3981320 | tf_op jit(solution)/shard_map/ppermute | solution.py:188
  60.0 267.0 %collective-permute-start.59 = (bf16[288,2304]{1,0:T(8,128)(2,1)}, bf16[288,2304]{1,0:T(8,128)(2,1)}, u32[]{:S(2)}, u32[]{:S(2)}) collective-permute-start(bf16[288,2304]{1,0:T(8,128)(2,1)} %param.29), channel_id=1, source_target_pairs={{0,16},{1,17},{2,18},{3,19},{4,20},{5,21},{6,22},{7,23},{8,24},{9,... | collective-permute-start | bytes 3981320 | tf_op jit(solution)/shard_map/ppermute | solution.py:188
  70.6 17.5 collective-permute-start.8
  88.0 31.2 %collective-permute-start.9 = (bf16[72,512]{1,0:T(8,128)(2,1)S(1)}, bf16[72,512]{1,0:T(8,128)(2,1)S(1)}, u32[]{:S(2)}, u32[]{:S(2)}) collective-permute-start(bf16[72,512]{1,0:T(8,128)(2,1)S(1)} %copy-done.151), channel_id=1, source_target_pairs={{0,9},{1,8},{2,11},{3,10},{4,13},{5,12},{6,15},{7,14},{8,1},{9,0},... | collective-permute-start | bytes 221192 | tf_op jit(solution)/shard_map/ppermute | solution.py:188
  228.7 33.8 %collective-permute-start.13 = (bf16[8,72,512]{2,1,0:T(8,128)(2,1)S(1)}, bf16[8,72,512]{2,1,0:T(8,128)(2,1)S(1)}, u32[]{:S(2)}, u32[]{:S(2)}) collective-permute-start(bf16[8,72,512]{2,1,0:T(8,128)(2,1)S(1)} %copy-done.111), channel_id=1, source_target_pairs={{0,4},{1,5},{2,6},{3,7},{4,0},{5,1},{6,2},{7,3},{8,12},{9,13},{10,... | collective-permute-start | bytes 1769480 | tf_op jit(solution)/shard_map/ppermute | solution.py:188
  233.9 27.0 %collective-permute-start.12 = (bf16[8,72,512]{2,1,0:T(8,128)(2,1)S(1)}, bf16[8,72,512]{2,1,0:T(8,128)(2,1)S(1)}, u32[]{:S(2)}, u32[]{:S(2)}) collective-permute-start(bf16[8,72,512]{2,1,0:T(8,128)(2,1)S(1)} %copy-done.111), channel_id=1, source_target_pairs={{0,16},{1,17},{2,18},{3,19},{4,20},{5,21},{6,22},{7,23},{8,24},{9,... | collective-permute-start | bytes 1769480 | tf_op jit(solution)/shard_map/ppermute | solution.py:188
  260.9 177.7 %collective-permute-start.47 = (bf16[8,72,1152]{2,1,0:T(8,128)(2,1)}, bf16[8,72,1152]{2,1,0:T(8,128)(2,1)}, u32[]{:S(2)}, u32[]{:S(2)}) collective-permute-start(bf16[8,72,1152]{2,1,0:T(8,128)(2,1)} %bitcast_dynamic-update-slice_fusion.35), channel_id=1, source_target_pairs={{0,4},{1,5},{2,6},{3,7},{4,0},{5,1},{6,2},{7,3},{8,12},{9,13},{10,... | collective-permute-start | bytes 3981320 | tf_op jit(solution)/shard_map/ppermute | solution.py:188
  262.7 28.3 %collective-permute-start.27 = (bf16[64,2304]{1,0:T(8,128)(2,1)S(1)}, bf16[64,2304]{1,0:T(8,128)(2,1)S(1)}, u32[]{:S(2)}, u32[]{:S(2)}) collective-permute-start(bf16[64,2304]{1,0:T(8,128)(2,1)S(1)} %get-tuple-element.257), channel_id=1, source_target_pairs={{0,2},{1,3},{2,0},{3,1},{4,6},{5,7},{6,4},{7,5},{8,10},{9,11},{10,... | collective-permute-start | bytes 884744 | tf_op jit(solution)/shard_map/ppermute | solution.py:188
  290.3 18.5 collective-permute-start.4
  306.2 118.6 %collective-permute-start.46 = (bf16[8,72,1152]{2,1,0:T(8,128)(2,1)}, bf16[8,72,1152]{2,1,0:T(8,128)(2,1)}, u32[]{:S(2)}, u32[]{:S(2)}) collective-permute-start(bf16[8,72,1152]{2,1,0:T(8,128)(2,1)} %bitcast_dynamic-update-slice_fusion.35), channel_id=1, source_target_pairs={{0,16},{1,17},{2,18},{3,19},{4,20},{5,21},{6,22},{7,23},{8,24},{9,... | collective-permute-start | bytes 3981320 | tf_op jit(solution)/shard_map/ppermute | solution.py:188
  323.9 102.5 %collective-permute-start.20 = (f32[3,2,2,256,256]{4,3,2,1,0:T(8,128)S(1)}, f32[3,2,2,256,256]{4,3,2,1,0:T(8,128)S(1)}, u32[]{:S(2)}, u32[]{:S(2)}) collective-permute-start(f32[3,2,2,256,256]{4,3,2,1,0:T(8,128)S(1)} %slice.994), channel_id=1, source_target_pairs={{0,1},{1,0},{2,3},{3,2},{4,5},{5,4},{6,7},{7,6},{8,9},{9,8},{10,11... | collective-permute-start | bytes 9437192 | tf_op jit(solution)/shard_map/ppermute | solution.py:188
  327.0 95.7 %collective-permute-start.56 = (bf16[8,72,1152]{2,1,0:T(8,128)(2,1)S(1)}, bf16[8,72,1152]{2,1,0:T(8,128)(2,1)}, u32[]{:S(2)}, u32[]{:S(2)}) collective-permute-start(bf16[8,72,1152]{2,1,0:T(8,128)(2,1)S(1)} %copy-done.75), channel_id=1, source_target_pairs={{0,16},{1,17},{2,18},{3,19},{4,20},{5,21},{6,22},{7,23},{8,24},{9,... | collective-permute-start | bytes 3981320 | tf_op jit(solution)/shard_map/ppermute | solution.py:188
  331.2 100.8 %collective-permute-start.57 = (bf16[8,72,1152]{2,1,0:T(8,128)(2,1)S(1)}, bf16[8,72,1152]{2,1,0:T(8,128)(2,1)}, u32[]{:S(2)}, u32[]{:S(2)}) collective-permute-start(bf16[8,72,1152]{2,1,0:T(8,128)(2,1)S(1)} %copy-done.75), channel_id=1, source_target_pairs={{0,4},{1,5},{2,6},{3,7},{4,0},{5,1},{6,2},{7,3},{8,12},{9,13},{10,... | collective-permute-start | bytes 3981320 | tf_op jit(solution)/shard_map/ppermute | solution.py:188
  422.7 32.3 %collective-permute-start.61 = (bf16[288,2304]{1,0:T(8,128)(2,1)}, bf16[288,2304]{1,0:T(8,128)(2,1)}, u32[]{:S(2)}, u32[]{:S(2)}) collective-permute-start(bf16[288,2304]{1,0:T(8,128)(2,1)} %collective-permute-done.59), channel_id=1, source_target_pairs={{0,4},{1,5},{2,6},{3,7},{4,0},{5,1},{6,2},{7,3},{8,12},{9,13},{10,... | collective-permute-start | bytes 3981320 | tf_op jit(solution)/shard_map/ppermute | solution.py:188
  424.8 218.9 %collective-permute-start.58 = (bf16[8,72,1152]{2,1,0:T(8,128)(2,1)}, bf16[8,72,1152]{2,1,0:T(8,128)(2,1)}, u32[]{:S(2)}, u32[]{:S(2)}) collective-permute-start(bf16[8,72,1152]{2,1,0:T(8,128)(2,1)} %collective-permute-done.56), channel_id=1, source_target_pairs={{0,4},{1,5},{2,6},{3,7},{4,0},{5,1},{6,2},{7,3},{8,12},{9,13},{10,... | collective-permute-start | bytes 3981320 | tf_op jit(solution)/shard_map/ppermute | solution.py:188
  426.4 217.3 %collective-permute-start.48 = (bf16[8,72,1152]{2,1,0:T(8,128)(2,1)}, bf16[8,72,1152]{2,1,0:T(8,128)(2,1)}, u32[]{:S(2)}, u32[]{:S(2)}) collective-permute-start(bf16[8,72,1152]{2,1,0:T(8,128)(2,1)} %collective-permute-done.46), channel_id=1, source_target_pairs={{0,4},{1,5},{2,6},{3,7},{4,0},{5,1},{6,2},{7,3},{8,12},{9,13},{10,... | collective-permute-start | bytes 3981320 | tf_op jit(solution)/shard_map/ppermute | solution.py:188
  432.0 110.6 %collective-permute-start.21 = (bf16[3,2,2,256,256]{4,3,2,1,0:T(8,128)(2,1)S(1)}, bf16[3,2,2,256,256]{4,3,2,1,0:T(8,128)(2,1)S(1)}, u32[]{:S(2)}, u32[]{:S(2)}) collective-permute-start(bf16[3,2,2,256,256]{4,3,2,1,0:T(8,128)(2,1)S(1)} %pad_maximum_fusion.5), channel_id=1, source_target_pairs={{0,4},{1,5},{2,6},{3,7},{8,12},{9,13},{10,14},{11,15},{16,20},{17,... | collective-permute-start | bytes 4718600 | tf_op jit(solution)/shard_map/ppermute | solution.py:422
  581.5 23.0 %collective-permute-start.30 = (bf16[2,128,1152]{2,1,0:T(8,128)(2,1)S(1)}, bf16[2,128,1152]{2,1,0:T(8,128)(2,1)S(1)}, u32[]{:S(2)}, u32[]{:S(2)}) collective-permute-start(bf16[2,128,1152]{2,1,0:T(8,128)(2,1)S(1)} %slice_bitcast_fusion.39), channel_id=1, source_target_pairs={{0,2},{1,3},{2,0},{3,1},{4,6},{5,7},{6,4},{7,5},{8,10},{9,11},{10,... | collective-permute-start | bytes 1769480 | tf_op jit(solution)/shard_map/ppermute | solution.py:188
  593.8 23.4 %collective-permute-start.68 = (bf16[2,128,1152]{2,1,0:T(8,128)(2,1)S(1)}, bf16[2,128,1152]{2,1,0:T(8,128)(2,1)S(1)}, u32[]{:S(2)}, u32[]{:S(2)}) collective-permute-start(bf16[2,128,1152]{2,1,0:T(8,128)(2,1)S(1)} %slice_bitcast_fusion.31), channel_id=1, source_target_pairs={{0,2},{1,3},{2,0},{3,1},{4,6},{5,7},{6,4},{7,5},{8,10},{9,11},{10,... | collective-permute-start | bytes 1769480 | tf_op jit(solution)/shard_map/ppermute | solution.py:188
  856.7 25.8 %collective-permute-start.78 = (bf16[2,128,1152]{2,1,0:T(8,128)(2,1)S(1)}, bf16[2,128,1152]{2,1,0:T(8,128)(2,1)S(1)}, u32[]{:S(2)}, u32[]{:S(2)}) collective-permute-start(bf16[2,128,1152]{2,1,0:T(8,128)(2,1)S(1)} %slice_bitcast_fusion.27), channel_id=1, source_target_pairs={{0,2},{1,3},{2,0},{3,1},{4,6},{5,7},{6,4},{7,5},{8,10},{9,11},{10,... | collective-permute-start | bytes 1769480 | tf_op jit(solution)/shard_map/ppermute | solution.py:188
  857.3 26.8 %collective-permute-start.80 = (bf16[2,128,1152]{2,1,0:T(8,128)(2,1)S(1)}, bf16[2,128,1152]{2,1,0:T(8,128)(2,1)S(1)}, u32[]{:S(2)}, u32[]{:S(2)}) collective-permute-start(bf16[2,128,1152]{2,1,0:T(8,128)(2,1)S(1)} %slice_bitcast_fusion.25), channel_id=1, source_target_pairs={{0,8},{1,9},{2,10},{3,11},{4,12},{5,13},{6,14},{7,15},{8,0},{9,1},... | collective-permute-start | bytes 1769480 | tf_op jit(solution)/shard_map/ppermute | solution.py:188
  859.2 35.9 %collective-permute-start.63 = (bf16[2,128,1152]{2,1,0:T(8,128)(2,1)S(1)}, bf16[2,128,1152]{2,1,0:T(8,128)(2,1)S(1)}, u32[]{:S(2)}, u32[]{:S(2)}) collective-permute-start(bf16[2,128,1152]{2,1,0:T(8,128)(2,1)S(1)} %slice_bitcast_fusion.35), channel_id=1, source_target_pairs={{0,2},{1,3},{2,0},{3,1},{4,6},{5,7},{6,4},{7,5},{8,10},{9,11},{10,... | collective-permute-start | bytes 1769480 | tf_op jit(solution)/shard_map/ppermute | solution.py:188
  869.8 26.9 %collective-permute-start.65 = (bf16[2,128,1152]{2,1,0:T(8,128)(2,1)S(1)}, bf16[2,128,1152]{2,1,0:T(8,128)(2,1)S(1)}, u32[]{:S(2)}, u32[]{:S(2)}) collective-permute-start(bf16[2,128,1152]{2,1,0:T(8,128)(2,1)S(1)} %slice_bitcast_fusion.33), channel_id=1, source_target_pairs={{0,8},{1,9},{2,10},{3,11},{4,12},{5,13},{6,14},{7,15},{8,0},{9,1},... | collective-permute-start | bytes 1769480 | tf_op jit(solution)/shard_map/ppermute | solution.py:188
  871.7 29.6 %collective-permute-start.96 = (bf16[128,1152]{1,0:T(8,128)(2,1)S(1)}, bf16[128,1152]{1,0:T(8,128)(2,1)S(1)}, u32[]{:S(2)}, u32[]{:S(2)}) collective-permute-start(bf16[128,1152]{1,0:T(8,128)(2,1)S(1)} %slice_bitcast_fusion.81), channel_id=1, source_target_pairs={{0,2},{1,3},{2,0},{3,1},{4,6},{5,7},{6,4},{7,5},{8,10},{9,11},{10,... | collective-permute-start | bytes 884744 | tf_op jit(solution)/shard_map/ppermute | solution.py:188
  882.4 20.6 %collective-permute-start.94 = (bf16[128,1152]{1,0:T(8,128)(2,1)S(1)}, bf16[128,1152]{1,0:T(8,128)(2,1)S(1)}, u32[]{:S(2)}, u32[]{:S(2)}) collective-permute-start(bf16[128,1152]{1,0:T(8,128)(2,1)S(1)} %slice_bitcast_fusion.83), channel_id=1, source_target_pairs={{0,8},{1,9},{2,10},{3,11},{4,12},{5,13},{6,14},{7,15},{8,0},{9,1},... | collective-permute-start | bytes 884744 | tf_op jit(solution)/shard_map/ppermute | solution.py:188
  884.4 23.3 %collective-permute-start.81 = (bf16[128,1152]{1,0:T(8,128)(2,1)S(1)}, bf16[128,1152]{1,0:T(8,128)(2,1)S(1)}, u32[]{:S(2)}, u32[]{:S(2)}) collective-permute-start(bf16[128,1152]{1,0:T(8,128)(2,1)S(1)} %slice_bitcast_fusion.93), channel_id=1, source_target_pairs={{0,2},{1,3},{2,0},{3,1},{4,6},{5,7},{6,4},{7,5},{8,10},{9,11},{10,... | collective-permute-start | bytes 884744 | tf_op jit(solution)/shard_map/ppermute | solution.py:188
  1143.4 154.6 %collective-permute-start.181 = (bf16[2,1,288,2304]{3,2,1,0:T(8,128)(2,1)}, bf16[2,1,288,2304]{3,2,1,0:T(8,128)(2,1)}, u32[]{:S(2)}, u32[]{:S(2)}) collective-permute-start(bf16[2,1,288,2304]{3,2,1,0:T(8,128)(2,1)} %constant_dynamic-slice_fusion.1), channel_id=1, source_target_pairs={{0,4},{1,5},{2,6},{3,7},{4,0},{5,1},{6,2},{7,3},{8,12},{9,13},{10,... | collective-permute-start | bytes 7962632 | tf_op jit(solution)/shard_map/ppermute | solution.py:188
  1182.5 111.1 %collective-permute-start.172 = (bf16[2,2,1,288,1152]{4,3,2,1,0:T(8,128)(2,1)}, bf16[2,2,1,288,1152]{4,3,2,1,0:T(8,128)(2,1)}, u32[]{:S(2)}, u32[]{:S(2)}) collective-permute-start(bf16[2,2,1,288,1152]{4,3,2,1,0:T(8,128)(2,1)} %constant_dynamic-slice_fusion.3), channel_id=1, source_target_pairs={{0,4},{1,5},{2,6},{3,7},{4,0},{5,1},{6,2},{7,3},{8,12},{9,13},{10,... | collective-permute-start | bytes 7962632 | tf_op jit(solution)/shard_map/ppermute | solution.py:188
  1265.8 19.8 collective-permute-start.112
  1279.8 60.1 %collective-permute-start.163 = (bf16[2,2,1,288,1152]{4,3,2,1,0:T(8,128)(2,1)S(1)}, bf16[2,2,1,288,1152]{4,3,2,1,0:T(8,128)(2,1)S(1)}, u32[]{:S(2)}, u32[]{:S(2)}) collective-permute-start(bf16[2,2,1,288,1152]{4,3,2,1,0:T(8,128)(2,1)S(1)} %constant_dynamic-slice_fusion.5), channel_id=1, source_target_pairs={{0,4},{1,5},{2,6},{3,7},{4,0},{5,1},{6,2},{7,3},{8,12},{9,13},{10,... | collective-permute-start | bytes 7962632 | tf_op jit(solution)/shard_map/ppermute | solution.py:188
  1285.7 58.7 %collective-permute-start.123 = (bf16[2,128,1152]{2,1,0:T(8,128)(2,1)}, bf16[2,128,1152]{2,1,0:T(8,128)(2,1)S(1)}, u32[]{:S(2)}, u32[]{:S(2)}) collective-permute-start(bf16[2,128,1152]{2,1,0:T(8,128)(2,1)} %slice_bitcast_fusion.7), channel_id=1, source_target_pairs={{0,2},{1,3},{2,0},{3,1},{4,6},{5,7},{6,4},{7,5},{8,10},{9,11},{10,... | collective-permute-start | bytes 1769480 | tf_op jit(solution)/shard_map/ppermute | solution.py:188
  1289.2 56.4 %collective-permute-start.125 = (bf16[2,128,1152]{2,1,0:T(8,128)(2,1)}, bf16[2,128,1152]{2,1,0:T(8,128)(2,1)S(1)}, u32[]{:S(2)}, u32[]{:S(2)}) collective-permute-start(bf16[2,128,1152]{2,1,0:T(8,128)(2,1)} %slice_bitcast_fusion.5), channel_id=1, source_target_pairs={{0,8},{1,9},{2,10},{3,11},{4,12},{5,13},{6,14},{7,15},{8,0},{9,1},... | collective-permute-start | bytes 1769480 | tf_op jit(solution)/shard_map/ppermute | solution.py:188
  1293.7 53.2 %collective-permute-start.113 = (bf16[2,128,1152]{2,1,0:T(8,128)(2,1)}, bf16[2,128,1152]{2,1,0:T(8,128)(2,1)S(1)}, u32[]{:S(2)}, u32[]{:S(2)}) collective-permute-start(bf16[2,128,1152]{2,1,0:T(8,128)(2,1)} %slice_bitcast_fusion.11), channel_id=1, source_target_pairs={{0,2},{1,3},{2,0},{3,1},{4,6},{5,7},{6,4},{7,5},{8,10},{9,11},{10,... | collective-permute-start | bytes 1769480 | tf_op jit(solution)/shard_map/ppermute | solution.py:188
  1298.6 50.3 %collective-permute-start.115 = (bf16[2,128,1152]{2,1,0:T(8,128)(2,1)}, bf16[2,128,1152]{2,1,0:T(8,128)(2,1)S(1)}, u32[]{:S(2)}, u32[]{:S(2)}) collective-permute-start(bf16[2,128,1152]{2,1,0:T(8,128)(2,1)} %slice_bitcast_fusion.9), channel_id=1, source_target_pairs={{0,8},{1,9},{2,10},{3,11},{4,12},{5,13},{6,14},{7,15},{8,0},{9,1},... | collective-permute-start | bytes 1769480 | tf_op jit(solution)/shard_map/ppermute | solution.py:188
  1344.4 26.2 %collective-permute-start.105 = (bf16[2,128,1152]{2,1,0:T(8,128)(2,1)S(1)}, bf16[2,128,1152]{2,1,0:T(8,128)(2,1)S(1)}, u32[]{:S(2)}, u32[]{:S(2)}) collective-permute-start(bf16[2,128,1152]{2,1,0:T(8,128)(2,1)S(1)} %slice_bitcast_fusion.13), channel_id=1, source_target_pairs={{0,8},{1,9},{2,10},{3,11},{4,12},{5,13},{6,14},{7,15},{8,0},{9,1},... | collective-permute-start | bytes 1769480 | tf_op jit(solution)/shard_map/ppermute | solution.py:188
  1345.6 213.4 %collective-permute-start.182 = (bf16[1,1,288,2304]{3,2,1,0:T(8,128)(2,1)}, bf16[1,1,288,2304]{3,2,1,0:T(8,128)(2,1)}, u32[]{:S(2)}, u32[]{:S(2)}) collective-permute-start(bf16[1,1,288,2304]{3,2,1,0:T(8,128)(2,1)} %constant_dynamic-slice_fusion), channel_id=1, source_target_pairs={{0,16},{1,17},{2,18},{3,19},{4,20},{5,21},{6,22},{7,23},{8,24},{9,... | collective-permute-start | bytes 3981320 | tf_op jit(solution)/shard_map/ppermute | solution.py:188
  1346.9 209.6 %collective-permute-start.173 = (bf16[1,2,1,288,1152]{4,3,2,1,0:T(8,128)(2,1)}, bf16[1,2,1,288,1152]{4,3,2,1,0:T(8,128)(2,1)}, u32[]{:S(2)}, u32[]{:S(2)}) collective-permute-start(bf16[1,2,1,288,1152]{4,3,2,1,0:T(8,128)(2,1)} %constant_dynamic-slice_fusion.2), channel_id=1, source_target_pairs={{0,16},{1,17},{2,18},{3,19},{4,20},{5,21},{6,22},{7,23},{8,24},{9,... | collective-permute-start | bytes 3981320 | tf_op jit(solution)/shard_map/ppermute | solution.py:188
  1348.9 215.1 %collective-permute-start.164 = (bf16[1,2,1,288,1152]{4,3,2,1,0:T(8,128)(2,1)}, bf16[1,2,1,288,1152]{4,3,2,1,0:T(8,128)(2,1)}, u32[]{:S(2)}, u32[]{:S(2)}) collective-permute-start(bf16[1,2,1,288,1152]{4,3,2,1,0:T(8,128)(2,1)} %constant_dynamic-slice_fusion.4), channel_id=1, source_target_pairs={{0,16},{1,17},{2,18},{3,19},{4,20},{5,21},{6,22},{7,23},{8,24},{9,... | collective-permute-start | bytes 3981320 | tf_op jit(solution)/shard_map/ppermute | solution.py:188
  1370.5 79.0 %collective-permute-start.124 = (bf16[128,1152]{1,0:T(8,128)(2,1)S(1)}, bf16[128,1152]{1,0:T(8,128)(2,1)S(1)}, u32[]{:S(2)}, u32[]{:S(2)}) collective-permute-start(bf16[128,1152]{1,0:T(8,128)(2,1)S(1)} %slice_bitcast_fusion.59), channel_id=1, source_target_pairs={{0,8},{1,9},{2,10},{3,11},{4,12},{5,13},{6,14},{7,15},{8,0},{9,1},... | collective-permute-start | bytes 884744 | tf_op jit(solution)/shard_map/ppermute | solution.py:188
  1370.9 81.3 %collective-permute-start.116 = (bf16[128,1152]{1,0:T(8,128)(2,1)S(1)}, bf16[128,1152]{1,0:T(8,128)(2,1)S(1)}, u32[]{:S(2)}, u32[]{:S(2)}) collective-permute-start(bf16[128,1152]{1,0:T(8,128)(2,1)S(1)} %slice_bitcast_fusion.65), channel_id=1, source_target_pairs={{0,2},{1,3},{2,0},{3,1},{4,6},{5,7},{6,4},{7,5},{8,10},{9,11},{10,... | collective-permute-start | bytes 884744 | tf_op jit(solution)/shard_map/ppermute | solution.py:188
  1449.6 76.0 %collective-permute-start.114 = (bf16[128,1152]{1,0:T(8,128)(2,1)S(1)}, bf16[128,1152]{1,0:T(8,128)(2,1)S(1)}, u32[]{:S(2)}, u32[]{:S(2)}) collective-permute-start(bf16[128,1152]{1,0:T(8,128)(2,1)S(1)} %slice_bitcast_fusion.67), channel_id=1, source_target_pairs={{0,8},{1,9},{2,10},{3,11},{4,12},{5,13},{6,14},{7,15},{8,0},{9,1},... | collective-permute-start | bytes 884744 | tf_op jit(solution)/shard_map/ppermute | solution.py:188
  1452.2 73.4 %collective-permute-start.106 = (bf16[128,1152]{1,0:T(8,128)(2,1)S(1)}, bf16[128,1152]{1,0:T(8,128)(2,1)S(1)}, u32[]{:S(2)}, u32[]{:S(2)}) collective-permute-start(bf16[128,1152]{1,0:T(8,128)(2,1)S(1)} %slice_bitcast_fusion.73), channel_id=1, source_target_pairs={{0,2},{1,3},{2,0},{3,1},{4,6},{5,7},{6,4},{7,5},{8,10},{9,11},{10,... | collective-permute-start | bytes 884744 | tf_op jit(solution)/shard_map/ppermute | solution.py:188
  1558.8 91.8 %collective-permute-start.180 = (bf16[72,1152]{1,0:T(8,128)(2,1)S(1)}, bf16[72,1152]{1,0:T(8,128)(2,1)S(1)}, u32[]{:S(2)}, u32[]{:S(2)}) collective-permute-start(bf16[72,1152]{1,0:T(8,128)(2,1)S(1)} %get-tuple-element.216), channel_id=1, source_target_pairs={{0,11},{1,10},{2,9},{3,8},{4,15},{5,14},{6,13},{7,12},{8,3},{9,2},... | collective-permute-start | bytes 497672 | tf_op jit(solution)/shard_map/ppermute | solution.py:188
  1558.9 60.2 %collective-permute-start.179 = (bf16[72,1152]{1,0:T(8,128)(2,1)S(1)}, bf16[72,1152]{1,0:T(8,128)(2,1)S(1)}, u32[]{:S(2)}, u32[]{:S(2)}) collective-permute-start(bf16[72,1152]{1,0:T(8,128)(2,1)S(1)} %get-tuple-element.217), channel_id=1, source_target_pairs={{0,10},{1,11},{2,8},{3,9},{4,14},{5,15},{6,12},{7,13},{8,2},{9,3},... | collective-permute-start | bytes 497672 | tf_op jit(solution)/shard_map/ppermute | solution.py:188
  1564.0 42.5 %collective-permute-start.178 = (bf16[72,1152]{1,0:T(8,128)(2,1)S(1)}, bf16[72,1152]{1,0:T(8,128)(2,1)S(1)}, u32[]{:S(2)}, u32[]{:S(2)}) collective-permute-start(bf16[72,1152]{1,0:T(8,128)(2,1)S(1)} %get-tuple-element.218), channel_id=1, source_target_pairs={{0,9},{1,8},{2,11},{3,10},{4,13},{5,12},{6,15},{7,14},{8,1},{9,0},... | collective-permute-start | bytes 497672 | tf_op jit(solution)/shard_map/ppermute | solution.py:188
  1578.7 23.2 %collective-permute-start.131 = (bf16[512,2304]{1,0:T(8,128)(2,1)S(1)}, bf16[512,2304]{1,0:T(8,128)(2,1)S(1)}, u32[]{:S(2)}, u32[]{:S(2)}) collective-permute-start(bf16[512,2304]{1,0:T(8,128)(2,1)S(1)} %maximum_maximum_fusion.7), channel_id=1, source_target_pairs={{0,1},{1,0},{2,3},{3,2},{4,5},{5,4},{6,7},{7,6},{8,9},{9,8},{10,11... | collective-permute-start | bytes 7077896 | tf_op jit(solution)/shard_map/ppermute | solution.py:188
  1601.9 159.3 %collective-permute-start.171 = (bf16[72,1152]{1,0:T(8,128)(2,1)}, bf16[72,1152]{1,0:T(8,128)(2,1)S(1)}, u32[]{:S(2)}, u32[]{:S(2)}) collective-permute-start(bf16[72,1152]{1,0:T(8,128)(2,1)} %get-tuple-element.224), channel_id=1, source_target_pairs={{0,11},{1,10},{2,9},{3,8},{4,15},{5,14},{6,13},{7,12},{8,3},{9,2},... | collective-permute-start | bytes 497672 | tf_op jit(solution)/shard_map/ppermute | solution.py:188
  1616.3 128.7 %collective-permute-start.170 = (bf16[72,1152]{1,0:T(8,128)(2,1)S(1)}, bf16[72,1152]{1,0:T(8,128)(2,1)S(1)}, u32[]{:S(2)}, u32[]{:S(2)}) collective-permute-start(bf16[72,1152]{1,0:T(8,128)(2,1)S(1)} %get-tuple-element.225), channel_id=1, source_target_pairs={{0,10},{1,11},{2,8},{3,9},{4,14},{5,15},{6,12},{7,13},{8,2},{9,3},... | collective-permute-start | bytes 497672 | tf_op jit(solution)/shard_map/ppermute | solution.py:188
  1618.0 18.1 collective-permute-start.133
  1619.2 17.8 collective-permute-start.135
  1636.1 108.3 %collective-permute-start.169 = (bf16[72,1152]{1,0:T(8,128)(2,1)S(1)}, bf16[72,1152]{1,0:T(8,128)(2,1)S(1)}, u32[]{:S(2)}, u32[]{:S(2)}) collective-permute-start(bf16[72,1152]{1,0:T(8,128)(2,1)S(1)} %get-tuple-element.226), channel_id=1, source_target_pairs={{0,9},{1,8},{2,11},{3,10},{4,13},{5,12},{6,15},{7,14},{8,1},{9,0},... | collective-permute-start | bytes 497672 | tf_op jit(solution)/shard_map/ppermute | solution.py:188
  1668.4 18.3 collective-permute-start.138
  1686.7 57.0 %collective-permute-start.168 = (bf16[72,1152]{1,0:T(8,128)(2,1)S(1)}, bf16[72,1152]{1,0:T(8,128)(2,1)S(1)}, u32[]{:S(2)}, u32[]{:S(2)}) collective-permute-start(bf16[72,1152]{1,0:T(8,128)(2,1)S(1)} %get-tuple-element.227), channel_id=1, source_target_pairs={{0,8},{1,9},{2,10},{3,11},{4,12},{5,13},{6,14},{7,15},{8,0},{9,1},... | collective-permute-start | bytes 497672 | tf_op jit(solution)/shard_map/ppermute | solution.py:188
  1743.1 62.5 %collective-permute-start.142 = (f32[3,2,2,2,256,256]{5,4,3,2,1,0:T(8,128)}, f32[3,2,2,2,256,256]{5,4,3,2,1,0:T(8,128)}, u32[]{:S(2)}, u32[]{:S(2)}) collective-permute-start(f32[3,2,2,2,256,256]{5,4,3,2,1,0:T(8,128)} %pad_maximum_fusion.1), channel_id=1, source_target_pairs={{0,1},{1,0},{2,3},{3,2},{4,5},{5,4},{6,7},{7,6},{8,9},{9,8},{10,11... | collective-permute-start | bytes 18874376 | tf_op jit(solution)/shard_map/ppermute | solution.py:188
  1809.7 43.2 %collective-permute-start.143 = (bf16[3,2,2,256,256]{4,3,2,1,0:T(8,128)(2,1)S(1)}, bf16[3,2,2,256,256]{4,3,2,1,0:T(8,128)(2,1)S(1)}, u32[]{:S(2)}, u32[]{:S(2)}) collective-permute-start(bf16[3,2,2,256,256]{4,3,2,1,0:T(8,128)(2,1)S(1)} %fusion.57), channel_id=1, source_target_pairs={{4,0},{5,1},{6,2},{7,3},{12,8},{13,9},{14,10},{15,11},{20,16},{21,... | collective-permute-start | bytes 4718600 | tf_op jit(solution)/shard_map/ppermute | solution.py:549
  1863.9 27.0 %collective-permute-start.149 = (bf16[2,2,1,288,512]{4,3,2,1,0:T(8,128)(2,1)S(1)}, bf16[2,2,1,288,512]{4,3,2,1,0:T(8,128)(2,1)S(1)}, u32[]{:S(2)}, u32[]{:S(2)}) collective-permute-start(bf16[2,2,1,288,512]{4,3,2,1,0:T(8,128)(2,1)S(1)} %constant_dynamic-slice_fusion.9), channel_id=1, source_target_pairs={{0,4},{1,5},{2,6},{3,7},{4,0},{5,1},{6,2},{7,3},{8,12},{9,13},{10,... | collective-permute-start | bytes 3538952 | tf_op jit(solution)/shard_map/ppermute | solution.py:188
  1886.9 48.2 %collective-permute-start.144 = (bf16[2,2,128,2304]{3,2,1,0:T(8,128)(2,1)}, bf16[2,2,128,2304]{3,2,1,0:T(8,128)(2,1)}, u32[]{:S(2)}, u32[]{:S(2)}) collective-permute-start(bf16[2,2,128,2304]{3,2,1,0:T(8,128)(2,1)} %bitcast.307), channel_id=1, source_target_pairs={{0,1},{1,0},{2,3},{3,2},{4,5},{5,4},{6,7},{7,6},{8,9},{9,8},{10,11... | collective-permute-start | bytes 7077896 | tf_op jit(solution)/shard_map/ppermute | solution.py:188
  1891.3 27.0 %collective-permute-start.150 = (bf16[1,2,1,288,512]{4,3,2,1,0:T(8,128)(2,1)S(1)}, bf16[1,2,1,288,512]{4,3,2,1,0:T(8,128)(2,1)S(1)}, u32[]{:S(2)}, u32[]{:S(2)}) collective-permute-start(bf16[1,2,1,288,512]{4,3,2,1,0:T(8,128)(2,1)S(1)} %constant_dynamic-slice_fusion.8), channel_id=1, source_target_pairs={{0,16},{1,17},{2,18},{3,19},{4,20},{5,21},{6,22},{7,23},{8,24},{9,... | collective-permute-start | bytes 1769480 | tf_op jit(solution)/shard_map/ppermute | solution.py:188
  1921.0 46.9 %collective-permute-start.157 = (bf16[72,512]{1,0:T(8,128)(2,1)S(1)}, bf16[72,512]{1,0:T(8,128)(2,1)}, u32[]{:S(2)}, u32[]{:S(2)}) collective-permute-start(bf16[72,512]{1,0:T(8,128)(2,1)S(1)} %get-tuple-element.284), channel_id=1, source_target_pairs={{0,11},{1,10},{2,9},{3,8},{4,15},{5,14},{6,13},{7,12},{8,3},{9,2},... | collective-permute-start | bytes 221192 | tf_op jit(solution)/shard_map/ppermute | solution.py:188
  1921.0 19.2 collective-permute-start.156
  (378 other events, 6044.9 us)

commit v2 on v1

v2 whole, which is shorter than its diff:
```python
import functools

import jax
import jax.numpy as jnp
from jax import lax
from jax.experimental import pallas as pl
from jax.experimental.pallas import tpu as pltpu
from jax.sharding import PartitionSpec as P

HEADS = 8
KV_HEADS = 4
HD = 256
HALF = HD // 2
SLOTS = 3
EPSILON = 1e-06
SOFT_CAP = 50.0
BF = jnp.bfloat16
F32 = jnp.float32
ALL = ("dp", "fsdp")
STEPS = (1.0, 16.0, 64.0)
VMEM_LIMIT = 60 * 1024 * 1024


def dequantized(codes, width):
    step = STEPS[width]
    if width == 0:
        return codes + BF(0.5)
    return jnp.floor(codes * BF(1.0 / step)) * BF(step) + BF(step / 2)


def rms_norm(values, gain_vector):
    return (
        values
        * lax.rsqrt(jnp.mean(values * values, axis=-1, keepdims=True) + EPSILON)
        * gain_vector
    )


def rotate(values, cosine, sine_part):
    first_half = values[..., :HALF]
    second = values[..., HALF:]
    return jnp.concatenate(
        [first_half * cosine - second * sine_part, second * cosine + first_half * sine_part],
        axis=-1,
    )


def dot(left, right):
    return jnp.dot(left, right, preferred_element_type=F32)


def dot_nt(left, right):
    return lax.dot_general(left, right, (((1,), (1,)), ((), ())), preferred_element_type=F32)


def dot_tn(left, right):
    return lax.dot_general(left, right, (((0,), (0,)), ((), ())), preferred_element_type=F32)


def gated(gate_in, up_in):
    return jax.nn.gelu(gate_in, approximate=True) * up_in


def score_block(qpos_ref, kpos_ref, q, k):
    tanh_part = jnp.tanh(dot_nt(q, k) * (1.0 / SOFT_CAP))
    causal = qpos_ref[...] >= kpos_ref[...]
    exp_scores = jnp.where(causal, jnp.exp(SOFT_CAP * tanh_part), 0.0)
    total = jnp.sum(exp_scores, axis=-1, keepdims=True)
    return tanh_part, exp_scores / total


def attend_kernel(qpos_ref, kpos_ref, q_ref, k_ref, v_ref, o_ref):
    _, probs = score_block(qpos_ref, kpos_ref, q_ref[0], k_ref[0])
    o_ref[0] = dot(probs.astype(BF), v_ref[0]).astype(BF)


def attend_back_kernel(
    qpos_ref,
    kpos_ref,
    qcos_ref,
    qsin_ref,
    kcos_ref,
    ksin_ref,
    q_ref,
    k_ref,
    v_ref,
    do_ref,
    dq_ref,
    dk_ref,
    dv_ref,
):
    q, k, v, do = q_ref[0], k_ref[0], v_ref[0], do_ref[0]

    @pl.when(pl.program_id(1) == 0)
    def _():
        dk_ref[...] = jnp.zeros_like(dk_ref)
        dv_ref[...] = jnp.zeros_like(dv_ref)

    tanh_part, probs = score_block(qpos_ref, kpos_ref, q, k)
    prob_grad = dot_nt(do, v)
    row_dot = jnp.sum(probs * prob_grad, axis=-1, keepdims=True)
    score_grad = (probs * (prob_grad - row_dot) * (1.0 - tanh_part * tanh_part)).astype(BF)
    dq = dot(score_grad, k) * HD ** (-0.5)
    dq_ref[0] = rotate(dq, qcos_ref[...], -qsin_ref[...])
    dk_ref[0] += dot_tn(score_grad, q)
    dv_ref[0] += dot_tn(probs.astype(BF), do)

    @pl.when(pl.program_id(1) == pl.num_programs(1) - 1)
    def _():
        dk_ref[0] = rotate(dk_ref[0], kcos_ref[...], -ksin_ref[...])


def attention_specs(q, keys, tok_rows):
    widths, rows, _ = q.shape
    chunk = 2 * tok_rows
    q_spec = pl.BlockSpec((1, chunk, HD), lambda w, i: (w, i, 0))
    k_spec = pl.BlockSpec((1, keys.shape[1], HD), lambda w, i: (w, 0, 0))
    qpos_spec = pl.BlockSpec((chunk, 1), lambda w, i: (i, 0))
    kpos_spec = pl.BlockSpec((1, keys.shape[1]), lambda w, i: (0, 0))
    turn_specs = [pl.BlockSpec((chunk, HALF), lambda w, i: (i, 0))] * 2
    turn_specs += [pl.BlockSpec((keys.shape[1], HALF), lambda w, i: (0, 0))] * 2
    return (widths, rows // chunk), q_spec, k_spec, qpos_spec, kpos_spec, turn_specs


def attention_cost(q, keys, products):
    pairs = q.shape[0] * q.shape[1] * keys.shape[1]
    return pl.CostEstimate(
        flops=2 * products * pairs * HD,
        bytes_accessed=2 * q.size + 4 * keys.size,
        transcendentals=2 * pairs,
    )


def attend(qpos, kpos, q, k, v, tok_rows):
    grid, q_spec, k_spec, qpos_spec, kpos_spec, _ = attention_specs(q, k, tok_rows)
    return pl.pallas_call(
        attend_kernel,
        grid=grid,
        in_specs=[qpos_spec, kpos_spec, q_spec, k_spec, k_spec],
        out_specs=q_spec,
        out_shape=jax.ShapeDtypeStruct(q.shape, BF),
        compiler_params=pltpu.CompilerParams(vmem_limit_bytes=VMEM_LIMIT),
        cost_estimate=attention_cost(q, k, 2),
        name="attend",
    )(qpos, kpos, q, k, v)


def attend_back(qpos, kpos, turns, q, k, v, do, tok_rows):
    grid, q_spec, k_spec, qpos_spec, kpos_spec, turn_specs = attention_specs(q, k, tok_rows)
    return pl.pallas_call(
        attend_back_kernel,
        grid=grid,
        in_specs=[qpos_spec, kpos_spec, *turn_specs, q_spec, k_spec, k_spec, q_spec],
        out_specs=[q_spec, k_spec, k_spec],
        out_shape=[
            jax.ShapeDtypeStruct(q.shape, F32),
            jax.ShapeDtypeStruct(k.shape, F32),
            jax.ShapeDtypeStruct(k.shape, F32),
        ],
        compiler_params=pltpu.CompilerParams(vmem_limit_bytes=VMEM_LIMIT),
        cost_estimate=attention_cost(q, k, 5),
        name="attend_back",
    )(qpos, kpos, *turns, q, k, v, do)


def project_kernel(
    a_ref, w_hbm, scale_ref, cos_ref, sin_ref, raw_ref, q_ref, kv_ref, kept_hbm, held, sems, out_sems
):
    @pl.when(pl.program_id(0) == 0)
    def _():
        for w in range(SLOTS):
            load_codes(w, (w_hbm,), (held.at[w],), sems)

    copies = keep_copies((held,), (kept_hbm,), out_sems)
    start_on_first(copies)
    a = a_ref[...]
    cosine, sine = cos_ref[...], sin_ref[...]
    for w in range(SLOTS):
        raw = dot(a, held[w])
        raw_ref[w] = raw.astype(BF)
        lin = raw * scale_ref[...]
        q_ref[w] = (rotate(lin[:, :HD], cosine, sine) * HD ** (-0.5)).astype(BF)
        kv_ref[w] = lin[:, HD:]
    wait_on_last(copies)


def project(a, codes, scale, cosine, sine):
    rows, model = a.shape
    cols = codes.shape[1]
    chunk = min(rows, 256)
    turn = pl.BlockSpec((chunk, HALF), lambda i: (i, 0))

    def out(count):
        return pl.BlockSpec((SLOTS, chunk, count), lambda i: (0, i, 0))

    return pl.pallas_call(
        project_kernel,
        grid=(rows // chunk,),
        in_specs=[
            pl.BlockSpec((chunk, model), lambda i: (i, 0)),
            pl.BlockSpec(memory_space=pl.ANY),
            pl.BlockSpec((1, cols), lambda i: (0, 0)),
            turn,
            turn,
        ],
        out_specs=[out(cols), out(HD), out(cols - HD), pl.BlockSpec(memory_space=pl.ANY)],
        out_shape=[
            jax.ShapeDtypeStruct((SLOTS, rows, cols), BF),
            jax.ShapeDtypeStruct((SLOTS, rows, HD), BF),
            jax.ShapeDtypeStruct((SLOTS, rows, cols - HD), F32),
            jax.ShapeDtypeStruct((SLOTS, model, cols), BF),
        ],
        scratch_shapes=[
            pltpu.VMEM((SLOTS, model, cols), BF),
            pltpu.SemaphoreType.DMA((1,)),
            pltpu.SemaphoreType.DMA((1,)),
        ],
        compiler_params=pltpu.CompilerParams(vmem_limit_bytes=VMEM_LIMIT),
        cost_estimate=pl.CostEstimate(
            flops=2 * SLOTS * rows * model * cols,
            bytes_accessed=2 * rows * model + 2 * model * cols + 8 * SLOTS * rows * cols,
            transcendentals=0,
        ),
        name="project",
    )(a, codes, scale[None], cosine, sine)


def heads_kernel(core_ref, own_ref, other_ref, cos_ref, sin_ref, k_ref, v_ref):
    own, other = own_ref[0], other_ref[0]
    cols = own.shape[1] // 2
    first = core_ref[0, 0] == 0
    low = jnp.where(first, own, other)
    high = jnp.where(first, other, own)
    k = jnp.concatenate([low[:, :cols], high[:, :cols]], axis=1)
    k_ref[0] = rotate(k, cos_ref[...], sin_ref[...]).astype(BF)
    v_ref[0] = jnp.concatenate([low[:, cols:], high[:, cols:]], axis=1).astype(BF)


def whole_heads_of(core, own, other, cosine, sine):
    widths, rows, cols = own.shape
    part = rows // 2
    mine = pl.BlockSpec((1, part, cols), lambda w, c: (w, c, 0))
    turn = pl.BlockSpec((part, HALF), lambda w, c: (c, 0))
    return pl.pallas_call(
        heads_kernel,
        grid=(widths, 2),
        in_specs=[
            pl.BlockSpec(memory_space=pltpu.SMEM),
            mine,
            pl.BlockSpec((1, part, cols), lambda w, c: (w, 1 - c, 0)),
            turn,
            turn,
        ],
        out_specs=[mine, mine],
        out_shape=[jax.ShapeDtypeStruct(own.shape, BF)] * 2,
        compiler_params=pltpu.CompilerParams(vmem_limit_bytes=VMEM_LIMIT),
        cost_estimate=pl.CostEstimate(flops=8 * own.size, bytes_accessed=12 * own.size, transcendentals=0),
        name="heads",
    )(core.reshape(1, 1).astype(jnp.int32), own, other, cosine, sine)


def norm_scale(values):
    return lax.rsqrt(jnp.mean(values * values, axis=-1, keepdims=True) + EPSILON)


def norm_back(values, gain, grad):
    r = norm_scale(values)
    weighted = grad * gain
    unit = values * r
    back = r * (weighted - unit * jnp.mean(weighted * unit, axis=-1, keepdims=True))
    return back, jnp.sum(grad * unit, axis=0, keepdims=True)


def output_partial_kernel(width, o_ref, w_ref, low_ref, high_ref, held):
    @pl.when(pl.program_id(0) == 0)
    def _():
        held[...] = dequantized(w_ref[...], width)

    store_halves(low_ref, high_ref, dot(o_ref[0], held[...]).astype(BF))


def output_partial(width, attended, codes):
    rows = attended.shape[1]
    model = codes.shape[1]
    chunk = min(rows // 2, 256)
    specs, shapes = halves_specs(rows, model, chunk)
    return pl.pallas_call(
        functools.partial(output_partial_kernel, width),
        grid=(rows // chunk,),
        in_specs=[
            pl.BlockSpec((1, chunk, HD), lambda i: (width, i, 0)),
            pl.BlockSpec((HD, model), lambda i: (0, 0)),
        ],
        out_specs=specs,
        out_shape=shapes,
        scratch_shapes=[pltpu.VMEM((HD, model), BF)],
        compiler_params=pltpu.CompilerParams(vmem_limit_bytes=VMEM_LIMIT),
        cost_estimate=pl.CostEstimate(
            flops=2 * rows * HD * model, bytes_accessed=2 * rows * model, transcendentals=0
        ),
        name="output_partial",
    )(attended, codes)


def output_norm_kernel(
    part_ref, from_x_ref, from_y_ref, x_ref, scale_ref, post_ref, pre_ref, raw_ref, middle_ref, two_ref
):
    raw = part_ref[...].astype(F32) + from_x_ref[...].astype(F32) + from_y_ref[...].astype(F32)
    raw_ref[...] = raw
    lin = raw * scale_ref[...]
    middle = x_ref[...].astype(F32) + lin * norm_scale(lin) * post_ref[...]
    middle_ref[...] = middle
    two_ref[...] = (middle * norm_scale(middle) * pre_ref[...]).astype(BF)


def output_norm(parts, x, scale, post_gain, pre_gain):
    rows, model = x.shape
    whole = pl.BlockSpec(memory_space=pltpu.VMEM)
    return pl.pallas_call(
        output_norm_kernel,
        in_specs=[whole] * 7,
        out_specs=[whole] * 3,
        out_shape=[
            jax.ShapeDtypeStruct((rows, model), F32),
            jax.ShapeDtypeStruct((rows, model), F32),
            jax.ShapeDtypeStruct((rows, model), BF),
        ],
        compiler_params=pltpu.CompilerParams(vmem_limit_bytes=VMEM_LIMIT),
        cost_estimate=pl.CostEstimate(flops=20 * rows * model, bytes_accessed=18 * rows * model, transcendentals=0),
        name="output_norm",
    )(*parts, x, scale[None], post_gain[None], pre_gain[None])


def loss_kernel(
    live_ref,
    part_ref,
    from_x_ref,
    from_y_ref,
    middle_ref,
    cot_ref,
    scale_ref,
    gain_ref,
    mixed_ref,
    round_ref,
    gain_sum_ref,
    scale_sum_ref,
):
    live = live_ref[0, 0]
    raw = part_ref[...].astype(F32) + from_x_ref[...].astype(F32) + from_y_ref[...].astype(F32)
    scale, gain = scale_ref[...], gain_ref[...]
    lin = raw * scale
    mixed_ref[...] = ((middle_ref[...] + lin * norm_scale(lin) * gain) * live).astype(BF)
    back, gain_sum_ref[...] = norm_back(lin, gain, cot_ref[...].astype(F32) * live)
    round_ref[...] = (back * scale).astype(BF)
    scale_sum_ref[...] = jnp.sum(raw * back, axis=0, keepdims=True)


def loss_step(live, parts, middle, cot, scale, gain):
    rows, model = middle.shape
    whole = pl.BlockSpec(memory_space=pltpu.VMEM)
    return pl.pallas_call(
        loss_kernel,
        in_specs=[pl.BlockSpec(memory_space=pltpu.SMEM)] + [whole] * 7,
        out_specs=[whole] * 4,
        out_shape=[
            jax.ShapeDtypeStruct((rows, model), BF),
            jax.ShapeDtypeStruct((rows, model), BF),
            jax.ShapeDtypeStruct((1, model), F32),
            jax.ShapeDtypeStruct((1, model), F32),
        ],
        compiler_params=pltpu.CompilerParams(vmem_limit_bytes=VMEM_LIMIT),
        cost_estimate=pl.CostEstimate(flops=20 * rows * model, bytes_accessed=16 * rows * model, transcendentals=0),
        name="loss_step",
    )(live, *parts, middle, cot, scale[None], gain[None])


def output_back_kernel(
    live_ref,
    part_ref,
    from_x_ref,
    from_y_ref,
    middle_ref,
    raw_ref,
    cot_ref,
    scale_ref,
    post_ref,
    pre_ref,
    middle_grad_ref,
    round_ref,
    pre_sum_ref,
    post_sum_ref,
    scale_sum_ref,
):
    two_grad = part_ref[...].astype(F32) + from_x_ref[...].astype(F32) + from_y_ref[...].astype(F32)
    back, pre_sum_ref[...] = norm_back(middle_ref[...], pre_ref[...], two_grad)
    middle_grad = cot_ref[...].astype(F32) * live_ref[0, 0] + back
    middle_grad_ref[...] = middle_grad
    raw, scale = raw_ref[...], scale_ref[...]
    lin_grad, post_sum_ref[...] = norm_back(raw * scale, post_ref[...], middle_grad)
    scale_sum_ref[...] = jnp.sum(raw * lin_grad, axis=0, keepdims=True)
    round_ref[...] = (lin_grad * scale).astype(BF)


def output_back(live, parts, middle, raw, cot, scale, post_gain, pre_gain):
    rows, model = middle.shape
    whole = pl.BlockSpec(memory_space=pltpu.VMEM)
    return pl.pallas_call(
        output_back_kernel,
        in_specs=[pl.BlockSpec(memory_space=pltpu.SMEM)] + [whole] * 9,
        out_specs=[whole] * 5,
        out_shape=[
            jax.ShapeDtypeStruct((rows, model), F32),
            jax.ShapeDtypeStruct((rows, model), BF),
            jax.ShapeDtypeStruct((1, model), F32),
            jax.ShapeDtypeStruct((1, model), F32),
            jax.ShapeDtypeStruct((1, model), F32),
        ],
        compiler_params=pltpu.CompilerParams(vmem_limit_bytes=VMEM_LIMIT),
        cost_estimate=pl.CostEstimate(flops=40 * rows * model, bytes_accessed=24 * rows * model, transcendentals=0),
        name="output_back",
    )(live, *parts, middle, raw, cot, scale[None], post_gain[None], pre_gain[None])


def head_back_kernel(width, count, *refs):
    pieces = refs[:count]
    w_ref, do_ref, joined, rows_held, w_held, piece_sems, out_sems = refs[count:]
    gathered = piece_copies(pieces, rows_held, piece_sems)
    start_on_first(gathered)

    @pl.when(pl.program_id(0) == 0)
    def _():
        w_held[...] = dequantized(w_ref[...], width)
        for copy in gathered:
            copy.wait()

    copies = keep_copies((rows_held,), (joined,), out_sems)
    start_on_first(copies)
    chunk = do_ref.shape[0]
    part = rows_held[pl.ds(pl.multiple_of(pl.program_id(0) * chunk, chunk), chunk)]
    do_ref[...] = dot_nt(part, w_held[...]).astype(BF)
    wait_on_last(copies)


def head_back(width, pieces, codes):
    rows = sum(piece.shape[0] for piece in pieces)
    model = codes.shape[1]
    chunk = min(rows, 256)
    whole = pl.BlockSpec(memory_space=pl.ANY)
    return pl.pallas_call(
        functools.partial(head_back_kernel, width, len(pieces)),
        grid=(rows // chunk,),
        in_specs=[whole] * len(pieces) + [pl.BlockSpec((HD, model), lambda i: (0, 0))],
        out_specs=[pl.BlockSpec((chunk, HD), lambda i: (i, 0)), whole],
        out_shape=[
            jax.ShapeDtypeStruct((rows, HD), BF),
            jax.ShapeDtypeStruct((rows, model), BF),
        ],
        scratch_shapes=[
            pltpu.VMEM((rows, model), BF),
            pltpu.VMEM((HD, model), BF),
            pltpu.SemaphoreType.DMA((len(pieces),)),
            pltpu.SemaphoreType.DMA((1,)),
        ],
        compiler_params=pltpu.CompilerParams(vmem_limit_bytes=VMEM_LIMIT),
        cost_estimate=pl.CostEstimate(
            flops=2 * rows * HD * model, bytes_accessed=4 * rows * model, transcendentals=0
        ),
        name="head_back",
    )(*pieces, codes)


def join_kernel(starts, *refs):
    result = refs[-1]
    step = pl.program_id(0)
    for piece, start in zip(refs[:-1], starts):

        @pl.when(step == start // result.shape[0])
        def _(piece=piece, start=start):
            result[pl.ds(start % result.shape[0], piece.shape[0])] = piece[...]


def join(*pieces):
    starts = [0]
    for piece in pieces:
        starts.append(starts[-1] + piece.shape[0])
    total, cols = starts[-1], pieces[0].shape[1]
    rows = pieces[0].shape[0]
    return pl.pallas_call(
        functools.partial(join_kernel, tuple(starts[:-1])),
        grid=(total // rows,),
        in_specs=[pl.BlockSpec(piece.shape, lambda i: (0, 0)) for piece in pieces],
        out_specs=pl.BlockSpec((rows, cols), lambda i: (i, 0)),
        out_shape=jax.ShapeDtypeStruct((total, cols), pieces[0].dtype),
        compiler_params=pltpu.CompilerParams(vmem_limit_bytes=VMEM_LIMIT),
        cost_estimate=pl.CostEstimate(flops=0, bytes_accessed=4 * total * cols, transcendentals=0),
        name="join",
    )(*pieces)


GELU_A = 0.7978845608028654
GELU_B = 0.044715


def load_codes(width, codes, held, sems):
    copies = [
        pltpu.make_async_copy(source, target, sems.at[i])
        for i, (source, target) in enumerate(zip(codes, held))
    ]
    for copy in copies:
        copy.start()
    for copy, target in zip(copies, held):
        copy.wait()
        rows = target.shape[0]
        step = 128 if rows % 128 == 0 else 16

        def turn(i, carry, target=target, step=step):
            part = pl.ds(pl.multiple_of(i * step, step), step)
            target[part] = dequantized(target[part], width)
            return carry

        lax.fori_loop(0, rows // step, turn, 0)


def halves_specs(rows, model, chunk):
    steps = rows // chunk // 2
    low = pl.BlockSpec((chunk, model), lambda i: (jnp.minimum(i, steps - 1), 0))
    high = pl.BlockSpec((chunk, model), lambda i: (jnp.maximum(i - steps, 0), 0))
    return [low, high], [jax.ShapeDtypeStruct((rows // 2, model), BF)] * 2


def store_halves(low_ref, high_ref, value):
    step, steps = pl.program_id(0), pl.num_programs(0)

    @pl.when(step < steps // 2)
    def _():
        low_ref[...] = value

    @pl.when(step >= steps // 2)
    def _():
        high_ref[...] = value


def keep_copies(held, kept, sems):
    return [
        pltpu.make_async_copy(source, target, sems.at[i])
        for i, (source, target) in enumerate(zip(held, kept))
    ]


def start_on_first(copies):
    @pl.when(pl.program_id(0) == 0)
    def _():
        for copy in copies:
            copy.start()


def wait_on_last(copies):
    @pl.when(pl.program_id(0) == pl.num_programs(0) - 1)
    def _():
        for copy in copies:
            copy.wait()


def piece_copies(pieces, held, sems):
    copies = []
    at = 0
    for i, piece in enumerate(pieces):
        rows = piece.shape[0]
        copies.append(pltpu.make_async_copy(piece, held.at[pl.ds(at, rows)], sems.at[i]))
        at += rows
    return copies


def ffn_in_kernel(width, count, *refs):
    pieces = refs[:count]
    (
        g_hbm,
        u_hbm,
        gs_ref,
        us_ref,
        gate_ref,
        up_ref,
        hidden_ref,
        a_hbm,
        gw_hbm,
        uw_hbm,
        a_held,
        g_held,
        u_held,
        piece_sems,
        sems,
        out_sems,
    ) = refs[count:]
    gathered = piece_copies(pieces, a_held, piece_sems)
    start_on_first(gathered)

    @pl.when(pl.program_id(0) == 0)
    def _():
        load_codes(width, (g_hbm, u_hbm), (g_held, u_held), sems)
        for copy in gathered:
            copy.wait()

    copies = keep_copies((a_held, g_held, u_held), (a_hbm, gw_hbm, uw_hbm), out_sems)
    start_on_first(copies)
    chunk = gate_ref.shape[0]
    a = a_held[pl.ds(pl.multiple_of(pl.program_id(0) * chunk, chunk), chunk)]
    gate = dot(a, g_held[...])
    up = dot(a, u_held[...])
    gate_ref[...] = gate.astype(BF)
    up_ref[...] = up.astype(BF)
    gate = gate * gs_ref[...]
    inner = jnp.tanh(GELU_A * (gate + GELU_B * gate * gate * gate))
    hidden_ref[...] = (0.5 * gate * (1.0 + inner) * (up * us_ref[...])).astype(BF)
    wait_on_last(copies)


def ffn_in(width, pieces, gate_codes, up_codes, g_scale, u_scale):
    rows = sum(piece.shape[0] for piece in pieces)
    model, features = gate_codes.shape
    chunk = min(rows, 256)
    whole = pl.BlockSpec(memory_space=pl.ANY)
    vector = pl.BlockSpec((1, features), lambda i: (0, 0))
    block = pl.BlockSpec((chunk, features), lambda i: (i, 0))
    return pl.pallas_call(
        functools.partial(ffn_in_kernel, width, len(pieces)),
        grid=(rows // chunk,),
        in_specs=[whole] * len(pieces) + [whole, whole, vector, vector],
        out_specs=[block] * 3 + [whole] * 3,
        out_shape=[jax.ShapeDtypeStruct((rows, features), BF)] * 3
        + [jax.ShapeDtypeStruct((rows, model), BF)]
        + [jax.ShapeDtypeStruct((model, features), BF)] * 2,
        scratch_shapes=[
            pltpu.VMEM((rows, model), BF),
            pltpu.VMEM((model, features), BF),
            pltpu.VMEM((model, features), BF),
            pltpu.SemaphoreType.DMA((len(pieces),)),
            pltpu.SemaphoreType.DMA((2,)),
            pltpu.SemaphoreType.DMA((3,)),
        ],
        compiler_params=pltpu.CompilerParams(vmem_limit_bytes=VMEM_LIMIT),
        cost_estimate=pl.CostEstimate(
            flops=4 * rows * model * features,
            bytes_accessed=2 * (rows * model + 2 * model * features + 3 * rows * features),
            transcendentals=rows * features,
        ),
        name="ffn_in",
    )(*pieces, gate_codes, up_codes, g_scale[None], u_scale[None])


def down_grad_kernel(counts, *refs):
    pieces, refs = refs[: sum(counts)], refs[sum(counts) :]
    widths = len(counts)
    h_refs, scale_ref, out_ref = refs[:widths], refs[widths], refs[widths + 1]
    joined, held = refs[widths + 2 : 2 * widths + 2], refs[2 * widths + 2]
    piece_sems, out_sems = refs[2 * widths + 3 :]
    groups = []
    at = 0
    for w, count in enumerate(counts):
        groups.append(piece_copies(pieces[at : at + count], held.at[w], piece_sems.at[w]))
        at += count
    for group in groups:
        start_on_first(group)
    copies = keep_copies([held.at[w] for w in range(widths)], joined, out_sems)
    first = pl.program_id(0) == 0
    product = None
    for w in range(widths):

        @pl.when(first)
        def _(w=w):
            for copy in groups[w]:
                copy.wait()
            copies[w].start()

        part = dot_tn(h_refs[w][...], held[w])
        product = part if product is None else product + part
    out_ref[...] = (product / scale_ref[...]).astype(BF)
    wait_on_last(copies)


def down_gradient(hiddens, piece_lists, scale):
    rows, features = hiddens[0].shape
    model = scale.shape[0]
    widths = len(hiddens)
    counts = tuple(len(pieces) for pieces in piece_lists)
    chunk = 128 if features % 128 == 0 else features
    whole = pl.BlockSpec(memory_space=pl.ANY)
    return pl.pallas_call(
        functools.partial(down_grad_kernel, counts),
        grid=(features // chunk,),
        in_specs=[whole] * sum(counts)
        + [pl.BlockSpec((rows, chunk), lambda i: (0, i))] * widths
        + [pl.BlockSpec((1, model), lambda i: (0, 0))],
        out_specs=[pl.BlockSpec((chunk, model), lambda i: (i, 0))] + [whole] * widths,
        out_shape=[jax.ShapeDtypeStruct((features, model), BF)]
        + [jax.ShapeDtypeStruct((rows, model), BF)] * widths,
        scratch_shapes=[
            pltpu.VMEM((widths, rows, model), BF),
            pltpu.SemaphoreType.DMA((widths, max(counts))),
            pltpu.SemaphoreType.DMA((widths,)),
        ],
        compiler_params=pltpu.CompilerParams(vmem_limit_bytes=VMEM_LIMIT),
        cost_estimate=pl.CostEstimate(
            flops=2 * widths * rows * model * features,
            bytes_accessed=2 * (2 * widths * rows * model + features * (model + widths * rows)),
            transcendentals=0,
        ),
        name="down_grad",
    )(*[piece for pieces in piece_lists for piece in pieces], *hiddens, scale[None])


def ffn_out_kernel(width, h_ref, d_hbm, low_ref, high_ref, dw_hbm, d_held, sems, out_sems):
    @pl.when(pl.program_id(0) == 0)
    def _():
        load_codes(width, (d_hbm,), (d_held,), sems)

    copies = keep_copies((d_held,), (dw_hbm,), out_sems)
    start_on_first(copies)
    store_halves(low_ref, high_ref, dot(h_ref[...], d_held[...]).astype(BF))
    wait_on_last(copies)


def ffn_out(width, hidden, down_codes):
    rows, features = hidden.shape
    model = down_codes.shape[1]
    chunk = min(rows // 2, 256)
    whole = pl.BlockSpec(memory_space=pl.ANY)
    specs, shapes = halves_specs(rows, model, chunk)
    return pl.pallas_call(
        functools.partial(ffn_out_kernel, width),
        grid=(rows // chunk,),
        in_specs=[pl.BlockSpec((chunk, features), lambda i: (i, 0)), whole],
        out_specs=specs + [whole],
        out_shape=shapes + [jax.ShapeDtypeStruct((features, model), BF)],
        scratch_shapes=[
            pltpu.VMEM((features, model), BF),
            pltpu.SemaphoreType.DMA((1,)),
            pltpu.SemaphoreType.DMA((1,)),
        ],
        compiler_params=pltpu.CompilerParams(vmem_limit_bytes=VMEM_LIMIT),
        cost_estimate=pl.CostEstimate(
            flops=2 * rows * model * features,
            bytes_accessed=2 * (rows * model + 2 * model * features + rows * features),
            transcendentals=0,
        ),
        name="ffn_out",
    )(hidden, down_codes)


def ffn_back_kernel(
    dr_ref,
    gate_ref,
    up_ref,
    d_hbm,
    g_hbm,
    u_hbm,
    gs_ref,
    us_ref,
    after_hbm,
    low_ref,
    high_ref,
    gr_ref,
    ur_ref,
    gsum_ref,
    usum_ref,
    d_held,
    g_held,
    u_held,
    sems,
):
    del after_hbm
    first = pl.program_id(0) == 0
    copies = keep_copies((d_hbm, g_hbm, u_hbm), (d_held, g_held, u_held), sems)
    start_on_first(copies)

    @pl.when(first)
    def _():
        gsum_ref[...] = jnp.zeros_like(gsum_ref)
        usum_ref[...] = jnp.zeros_like(usum_ref)
        copies[0].wait()

    hidden_grad = dot_nt(dr_ref[...], d_held[...])
    gate_raw = gate_ref[...].astype(F32)
    up_raw = up_ref[...].astype(F32)
    gate = gate_raw * gs_ref[...]
    up = up_raw * us_ref[...]
    square = gate * gate
    inner = jnp.tanh(GELU_A * (gate + GELU_B * gate * square))
    half_sum = 0.5 * (1.0 + inner)
    slope = half_sum + 0.5 * gate * (1.0 - inner * inner) * (
        GELU_A * (1.0 + 3.0 * GELU_B * square)
    )
    gate_grad = hidden_grad * up * slope
    up_grad = hidden_grad * (gate * half_sum)
    gsum_ref[...] += jnp.sum(gate_raw * gate_grad, axis=0, keepdims=True)
    usum_ref[...] += jnp.sum(up_raw * up_grad, axis=0, keepdims=True)
    gate_round = (gate_grad * gs_ref[...]).astype(BF)
    up_round = (up_grad * us_ref[...]).astype(BF)
    gr_ref[...] = gate_round
    ur_ref[...] = up_round

    @pl.when(first)
    def _():
        copies[1].wait()
        copies[2].wait()

    store_halves(
        low_ref,
        high_ref,
        (dot_nt(gate_round, g_held[...]) + dot_nt(up_round, u_held[...])).astype(BF),
    )


def ffn_back(down_round, gate_raw, up_raw, down_w, gate_w, up_w, g_scale, u_scale, after):
    rows, model = down_round.shape
    features = gate_w.shape[1]
    chunk = min(rows // 2, 256)
    whole = pl.BlockSpec(memory_space=pl.ANY)
    vector = pl.BlockSpec((1, features), lambda i: (0, 0))
    block = pl.BlockSpec((chunk, features), lambda i: (i, 0))
    wide = pl.BlockSpec((chunk, model), lambda i: (i, 0))
    specs, shapes = halves_specs(rows, model, chunk)
    return pl.pallas_call(
        ffn_back_kernel,
        grid=(rows // chunk,),
        in_specs=[wide, block, block, whole, whole, whole, vector, vector, whole],
        out_specs=specs + [block, block, vector, vector],
        out_shape=shapes
        + [
            jax.ShapeDtypeStruct((rows, features), BF),
            jax.ShapeDtypeStruct((rows, features), BF),
            jax.ShapeDtypeStruct((1, features), F32),
            jax.ShapeDtypeStruct((1, features), F32),
        ],
        scratch_shapes=[
            pltpu.VMEM((features, model), BF),
            pltpu.VMEM((model, features), BF),
            pltpu.VMEM((model, features), BF),
            pltpu.SemaphoreType.DMA((3,)),
        ],
        compiler_params=pltpu.CompilerParams(vmem_limit_bytes=VMEM_LIMIT),
        cost_estimate=pl.CostEstimate(
            flops=6 * rows * model * features,
            bytes_accessed=2 * (2 * rows * model + 3 * model * features + 4 * rows * features),
            transcendentals=rows * features,
        ),
        name="ffn_back",
    )(down_round, gate_raw, up_raw, down_w, gate_w, up_w, g_scale[None], u_scale[None], after)


def project_back_kernel(round_ref, w_hbm, low_ref, high_ref, held, sems):
    copies = keep_copies((w_hbm,), (held,), sems)
    start_on_first(copies)

    @pl.when(pl.program_id(0) == 0)
    def _():
        copies[0].wait()

    product = dot_nt(round_ref[0], held[0])
    for w in range(1, SLOTS):
        product = product + dot_nt(round_ref[w], held[w])
    store_halves(low_ref, high_ref, product.astype(BF))


def project_back(rounded, weights):
    _, rows, cols = rounded.shape
    model = weights.shape[1]
    chunk = min(rows // 2, 256)
    specs, shapes = halves_specs(rows, model, chunk)
    return pl.pallas_call(
        project_back_kernel,
        grid=(rows // chunk,),
        in_specs=[
            pl.BlockSpec((SLOTS, chunk, cols), lambda i: (0, i, 0)),
            pl.BlockSpec(memory_space=pl.ANY),
        ],
        out_specs=specs,
        out_shape=shapes,
        scratch_shapes=[pltpu.VMEM((SLOTS, model, cols), BF), pltpu.SemaphoreType.DMA((1,))],
        compiler_params=pltpu.CompilerParams(vmem_limit_bytes=VMEM_LIMIT),
        cost_estimate=pl.CostEstimate(
            flops=2 * SLOTS * rows * model * cols,
            bytes_accessed=2 * (rows * model + SLOTS * cols * (model + rows)),
            transcendentals=0,
        ),
        name="project_back",
    )(rounded, weights)


def shards(
    tokens,
    query_codes,
    key_codes,
    value_codes,
    output_codes,
    gate_codes,
    up_codes,
    down_codes,
    query_scale,
    key_scale,
    value_scale,
    output_scale,
    gate_scale,
    up_scale,
    down_scale,
    pre_attn_gain,
    post_attn_gain,
    pre_ffw_gain,
    post_ffw_gain,
    slot_width,
    slot_live,
    cotangent,
):
    planes = lax.axis_size("dp")
    width = lax.axis_size("fsdp")
    devices = planes * width
    group_count = width // 8
    rank = lax.axis_index("fsdp")
    me = lax.axis_index("dp") * width + rank
    t_index, group = rank % 8, rank // 8
    core = rank % 2
    CORE, X, Y = 1, 2, 4
    groups = None
    if group_count > 1:
        groups = [[g * 8 + j for j in range(8)] for g in range(group_count)]
        across = [[g * 8 + j for g in range(group_count)] for j in range(8)]

    def swap(values, mask):
        return lax.ppermute(values, "fsdp", [(i, i ^ mask) for i in range(width)])

    def swap_all(values, mask):
        return lax.ppermute(values, ALL, [(i, i ^ mask) for i in range(devices)])

    tok_rows, model = tokens.shape
    group_rows = 8 * tok_rows
    d_rows = query_codes.shape[0]
    o_rows = output_codes.shape[0]
    ff_rows = down_codes.shape[0]
    q_cols = query_codes.shape[1] // 8
    k_cols = key_codes.shape[1] // 8
    ff_cols = ff_rows * planes * group_count
    widths = range(SLOTS)

    def tp_pieces(block):
        from_x = swap(block, X)
        from_y = swap(block, Y)
        cut = block.shape[0] // 2
        first = swap(from_y[:cut], X)
        second = swap(from_x[cut:], Y)
        same = [block, from_x, from_y, first, second]
        return same + [swap(piece, CORE) for piece in same]

    def tp_gather(block):
        return join(*tp_pieces(block))

    def after(values, *others):
        return lax.optimization_barrier((values, *others))[0]

    def core_sum(low, high):
        return (low.astype(F32) + swap(high, CORE).astype(F32)).astype(BF)

    def tp_scatter(low, high):
        return plane_sum(core_sum(low, high))

    def plane_sum(pair):
        rows = pair.shape[0] // 4
        cut = rows // 2
        pair = pair.reshape(2, 2, rows, model)
        got_x = swap(pair[1, 1, :cut], X)
        got_y = swap(pair[1, 1, cut:], Y)
        for_x = jnp.concatenate(
            [pair[0, 1, :cut], (pair[0, 1, cut:].astype(F32) + got_y.astype(F32)).astype(BF)]
        )
        for_y = jnp.concatenate(
            [(pair[1, 0, :cut].astype(F32) + got_x.astype(F32)).astype(BF), pair[1, 0, cut:]]
        )
        return pair[0, 0], swap(for_x, X), swap(for_y, Y)

    def total(parts):
        return sum(part.astype(F32) for part in parts)

    def tp_columns(blocks):
        return lax.all_to_all(blocks, "fsdp", 0, 0, tiled=True, axis_index_groups=groups)

    def gather_rows(rows):
        if group_count > 1:
            rows = lax.all_gather(rows, "fsdp", axis=0, tiled=True, axis_index_groups=across)
        return lax.all_gather(rows, "dp", axis=0, tiled=True)

    def scatter_rows(grad):
        rows = lax.psum_scatter(grad, "dp", scatter_dimension=0, tiled=True)
        if group_count > 1:
            rows = lax.psum_scatter(
                rows, "fsdp", scatter_dimension=0, tiled=True, axis_index_groups=across
            )
        return rows

    small = jnp.concatenate(
        [query_scale, key_scale, value_scale, output_scale, gate_scale, up_scale, down_scale]
    )
    all_small = small[None]
    for bit in range(devices.bit_length() - 1):
        all_small = jnp.concatenate([all_small, swap_all(all_small, 1 << bit)], axis=0)
    order = jnp.arange(devices, dtype=jnp.int32) ^ me
    all_small = all_small[order]
    cuts = []
    at = 0
    for vector in (
        query_scale,
        key_scale,
        value_scale,
        output_scale,
        gate_scale,
        up_scale,
        down_scale,
    ):
        cuts.append(all_small[:, at : at + vector.shape[0]].reshape(-1))
        at += vector.shape[0]
    q_scale_all, k_scale_all, v_scale_all, o_scale_all, g_scale_all, u_scale_all, d_scale_all = cuts

    def own_ff(vector):
        cut = vector.reshape(planes * group_count, 8, ff_rows)
        return lax.dynamic_index_in_dim(cut, t_index, 1, keepdims=False).reshape(ff_cols)

    qkv_scale = jnp.concatenate(
        [
            lax.dynamic_slice_in_dim(q_scale_all, t_index * q_cols, q_cols),
            lax.dynamic_slice_in_dim(k_scale_all, t_index * k_cols, k_cols),
            lax.dynamic_slice_in_dim(v_scale_all, t_index * k_cols, k_cols),
        ]
    )
    g_scale = own_ff(g_scale_all)
    u_scale = own_ff(u_scale_all)

    def by_head(codes):
        return codes.reshape(codes.shape[0], 8, -1).transpose(1, 0, 2)

    def by_head_back(blocks):
        return blocks.transpose(1, 0, 2).reshape(blocks.shape[1], -1)

    def by_ff(codes):
        cut = codes.reshape(d_rows, planes * group_count, 8, ff_rows)
        return cut.transpose(2, 0, 1, 3).reshape(8, d_rows, ff_cols)

    def by_ff_back(blocks):
        cut = blocks.reshape(8, d_rows, planes * group_count, ff_rows)
        return cut.transpose(1, 2, 0, 3).reshape(d_rows, 8 * ff_cols)

    def merged(blocks):
        return blocks.reshape(8 * d_rows, blocks.shape[2])

    qkv_blocks = jnp.concatenate(
        [by_head(query_codes), by_head(key_codes), by_head(value_codes)], axis=2
    )
    inputs = tokens.astype(F32)
    qkv_codes = gather_rows(merged(tp_columns(qkv_blocks)))
    normed = tp_gather(rms_norm(inputs, pre_attn_gain).astype(BF))

    whole_heads = group_count == 1 and 8 % planes == 0
    heads_per_plane = max(1, 8 // planes)

    def turn(step):
        pairs = []
        for source in range(8):
            plane = (source + step) % planes
            pairs.append((source, plane * heads_per_plane + source // planes))
        return pairs

    def pieces_to_heads(pieces):
        result = jnp.zeros_like(pieces)
        for step in range(planes):
            piece = lax.dynamic_index_in_dim(pieces, (rank + step) % planes, 0, keepdims=False)
            moved = lax.ppermute(piece, "fsdp", turn(step))
            place = (rank // heads_per_plane - step) % planes
            result = lax.dynamic_update_index_in_dim(result, moved, place, 0)
        return result

    def heads_to_pieces(pieces):
        result = jnp.zeros_like(pieces)
        for step in range(planes):
            place = (rank // heads_per_plane - step) % planes
            piece = lax.dynamic_index_in_dim(pieces, place, 0, keepdims=False)
            moved = lax.ppermute(piece, "fsdp", [(b, a) for a, b in turn(step)])
            result = lax.dynamic_update_index_in_dim(result, moved, (rank + step) % planes, 0)
        return result

    gate_mine = merged(tp_columns(by_ff(after(gate_codes, normed, qkv_scale))))
    normed, gate_mine = lax.optimization_barrier((normed, gate_mine))
    gate_codes_t = gather_rows(gate_mine)
    output_pieces = gather_rows(output_codes)

    blocks_at = jnp.stack([t_index ^ (c + 2 * x + 4 * y) for c in (0, 1) for y in (0, 1) for x in (0, 1)])
    positions = ((group * 8 + blocks_at) * tok_rows)[:, None] + jnp.arange(tok_rows, dtype=jnp.int32)
    positions = positions.reshape(group_rows)
    far = jnp.int32(1 << 30)
    key_positions = []
    for back in range(group_count):
        earlier = positions - back * group_rows
        key_positions.append(jnp.where(earlier >= 0, earlier, far))
    kpos = jnp.concatenate(key_positions)[None, :]
    qpos = positions[:, None]
    inv_rates = 10000.0 ** (-jnp.arange(HALF, dtype=F32) / HALF)
    angles = positions.astype(F32)[:, None] * inv_rates[None, :]
    cosine, sine = jnp.cos(angles), jnp.sin(angles)
    key_angles = jnp.concatenate(
        [(positions - back * group_rows).astype(F32) for back in range(group_count)]
    )[:, None] * inv_rates[None, :]

    qkv_raw, q, kv_own, qkv_w = project(normed, qkv_codes, qkv_scale, cosine, sine)
    k_near, v_near = whole_heads_of(core, kv_own, swap(kv_own, CORE), cosine, sine)

    if whole_heads:
        head_codes = pieces_to_heads(output_pieces.reshape(planes, o_rows, model)).reshape(HD, model)
    else:
        every = lax.all_gather(output_codes, ALL, axis=0, tiled=True)
        head_codes = lax.dynamic_slice_in_dim(every, t_index * HD, HD, 0)

    def turned(values):
        middle_row = group_rows // 2
        return jnp.concatenate([values[..., middle_row:, :], values[..., :middle_row, :]], axis=-2)

    def back_pairs(back):
        return [(i, i + 8 * back) for i in range(width) if i + 8 * back < width]

    k_parts, v_parts = [k_near], [v_near]
    for back in range(1, group_count):
        k_parts.append(lax.ppermute(k_near, "fsdp", back_pairs(back)))
        v_parts.append(lax.ppermute(v_near, "fsdp", back_pairs(back)))
    k_all = jnp.concatenate(k_parts, axis=1)
    v_all = jnp.concatenate(v_parts, axis=1)
    attended = attend(qpos, kpos, q, k_all, v_all, tok_rows)

    up_codes_t = gather_rows(merged(tp_columns(by_ff(after(up_codes, k_near)))))
    down_codes_t = gather_rows(down_codes)

    slot_of, live_of, cot_of = [], [], []
    for w in widths:
        slot = jnp.int32(0)
        for s in range(SLOTS):
            slot = jnp.where(slot_width[0, s] == w, s, slot)
        slot_of.append(slot)
        live = lax.dynamic_index_in_dim(slot_live[0], slot, 0, keepdims=False)
        live_of.append(live.astype(F32).reshape(1, 1))
        cot_of.append(lax.dynamic_index_in_dim(cotangent, slot, 0, keepdims=False))
    kept = [dict() for w in widths]
    for w in widths:
        k = kept[w]
        blocks = attended if w == 0 else after(attended, kept[w - 1]["low"])
        k["low"], high = output_partial(w, blocks, head_codes)
        k["out_raw"], k["middle"], two = output_norm(
            tp_scatter(k["low"], high), tokens, o_scale_all, post_attn_gain, pre_ffw_gain
        )
        k["two_pieces"] = tp_pieces(two)
    for w in widths:
        k = kept[w]
        (
            k["gate_raw"],
            k["up_raw"],
            k["hidden"],
            k["normed_two"],
            k["gate_w"],
            k["up_w"],
        ) = ffn_in(w, k["two_pieces"], gate_codes_t, up_codes_t, g_scale, u_scale)

    hiddens = lax.optimization_barrier(tuple(kept[w]["hidden"] for w in widths))
    for w in widths:
        k = kept[w]
        k["hidden"] = hiddens[w] if w == 0 else after(hiddens[w], kept[w - 1]["down_w"])
        if w == 2:
            k["hidden"], kept[0]["pair"] = lax.optimization_barrier((k["hidden"], kept[0]["pair"]))
        low, high, k["down_w"] = ffn_out(w, k["hidden"], down_codes_t)
        k["pair"] = core_sum(low, high)
    for w in widths:
        kept[w]["down_parts"] = plane_sum(kept[w]["pair"])

    mixed = jnp.zeros((SLOTS, tok_rows, model), BF)
    for w in widths:
        k = kept[w]
        cot = cot_of[w] if w == 0 else after(cot_of[w], kept[w - 1]["gain_four"])
        result, rounded, k["gain_four"], k["down_scale_sum"] = loss_step(
            live_of[w], k["down_parts"], k["middle"], cot, d_scale_all, post_ffw_gain
        )
        mixed = lax.dynamic_update_index_in_dim(mixed, result, slot_of[w], 0)
        k["down_pieces"] = tp_pieces(rounded)
    down_total, *down_rounds = down_gradient(
        [kept[w]["hidden"] for w in widths], [kept[w]["down_pieces"] for w in widths], d_scale_all
    )
    down_sum = scatter_rows(down_total)
    for w in widths:
        k = kept[w]
        low, high, k["gate_round"], k["up_round"], k["gate_sum"], k["up_sum"] = ffn_back(
            down_rounds[w],
            k["gate_raw"],
            k["up_raw"],
            k["down_w"],
            k["gate_w"],
            k["up_w"],
            g_scale,
            u_scale,
            down_total if w == 0 else kept[w - 1]["gate_sum"],
        )
        k["two_parts"] = tp_scatter(low, high)
    normed_two_rows = jnp.concatenate([kept[w]["normed_two"] for w in widths], axis=0)
    gate_rounds = [kept[w]["gate_round"] for w in widths]
    *gate_rounds, down_sum = lax.optimization_barrier((*gate_rounds, down_sum))
    gate_total = dot_tn(normed_two_rows, jnp.concatenate(gate_rounds, axis=0))
    gate_sum = scatter_rows((gate_total / g_scale).astype(BF))
    for w in widths:
        k = kept[w]
        cot = cot_of[w] if w == 0 else after(cot_of[w], kept[w - 1]["gain_two"])
        k["middle_grad"], rounded, k["gain_three"], k["gain_two"], k["out_scale_sum"] = output_back(
            live_of[w],
            k["two_parts"],
            k["middle"],
            k["out_raw"],
            cot,
            o_scale_all,
            post_attn_gain,
            pre_ffw_gain,
        )
        k["out_pieces"] = tp_pieces(rounded)
    up_rounds = [kept[w]["up_round"] for w in widths]
    *up_rounds, _ = lax.optimization_barrier((*up_rounds, kept[2]["gain_two"]))
    up_total = dot_tn(normed_two_rows, jnp.concatenate(up_rounds, axis=0))
    up_total, gate_sum = lax.optimization_barrier(((up_total / u_scale).astype(BF), gate_sum))
    up_sum = scatter_rows(up_total)
    for w in widths:
        k = kept[w]
        codes = head_codes if w == 0 else after(head_codes, kept[w - 1]["o_grad"])
        k["o_grad"], k["out_round"] = head_back(w, k["out_pieces"], codes)

    o_grad = jnp.stack([kept[w]["o_grad"] for w in widths])
    turns = (cosine, sine, jnp.cos(key_angles), jnp.sin(key_angles))
    out_total = dot_tn(
        attended.reshape(SLOTS * group_rows, HD),
        jnp.concatenate([kept[w]["out_round"] for w in widths], axis=0),
    )
    out_total = (out_total / o_scale_all).astype(BF)
    if whole_heads:
        out_pieces = heads_to_pieces(out_total.reshape(planes, o_rows, model))
        out_pieces = out_pieces.reshape(planes * o_rows, model)
    else:
        whole = jnp.zeros((HEADS * HD, model), BF)
        out_pieces = lax.dynamic_update_slice_in_dim(whole, out_total, t_index * HD, 0)
    q_grad, dk, dv = attend_back(qpos, kpos, turns, q, k_all, v_all, o_grad, tok_rows)
    other = 1 - core

    def half_of(values, which):
        return lax.dynamic_slice_in_dim(values, which * k_cols, k_cols, values.ndim - 1)

    kv_grad = None
    for back in range(group_count):
        part = slice(back * group_rows, (back + 1) * group_rows)
        dkv = jnp.concatenate([half_of(dk[:, part], core), half_of(dv[:, part], core)], axis=-1)
        gone = jnp.concatenate([half_of(dk[:, part], other), half_of(dv[:, part], other)], axis=-1)
        dkv = dkv + turned(swap(gone, CORE))
        if back == 0:
            kv_grad = dkv
        else:
            pairs = [(b, a) for a, b in back_pairs(back)]
            kv_grad = kv_grad + lax.ppermute(dkv, "fsdp", pairs)
    qkv_grad = jnp.concatenate([q_grad, kv_grad], axis=-1)
    qkv_round = (qkv_grad * qkv_scale).astype(BF)
    qkv_scale_acc = jnp.sum(qkv_raw.astype(F32) * qkv_grad, axis=(0, 1))
    qkv_rows = jnp.sum(qkv_round.astype(F32), axis=0).astype(BF)
    qkv_total = (dot_tn(normed, qkv_rows) / qkv_scale).astype(BF)
    qkv_total, out_pieces = lax.optimization_barrier((qkv_total, out_pieces))
    qkv_sum = scatter_rows(qkv_total)
    if whole_heads:
        out_sum = scatter_rows(out_pieces)
    else:
        out_sum = lax.psum_scatter(out_pieces, ALL, scatter_dimension=0, tiled=True)
    normed_parts = tp_scatter(*project_back(qkv_round, qkv_w))
    gate_grad = by_ff_back(tp_columns(gate_sum.reshape(8, d_rows, ff_cols))).astype(F32)
    up_grad = by_ff_back(tp_columns(up_sum.reshape(8, d_rows, ff_cols))).astype(F32)
    down_grad = down_sum.reshape(ff_rows, model).astype(F32)
    normed_parts, qkv_sum, gate_grad, up_grad, down_grad = lax.optimization_barrier(
        (normed_parts, qkv_sum, gate_grad, up_grad, down_grad)
    )
    normed_grad = total(normed_parts)
    _, pull_one = jax.vjp(rms_norm, inputs, pre_attn_gain)
    input_part, gain_one = pull_one(normed_grad)
    input_total = input_part + sum(kept[w]["middle_grad"] for w in widths)

    output_grad = out_sum.reshape(o_rows, model).astype(F32)
    qkv_back = tp_columns(qkv_sum.reshape(8, d_rows, q_cols + 2 * k_cols))
    query_grad = by_head_back(qkv_back[:, :, :q_cols]).astype(F32)
    key_grad = by_head_back(qkv_back[:, :, q_cols : q_cols + k_cols]).astype(F32)
    value_grad = by_head_back(qkv_back[:, :, q_cols + k_cols :]).astype(F32)

    def placed(part, count):
        whole = jnp.zeros((8 * count,), F32)
        return lax.dynamic_update_slice_in_dim(whole, part, t_index * count, 0)

    def placed_ff(part):
        whole = jnp.zeros((planes * group_count, 8, ff_rows), F32)
        block = part.reshape(planes * group_count, 1, ff_rows)
        return lax.dynamic_update_slice(whole, block, (0, t_index, 0)).reshape(-1)

    def over_widths(name):
        return sum(kept[w][name][0] for w in widths)

    vectors = [
        placed(qkv_scale_acc[:q_cols], q_cols),
        placed(qkv_scale_acc[q_cols : q_cols + k_cols], k_cols),
        placed(qkv_scale_acc[q_cols + k_cols :], k_cols),
        over_widths("out_scale_sum"),
        placed_ff(over_widths("gate_sum")),
        placed_ff(over_widths("up_sum")),
        over_widths("down_scale_sum"),
        gain_one,
        over_widths("gain_two"),
        over_widths("gain_three"),
        over_widths("gain_four"),
    ]
    summed = jnp.concatenate([v.reshape(devices, -1) for v in vectors], axis=1)[order]
    for bit in reversed(range(devices.bit_length() - 1)):
        keep = 1 << bit
        summed = summed[:keep] + swap_all(summed[keep:], keep)
    summed = summed[0]
    vector_grads = []
    at = 0
    for v in vectors:
        size = v.shape[0] // devices
        vector_grads.append(summed[at : at + size])
        at += size

    return (
        mixed,
        input_total,
        query_grad,
        key_grad,
        value_grad,
        output_grad,
        gate_grad,
        up_grad,
        down_grad,
        *vector_grads,
    )


def solution(mesh):
    rows = P(ALL, None)
    vector = P(ALL)
    in_specs = (
        (rows,) * 8
        + (vector,) * 7
        + (P(),) * 4
        + (P("dp", None), P("dp", None), P(None, ALL, None))
    )
    out_specs = (P(None, ALL, None),) + (rows,) * 8 + (vector,) * 11
    return jax.shard_map(shards, mesh=mesh, in_specs=in_specs, out_specs=out_specs, check_vma=False)
```

time: 2000 us -> 1170 us (0.58)
  waiting for transfers between devices: 976 us -> 296 us
  Pallas kernels: 27.8 us -> 401 us
  matrix products: 320 us -> 61.2 us
  other arithmetic: 280 us -> 58.6 us
  local copies, waits for them, and re-layouts: 216 us -> 128 us
  blocking collectives: 0 us -> 59.4 us
  starting transfers between devices: 159 us -> 134 us
    ppermute x188 -> x160, waiting for transfers between devices: 976 us -> 270 us  [the longest x142 225 us: swap(): return lax.ppermute(values, 'fsdp', [(i, i ^ mask) for i in range(width)])]
    pallas_call x0 -> x29, Pallas kernels: none -> 363 us  [the longest x3 99.1 us: ffn_back(): pl.pallas_call(ffn_back_kernel, grid=(rows // chunk,), in_specs=[wide, bl...]
    dot_general x30 -> x0, matrix products: 241 us -> none  [the longest x15 140 us: dot_nt(): lax.dot_general(left, right, (((1,), (1,)), ((), ())), preferred_element_...]
    concatenate x22 -> x25, other arithmetic: 132 us -> 10.7 us  [the longest x10 5.27 us: plane_sum(): jnp.concatenate([pair[0, 1, :cut], (pair[0, 1, cut:].astype(F32) + got_y....]
    all_to_all x0 -> x3, blocking collectives: none -> 59.4 us  [tp_columns(): lax.all_to_all(blocks, 'fsdp', 0, 0, tiled=True, axis_index_groups=groups)]
    unnamed x56 -> x5, other arithmetic: 39 us -> 0.08 us
    ppermute x188 -> x160, starting transfers between devices: 159 us -> 121 us  [the longest x142 89.2 us: swap(): return lax.ppermute(values, 'fsdp', [(i, i ^ mask) for i in range(width)])]
    dynamic_update_slice x72 -> x16, local copies, waits for them, and re-layouts: 39.9 us -> 7.5 us  [the longest x3 2.85 us: placed(): return lax.dynamic_update_slice_in_dim(whole, part, t_index * count, 0)]
  transfers between devices with their start and end apart: 188 -> 173, of which waited for: 111 -> 71; matrix products, arithmetic and copies ran while one was open for 29% -> 19% of each run, Pallas kernels for 1% -> 28%
where the time goes in v2:
time: 1170 us; the launch traced here: 1160 us
  Pallas kernels  401 us (34%)
  waiting for transfers between devices  296 us (25%)
  starting transfers between devices  134 us (11%)
  local copies, waits for them, and re-layouts  128 us (11%)
  matrix products  61.2 us (5%)
  blocking collectives  59.4 us (5%)
  other arithmetic  58.6 us (5%)
  between operations  23.2 us (2%)
    ppermute x142, waiting for transfers between devices, swap(): return lax.ppermute(values, 'fsdp', [(i, i ^ mask) for i in range(width)])  225 us
    pallas_call x3, Pallas kernels, ffn_back(): pl.pallas_call(ffn_back_kernel, grid=(rows // chunk,), in_specs=[wide, bl...  99.1 us
    ppermute x142, starting transfers between devices, swap(): return lax.ppermute(values, 'fsdp', [(i, i ^ mask) for i in range(width)])  89.2 us
    pallas_call x3, Pallas kernels, ffn_in(): pl.pallas_call(functools.partial(ffn_in_kernel, width, len(pieces)), grid...  65.3 us
    dot_general x4, matrix products, dot_tn(): lax.dot_general(left, right, (((0,), (0,)), ((), ())), preferred_element_...  61.2 us
    all_to_all x3, blocking collectives, tp_columns(): lax.all_to_all(blocks, 'fsdp', 0, 0, tiled=True, axis_index_groups=groups)  59.4 us
    pallas_call x3, Pallas kernels, ffn_out(): pl.pallas_call(functools.partial(ffn_out_kernel, width), grid=(rows // ch...  40.5 us
    pallas_call x1, Pallas kernels, down_gradient(): pl.pallas_call(functools.partial(down_grad_kernel, counts), grid=(feature...  33.2 us
  transfers between devices with their start and end apart: 173, of which 71 were waited for; matrix products, arithmetic and copies ran while one was open for 19% of the time, Pallas kernels for 28%

profile of v2, /device:TPU:0, one launch (start us, length us, event | category | flops | bytes accessed | tf_op | source)
XLA Modules:
  0.0 1160.9 jit_solution(10803751475804353381)
XLA Ops:
  9.5 15.5 %all_to_all.30 = bf16[8,72,512]{2,1,0:T(8,128)(2,1)} all-to-all(bf16[8,72,512]{2,1,0:T(8,128)(2,1)S(1)} %pad_maximum_fusion.3), channel_id=1, replica_groups=mesh['dp'=4,'fsdp'=8] {'fsdp'}, dimensions={0} | all-to-all | bytes 1179648 | tf_op jit(solution)/shard_map/all_to_all | solution.py:982
  29.6 11.5 collective-permute-done.10
  46.6 4.4 collective-permute-done.12
  64.2 6.0 join.1.a_ref
  76.0 22.4 %all_to_all.31 = bf16[8,72,1152]{2,1,0:T(8,128)(2,1)} all-to-all(bf16[8,72,1152]{2,1,0:T(8,128)(2,1)S(1)} %reshape.530), channel_id=1, replica_groups=mesh['dp'=4,'fsdp'=8] {'fsdp'}, dimensions={0} | all-to-all | bytes 2654208 | tf_op jit(solution)/shard_map/all_to_all | solution.py:982
  101.7 17.5 %project.1 = (bf16[3,1024,512]{2,1,0:T(8,128)(2,1)}, bf16[3,1024,256]{2,1,0:T(8,128)(2,1)}, f32[3,1024,256]{2,1,0:T(8,128)}, bf16[3,2304,512]{2,1,0:T(8,128)(2,1)}) custom-call(bf16[1024,2304]{1,0:T(8,128)(2,1)} %join.1.a_ref, bf16[2304,512]{1,0:T(8,128)(2,1)} %all-gather.6.cloned.1.call-done.w_hbm, f32[1,512]{1,0:T(1,128)} %bitcast.437, ...), custom_call_target="tpu_custom_call" | custom-call | flops 7247757312 | bytes 19660800 | tf_op jit(solution)/shard_map/project/pallas_call | solution.py:196
  119.4 5.8 collective-permute-done.14.other_ref
  126.9 6.5 heads.1
  139.2 21.5 %all_to_all.32 = bf16[8,72,1152]{2,1,0:T(8,128)(2,1)} all-to-all(bf16[8,72,1152]{2,1,0:T(8,128)(2,1)S(1)} %reshape.541), channel_id=1, replica_groups=mesh['dp'=4,'fsdp'=8] {'fsdp'}, dimensions={0} | all-to-all | bytes 2654208 | tf_op jit(solution)/shard_map/all_to_all | solution.py:982
  165.0 5.1 collective-permute-start.16
  180.3 15.0 %attend.1.o_ref = bf16[3,1024,256]{2,1,0:T(8,128)(2,1)} custom-call(s32[1024,1]{1,0:T(8,128)} %copy.60.qpos_ref, s32[1,1024]{1,0:T(1,128)} %compare_select_fusion.kpos_ref, bf16[3,1024,256]{2,1,0:T(8,128)(2,1)} %get-tuple-element.167.q_ref, bf16[3,1024,256]{2,1,0:T(8,128)(2,1)} %get-tuple-element.169.k_ref, bf16[3,1024,256]{2,1,0:T(8,128)(2,1)} %get-tuple-element.170.v_ref), custom_call_target="tpu_custom_call" | custom-call | flops 3221225472 | bytes 4718592 | tf_op jit(solution)/shard_map/attend/pallas_call | solution.py:136
  195.3 6.0 output_partial.3
  201.3 6.1 output_partial.4
  207.3 6.1 output_partial.5
  217.8 4.9 collective-permute-done.47
  253.2 7.7 collective-permute-done.51.from_y_ref
  266.9 6.7 collective-permute-done.37.from_y_ref
  279.7 6.6 collective-permute-done.23.from_y_ref
  291.6 7.3 collective-permute-done.53.refs_2_
  301.0 10.5 collective-permute-done.39.refs_2_
  319.0 5.2 collective-permute-done.25.refs_2_
  328.0 6.3 collective-permute-done.54.refs_3_
  346.8 22.1 %ffn_in.5 = (bf16[1024,1152]{1,0:T(8,128)(2,1)}, bf16[1024,1152]{1,0:T(8,128)(2,1)}, bf16[1024,1152]{1,0:T(8,128)(2,1)}, bf16[1024,2304]{1,0:T(8,128)(2,1)}, bf1...) custom-call(bf16[128,2304]{1,0:T(8,128)(2,1)} %get-tuple-element.185.refs_0_, ...), custom_call_target="tpu_custom_call" | custom-call | flops 10871635968 | bytes 22413312 | tf_op jit(solution)/shard_map/ffn_in/pallas_call | solution.py:624
  370.2 21.9 %ffn_in.4 = (bf16[1024,1152]{1,0:T(8,128)(2,1)}, bf16[1024,1152]{1,0:T(8,128)(2,1)}, bf16[1024,1152]{1,0:T(8,128)(2,1)}, bf16[1024,2304]{1,0:T(8,128)(2,1)}, bf1...) custom-call(bf16[128,2304]{1,0:T(8,128)(2,1)} %get-tuple-element.180.refs_0_, ...), custom_call_target="tpu_custom_call" | custom-call | flops 10871635968 | bytes 22413312 | tf_op jit(solution)/shard_map/ffn_in/pallas_call | solution.py:624
  393.2 21.3 %ffn_in.3 = (bf16[1024,1152]{1,0:T(8,128)(2,1)}, bf16[1024,1152]{1,0:T(8,128)(2,1)}, bf16[1024,1152]{1,0:T(8,128)(2,1)}, bf16[1024,2304]{1,0:T(8,128)(2,1)}, bf1...) custom-call(bf16[128,2304]{1,0:T(8,128)(2,1)} %get-tuple-element.173.refs_0_, bf16[128,2304]{1,0:T(8,128)(2,1)} %copy-done.78, ...), custom_call_target="tpu_custom_call" | custom-call | flops 10871635968 | bytes 22413312 | tf_op jit(solution)/shard_map/ffn_in/pallas_call | solution.py:624
  414.5 12.9 %ffn_out.3 = (bf16[512,2304]{1,0:T(8,128)(2,1)}, bf16[512,2304]{1,0:T(8,128)(2,1)}, bf16[1152,2304]{1,0:T(8,128)(2,1)}) custom-call(bf16[1024,1152]{1,0:T(8,128)(2,1)} %get-tuple-element.189.h_ref.refs_30_, bf16[1152,2304]{1,0:T(8,128)(2,1)} %all-gather.14.cloned.1.call-done.d_hbm), custom_call_target="tpu_custom_call" | custom-call | flops 5435817984 | bytes 17694720 | tf_op jit(solution)/shard_map/ffn_out/pallas_call | solution.py:728
  427.5 13.7 %ffn_out.4 = (bf16[512,2304]{1,0:T(8,128)(2,1)}, bf16[512,2304]{1,0:T(8,128)(2,1)}, bf16[1152,2304]{1,0:T(8,128)(2,1)}) custom-call(bf16[1024,1152]{1,0:T(8,128)(2,1)} %get-tuple-element.191.h_ref.refs_31_, bf16[1152,2304]{1,0:T(8,128)(2,1)} %all-gather.14.cloned.1.call-done.d_hbm), custom_call_target="tpu_custom_call" | custom-call | flops 5435817984 | bytes 17694720 | tf_op jit(solution)/shard_map/ffn_out/pallas_call | solution.py:728
  459.4 13.9 %ffn_out.5 = (bf16[512,2304]{1,0:T(8,128)(2,1)}, bf16[512,2304]{1,0:T(8,128)(2,1)}, bf16[1152,2304]{1,0:T(8,128)(2,1)}) custom-call(bf16[1024,1152]{1,0:T(8,128)(2,1)} %get-tuple-element.205.h_ref.refs_32_, bf16[1152,2304]{1,0:T(8,128)(2,1)} %all-gather.14.cloned.1.call-done.d_hbm), custom_call_target="tpu_custom_call" | custom-call | flops 5435817984 | bytes 17694720 | tf_op jit(solution)/shard_map/ffn_out/pallas_call | solution.py:728
  478.0 5.7 collective-permute-done.67
  495.4 21.1 %collective-permute-done.65.from_y_ref = bf16[128,2304]{1,0:T(8,128)(2,1)} collective-permute-done((bf16[128,2304]{1,0:T(8,128)(2,1)S(1)}, bf16[128,2304]{1,0:T(8,128)(2,1)}, u32[]{:S(2)}, u32[]{:S(2)}) %collective-permute-start.65) | collective-permute-done | bytes 589856 | tf_op jit(solution)/shard_map/ppermute | solution.py:928
  533.6 11.1 collective-permute-done.86.refs_12_
  546.9 10.5 collective-permute-done.77.refs_2_
  564.8 5.2 collective-permute-done.75.from_y_ref
  583.6 10.9 collective-permute-done.95.refs_22_
  599.1 6.2 collective-permute-done.96.refs_23_
  610.7 33.2 %down_grad.1 = (bf16[1152,2304]{1,0:T(8,128)(2,1)}, bf16[1024,2304]{1,0:T(8,128)(2,1)}, bf16[1024,2304]{1,0:T(8,128)(2,1)}, bf16[1024,2304]{1,0:T(8,128)(2,1)}) custom-call(bf16[128,2304]{1,0:T(8,128)(2,1)} %get-tuple-element.212.refs_0_, bf16[128,2304]{1,0:T(8,128)(2,1)} %copy-done.76, bf16[128,2304]{1,0:T(8,128)(2,1)} %copy-done.73, ...), custom_call_target="tpu_custom_call" | custom-call | flops 16307453952 | bytes 40697856 | tf_op jit(solution)/shard_map/down_grad/pallas_call | solution.py:687
  651.2 5.0 copy-done.22
  656.2 32.9 %ffn_back.3 = (bf16[512,2304]{1,0:T(8,128)(2,1)}, bf16[512,2304]{1,0:T(8,128)(2,1)}, bf16[1024,1152]{1,0:T(8,128)(2,1)}, bf16[1024,1152]{1,0:T(8,128)(2,1)}, f32[1,1152]{1,0:T(1,128)}, /*index=5*/f32[1,1152]{1,0:T(1,128)}) custom-call(bf16[1024,2304]{1,0:T(8,128)(2,1)} %get-tuple-element.215.dr_ref, bf16[1024,1152]{1,0:T(8,128)(2,1)} %get-tuple-element.216.gate_ref, ...), custom_call_target="tpu_custom_call" | custom-call | flops 16307453952 | bytes 34799616 | tf_op jit(solution)/shard_map/ffn_back/pallas_call | solution.py:822
  689.2 33.0 %ffn_back.4 = (bf16[512,2304]{1,0:T(8,128)(2,1)}, bf16[512,2304]{1,0:T(8,128)(2,1)}, bf16[1024,1152]{1,0:T(8,128)(2,1)}, bf16[1024,1152]{1,0:T(8,128)(2,1)}, f32[1,1152]{1,0:T(1,128)}, /*index=5*/f32[1,1152]{1,0:T(1,128)}) custom-call(bf16[1024,2304]{1,0:T(8,128)(2,1)} %get-tuple-element.226.dr_ref, bf16[1024,1152]{1,0:T(8,128)(2,1)} %get-tuple-element.227.gate_ref, ...), custom_call_target="tpu_custom_call" | custom-call | flops 16307453952 | bytes 34799616 | tf_op jit(solution)/shard_map/ffn_back/pallas_call | solution.py:822
  722.7 33.3 %ffn_back.5 = (bf16[512,2304]{1,0:T(8,128)(2,1)}, bf16[512,2304]{1,0:T(8,128)(2,1)}, bf16[1024,1152]{1,0:T(8,128)(2,1)}, bf16[1024,1152]{1,0:T(8,128)(2,1)}, f32[1,1152]{1,0:T(1,128)}, /*index=5*/f32[1,1152]{1,0:T(1,128)}) custom-call(bf16[1024,2304]{1,0:T(8,128)(2,1)} %get-tuple-element.240.dr_ref, bf16[1024,1152]{1,0:T(8,128)(2,1)} %get-tuple-element.241.gate_ref, ...), custom_call_target="tpu_custom_call" | custom-call | flops 16307453952 | bytes 34799616 | tf_op jit(solution)/shard_map/ffn_back/pallas_call | solution.py:822
  767.3 25.1 %fusion.7 = bf16[2304,1152]{1,0:T(8,128)(2,1)} fusion(bf16[3072,2304]{1,0:T(8,128)(2,1)} %copy-done.22, bf16[1024,1152]{1,0:T(8,128)(2,1)} %get-tuple-element.280, bf16[1024,1152]{1,0:T(8,128)(2,1)} %get-tuple-element.279, bf16[1024,1152]{1,0:T(8,128)(2,1)} %get-tuple-element.278, f32[1152]{0:T(1024)S(1)} %div.96), kind=kOutput, calls=%fused_computation.11 | convolution fusion | flops 16333996032 | bytes 26546688 | tf_op jit(solution)/shard_map/dot_general | solution.py:57
  810.6 8.8 collective-permute-done.107.from_y_ref
  821.2 5.2 output_back.3
  833.0 5.2 output_back.4
  840.1 4.6 collective-permute-done.135.from_y_ref
  845.7 5.1 output_back.5
  850.8 25.0 %fusion.6 = bf16[2304,1152]{1,0:T(8,128)(2,1)} fusion(bf16[3072,2304]{1,0:T(8,128)(2,1)} %copy-done.22, bf16[1024,1152]{1,0:T(8,128)(2,1)} %get-tuple-element.274, bf16[1024,1152]{1,0:T(8,128)(2,1)} %get-tuple-element.273, bf16[1024,1152]{1,0:T(8,128)(2,1)} %get-tuple-element.272, f32[1152]{0:T(1024)S(1)} %div.93), kind=kOutput, calls=%fused_computation.10 | convolution fusion | flops 16333996032 | bytes 26546688 | tf_op jit(solution)/shard_map/dot_general | solution.py:57
  875.7 10.9 reduce-scatter.10.cloned.1.call-done
  891.0 11.1 collective-permute-done.137.refs_2_
  906.6 4.8 collective-permute-done.110.refs_3_
  912.1 5.7 collective-permute-done.124.refs_3_
  918.3 5.0 collective-permute-done.138.refs_3_
  923.9 7.7 collective-permute-done.139.refs_4_
  938.6 7.9 head_back.3
  946.5 7.6 head_back.4
  954.2 7.7 head_back.5
  964.2 22.6 %attend_back.1 = (f32[3,1024,256]{2,1,0:T(8,128)}, f32[3,1024,256]{2,1,0:T(8,128)}, f32[3,1024,256]{2,1,0:T(8,128)}) custom-call(s32[1024,1]{1,0:T(8,128)} %copy.60.qpos_ref, s32[1,1024]{1,0:T(1,128)} %compare_select_fusion.kpos_ref, f32[1024,128]{1,0:T(8,128)} %get-tuple-element.410.cos_ref.qcos_ref.kcos_ref, ...), custom_call_target="tpu_custom_call" | custom-call | flops 8053063680 | bytes 4718592 | tf_op jit(solution)/shard_map/attend_back/pallas_call | solution.py:150
  991.2 7.3 fusion.21
  999.3 4.9 collective-permute-start.152
  1008.1 8.0 collective-permute-done.152
  1030.4 14.4 %project_back.1 = (bf16[512,2304]{1,0:T(8,128)(2,1)}, bf16[512,2304]{1,0:T(8,128)(2,1)}) custom-call(bf16[3,1024,512]{2,1,0:T(8,128)(2,1)} %get-tuple-element.315.round_ref, bf16[3,2304,512]{2,1,0:T(8,128)(2,1)} %get-tuple-element.258.w_hbm), custom_call_target="tpu_custom_call" | custom-call | flops 7247757312 | bytes 14942208 | tf_op jit(solution)/shard_map/project_back/pallas_call | solution.py:869
  1071.6 10.5 all-to-all-done.3
  1101.6 4.4 reshape.582
  1113.7 4.7 reshape.583
  (892 shorter events, 394.9 us)
Async XLA Ops:
  7.2 94.5 %all-gather.6.cloned.1.call-start = ((), (), s32[]{:S(2)}) async-start(), calls=%async_computation.11 | async-start | bytes 2949120 | tf_op jit(solution)/shard_map/all_gather | solution.py:987
  25.0 135.8 %all-gather.8.cloned.1.call-start = ((), (), s32[]{:S(2)}) async-start(), calls=%async_computation.12 | async-start | bytes 1474560 | tf_op jit(solution)/shard_map/all_gather | solution.py:987
  25.5 27.3 %collective-permute-start.1 = (bf16[128,2304]{1,0:T(8,128)(2,1)S(1)}, bf16[128,2304]{1,0:T(8,128)(2,1)S(1)}, u32[]{:S(2)}, u32[]{:S(2)}) collective-permute-start(bf16[128,2304]{1,0:T(8,128)(2,1)S(1)} %fusion.26.refs_0_), channel_id=1, source_target_pairs={{0,4},{1,5},{2,6},{3,7},{4,0},{5,1},{6,2},{7,3},{8,12},{9,13},{10,... | collective-permute-start | bytes 1769480 | tf_op jit(solution)/shard_map/ppermute | solution.py:928
  26.2 27.5 %collective-permute-start = (bf16[128,2304]{1,0:T(8,128)(2,1)S(1)}, bf16[128,2304]{1,0:T(8,128)(2,1)S(1)}, u32[]{:S(2)}, u32[]{:S(2)}) collective-permute-start(bf16[128,2304]{1,0:T(8,128)(2,1)S(1)} %fusion.26.refs_0_), channel_id=1, source_target_pairs={{0,2},{1,3},{2,0},{3,1},{4,6},{5,7},{6,4},{7,5},{8,10},{9,11},{10,... | collective-permute-start | bytes 1769480 | tf_op jit(solution)/shard_map/ppermute | solution.py:928
  55.9 291.0 %all-gather.10.cloned.1.call-start = ((), (), s32[]{:S(2)}) async-start(), calls=%async_computation.13 | async-start | bytes 6635520 | tf_op jit(solution)/shard_map/all_gather | solution.py:987
  98.4 248.4 %all-gather.12.cloned.1.call-start = ((), (), s32[]{:S(2)}) async-start(), calls=%async_computation.14 | async-start | bytes 6635520 | tf_op jit(solution)/shard_map/all_gather | solution.py:987
  160.7 253.8 %all-gather.14.cloned.1.call-start = ((), (), s32[]{:S(2)}) async-start(), calls=%async_computation.15 | async-start | bytes 6635520 | tf_op jit(solution)/shard_map/all_gather | solution.py:987
  215.2 552.1 %reduce-scatter.8.cloned.1.call-start = ((), (), s32[]{:S(2)}) async-start(), calls=%async_computation.17 | async-start | bytes 6635520 | tf_op jit(solution)/shard_map/reduce_scatter | solution.py:990
  237.0 23.9 %collective-permute-start.51 = (bf16[128,2304]{1,0:T(8,128)(2,1)S(1)}, bf16[128,2304]{1,0:T(8,128)(2,1)S(1)}, u32[]{:S(2)}, u32[]{:S(2)}) collective-permute-start(bf16[128,2304]{1,0:T(8,128)(2,1)S(1)} %pad_maximum_fusion.9), channel_id=1, source_target_pairs={{0,4},{1,5},{2,6},{3,7},{4,0},{5,1},{6,2},{7,3},{8,12},{9,13},{10,... | collective-permute-start | bytes 1769480 | tf_op jit(solution)/shard_map/ppermute | solution.py:928
  244.1 29.5 %collective-permute-start.37 = (bf16[128,2304]{1,0:T(8,128)(2,1)}, bf16[128,2304]{1,0:T(8,128)(2,1)}, u32[]{:S(2)}, u32[]{:S(2)}) collective-permute-start(bf16[128,2304]{1,0:T(8,128)(2,1)} %pad_maximum_fusion.7), channel_id=1, source_target_pairs={{0,4},{1,5},{2,6},{3,7},{4,0},{5,1},{6,2},{7,3},{8,12},{9,13},{10,... | collective-permute-start | bytes 1769480 | tf_op jit(solution)/shard_map/ppermute | solution.py:928
  248.3 26.6 %collective-permute-start.35 = (bf16[128,2304]{1,0:T(8,128)(2,1)}, bf16[128,2304]{1,0:T(8,128)(2,1)}, u32[]{:S(2)}, u32[]{:S(2)}) collective-permute-start(bf16[128,2304]{1,0:T(8,128)(2,1)} %pad_maximum_fusion.6), channel_id=1, source_target_pairs={{0,2},{1,3},{2,0},{3,1},{4,6},{5,7},{6,4},{7,5},{8,10},{9,11},{10,... | collective-permute-start | bytes 1769480 | tf_op jit(solution)/shard_map/ppermute | solution.py:928
  250.5 35.8 %collective-permute-start.23 = (bf16[128,2304]{1,0:T(8,128)(2,1)}, bf16[128,2304]{1,0:T(8,128)(2,1)}, u32[]{:S(2)}, u32[]{:S(2)}) collective-permute-start(bf16[128,2304]{1,0:T(8,128)(2,1)} %pad_maximum_fusion.5), channel_id=1, source_target_pairs={{0,4},{1,5},{2,6},{3,7},{4,0},{5,1},{6,2},{7,3},{8,12},{9,13},{10,... | collective-permute-start | bytes 1769480 | tf_op jit(solution)/shard_map/ppermute | solution.py:928
  260.9 26.9 %collective-permute-start.21 = (bf16[128,2304]{1,0:T(8,128)(2,1)}, bf16[128,2304]{1,0:T(8,128)(2,1)}, u32[]{:S(2)}, u32[]{:S(2)}) collective-permute-start(bf16[128,2304]{1,0:T(8,128)(2,1)} %pad_maximum_fusion.4), channel_id=1, source_target_pairs={{0,2},{1,3},{2,0},{3,1},{4,6},{5,7},{6,4},{7,5},{8,10},{9,11},{10,... | collective-permute-start | bytes 1769480 | tf_op jit(solution)/shard_map/ppermute | solution.py:928
  266.0 32.9 %collective-permute-start.53 = (bf16[128,2304]{1,0:T(8,128)(2,1)}, bf16[128,2304]{1,0:T(8,128)(2,1)}, u32[]{:S(2)}, u32[]{:S(2)}) collective-permute-start(bf16[128,2304]{1,0:T(8,128)(2,1)} %get-tuple-element.185.refs_0_), channel_id=1, source_target_pairs={{0,4},{1,5},{2,6},{3,7},{4,0},{5,1},{6,2},{7,3},{8,12},{9,13},{10,... | collective-permute-start | bytes 1769480 | tf_op jit(solution)/shard_map/ppermute | solution.py:928
  273.7 26.5 %collective-permute-start.52 = (bf16[128,2304]{1,0:T(8,128)(2,1)}, bf16[128,2304]{1,0:T(8,128)(2,1)}, u32[]{:S(2)}, u32[]{:S(2)}) collective-permute-start(bf16[128,2304]{1,0:T(8,128)(2,1)} %get-tuple-element.185.refs_0_), channel_id=1, source_target_pairs={{0,2},{1,3},{2,0},{3,1},{4,6},{5,7},{6,4},{7,5},{8,10},{9,11},{10,... | collective-permute-start | bytes 1769480 | tf_op jit(solution)/shard_map/ppermute | solution.py:928
  278.7 32.8 %collective-permute-start.39 = (bf16[128,2304]{1,0:T(8,128)(2,1)}, bf16[128,2304]{1,0:T(8,128)(2,1)S(1)}, u32[]{:S(2)}, u32[]{:S(2)}) collective-permute-start(bf16[128,2304]{1,0:T(8,128)(2,1)} %get-tuple-element.180.refs_0_), channel_id=1, source_target_pairs={{0,4},{1,5},{2,6},{3,7},{4,0},{5,1},{6,2},{7,3},{8,12},{9,13},{10,... | collective-permute-start | bytes 1769480 | tf_op jit(solution)/shard_map/ppermute | solution.py:928
  286.3 26.8 %collective-permute-start.38 = (bf16[128,2304]{1,0:T(8,128)(2,1)}, bf16[128,2304]{1,0:T(8,128)(2,1)}, u32[]{:S(2)}, u32[]{:S(2)}) collective-permute-start(bf16[128,2304]{1,0:T(8,128)(2,1)} %get-tuple-element.180.refs_0_), channel_id=1, source_target_pairs={{0,2},{1,3},{2,0},{3,1},{4,6},{5,7},{6,4},{7,5},{8,10},{9,11},{10,... | collective-permute-start | bytes 1769480 | tf_op jit(solution)/shard_map/ppermute | solution.py:928
  287.8 28.8 %collective-permute-start.56 = (bf16[128,2304]{1,0:T(8,128)(2,1)}, bf16[128,2304]{1,0:T(8,128)(2,1)}, u32[]{:S(2)}, u32[]{:S(2)}) collective-permute-start(bf16[128,2304]{1,0:T(8,128)(2,1)} %get-tuple-element.185.refs_0_), channel_id=1, source_target_pairs={{0,1},{1,0},{2,3},{3,2},{4,5},{5,4},{6,7},{7,6},{8,9},{9,8},{10,11... | collective-permute-start | bytes 1769480 | tf_op jit(solution)/shard_map/ppermute | solution.py:928
  300.1 24.0 %collective-permute-start.25 = (bf16[128,2304]{1,0:T(8,128)(2,1)}, bf16[128,2304]{1,0:T(8,128)(2,1)S(1)}, u32[]{:S(2)}, u32[]{:S(2)}) collective-permute-start(bf16[128,2304]{1,0:T(8,128)(2,1)} %get-tuple-element.173.refs_0_), channel_id=1, source_target_pairs={{0,4},{1,5},{2,6},{3,7},{4,0},{5,1},{6,2},{7,3},{8,12},{9,13},{10,... | collective-permute-start | bytes 1769480 | tf_op jit(solution)/shard_map/ppermute | solution.py:928
  345.3 23.7 %collective-permute-start.27 = (bf16[64,2304]{1,0:T(8,128)(2,1)S(1)}, bf16[64,2304]{1,0:T(8,128)(2,1)S(1)}, u32[]{:S(2)}, u32[]{:S(2)}) collective-permute-start(bf16[64,2304]{1,0:T(8,128)(2,1)S(1)} %slice.581), channel_id=1, source_target_pairs={{0,4},{1,5},{2,6},{3,7},{4,0},{5,1},{6,2},{7,3},{8,12},{9,13},{10,... | collective-permute-start | bytes 884744 | tf_op jit(solution)/shard_map/ppermute | solution.py:928
  345.8 23.9 %collective-permute-start.43 = (bf16[128,2304]{1,0:T(8,128)(2,1)}, bf16[128,2304]{1,0:T(8,128)(2,1)}, u32[]{:S(2)}, u32[]{:S(2)}) collective-permute-start(bf16[128,2304]{1,0:T(8,128)(2,1)} %collective-permute-done.38.refs_1_), channel_id=1, source_target_pairs={{0,1},{1,0},{2,3},{3,2},{4,5},{5,4},{6,7},{7,6},{8,9},{9,8},{10,11... | collective-permute-start | bytes 1769480 | tf_op jit(solution)/shard_map/ppermute | solution.py:928
  345.8 24.3 %collective-permute-start.44 = (bf16[128,2304]{1,0:T(8,128)(2,1)S(1)}, bf16[128,2304]{1,0:T(8,128)(2,1)}, u32[]{:S(2)}, u32[]{:S(2)}) collective-permute-start(bf16[128,2304]{1,0:T(8,128)(2,1)S(1)} %collective-permute-done.39.refs_2_), channel_id=1, source_target_pairs={{0,1},{1,0},{2,3},{3,2},{4,5},{5,4},{6,7},{7,6},{8,9},{9,8},{10,11... | collective-permute-start | bytes 1769480 | tf_op jit(solution)/shard_map/ppermute | solution.py:928
  346.3 22.9 %collective-permute-start.45 = (bf16[64,2304]{1,0:T(8,128)(2,1)S(1)}, bf16[64,2304]{1,0:T(8,128)(2,1)}, u32[]{:S(2)}, u32[]{:S(2)}) collective-permute-start(bf16[64,2304]{1,0:T(8,128)(2,1)S(1)} %collective-permute-done.40.refs_3_), channel_id=1, source_target_pairs={{0,1},{1,0},{2,3},{3,2},{4,5},{5,4},{6,7},{7,6},{8,9},{9,8},{10,11... | collective-permute-start | bytes 884744 | tf_op jit(solution)/shard_map/ppermute | solution.py:928
  346.4 23.2 %collective-permute-start.46 = (bf16[64,2304]{1,0:T(8,128)(2,1)}, bf16[64,2304]{1,0:T(8,128)(2,1)}, u32[]{:S(2)}, u32[]{:S(2)}) collective-permute-start(bf16[64,2304]{1,0:T(8,128)(2,1)} %collective-permute-done.41.refs_4_), channel_id=1, source_target_pairs={{0,1},{1,0},{2,3},{3,2},{4,5},{5,4},{6,7},{7,6},{8,9},{9,8},{10,11... | collective-permute-start | bytes 884744 | tf_op jit(solution)/shard_map/ppermute | solution.py:928
  369.0 23.1 %collective-permute-start.28 = (bf16[128,2304]{1,0:T(8,128)(2,1)S(1)}, bf16[128,2304]{1,0:T(8,128)(2,1)S(1)}, u32[]{:S(2)}, u32[]{:S(2)}) collective-permute-start(bf16[128,2304]{1,0:T(8,128)(2,1)S(1)} %copy-done.139), channel_id=1, source_target_pairs={{0,1},{1,0},{2,3},{3,2},{4,5},{5,4},{6,7},{7,6},{8,9},{9,8},{10,11... | collective-permute-start | bytes 1769480 | tf_op jit(solution)/shard_map/ppermute | solution.py:928
  369.2 23.0 %collective-permute-start.29 = (bf16[128,2304]{1,0:T(8,128)(2,1)S(1)}, bf16[128,2304]{1,0:T(8,128)(2,1)}, u32[]{:S(2)}, u32[]{:S(2)}) collective-permute-start(bf16[128,2304]{1,0:T(8,128)(2,1)S(1)} %collective-permute-done.24.refs_1_), channel_id=1, source_target_pairs={{0,1},{1,0},{2,3},{3,2},{4,5},{5,4},{6,7},{7,6},{8,9},{9,8},{10,11... | collective-permute-start | bytes 1769480 | tf_op jit(solution)/shard_map/ppermute | solution.py:928
  369.6 22.6 %collective-permute-start.30 = (bf16[128,2304]{1,0:T(8,128)(2,1)S(1)}, bf16[128,2304]{1,0:T(8,128)(2,1)}, u32[]{:S(2)}, u32[]{:S(2)}) collective-permute-start(bf16[128,2304]{1,0:T(8,128)(2,1)S(1)} %collective-permute-done.25.refs_2_), channel_id=1, source_target_pairs={{0,1},{1,0},{2,3},{3,2},{4,5},{5,4},{6,7},{7,6},{8,9},{9,8},{10,11... | collective-permute-start | bytes 1769480 | tf_op jit(solution)/shard_map/ppermute | solution.py:928
  369.7 22.5 %collective-permute-start.31 = (bf16[64,2304]{1,0:T(8,128)(2,1)}, bf16[64,2304]{1,0:T(8,128)(2,1)S(1)}, u32[]{:S(2)}, u32[]{:S(2)}) collective-permute-start(bf16[64,2304]{1,0:T(8,128)(2,1)} %collective-permute-done.26.refs_3_), channel_id=1, source_target_pairs={{0,1},{1,0},{2,3},{3,2},{4,5},{5,4},{6,7},{7,6},{8,9},{9,8},{10,11... | collective-permute-start | bytes 884744 | tf_op jit(solution)/shard_map/ppermute | solution.py:928
  370.1 22.1 %collective-permute-start.32 = (bf16[64,2304]{1,0:T(8,128)(2,1)S(1)}, bf16[64,2304]{1,0:T(8,128)(2,1)S(1)}, u32[]{:S(2)}, u32[]{:S(2)}) collective-permute-start(bf16[64,2304]{1,0:T(8,128)(2,1)S(1)} %collective-permute-done.27.refs_4_), channel_id=1, source_target_pairs={{0,1},{1,0},{2,3},{3,2},{4,5},{5,4},{6,7},{7,6},{8,9},{9,8},{10,11... | collective-permute-start | bytes 884744 | tf_op jit(solution)/shard_map/ppermute | solution.py:928
  487.3 35.8 %collective-permute-start.70 = (bf16[128,2304]{1,0:T(8,128)(2,1)}, bf16[128,2304]{1,0:T(8,128)(2,1)S(1)}, u32[]{:S(2)}, u32[]{:S(2)}) collective-permute-start(bf16[128,2304]{1,0:T(8,128)(2,1)} %pad_maximum_fusion.13), channel_id=1, source_target_pairs={{0,4},{1,5},{2,6},{3,7},{4,0},{5,1},{6,2},{7,3},{8,12},{9,13},{10,... | collective-permute-start | bytes 1769480 | tf_op jit(solution)/shard_map/ppermute | solution.py:928
  488.7 34.4 %collective-permute-start.68 = (bf16[128,2304]{1,0:T(8,128)(2,1)}, bf16[128,2304]{1,0:T(8,128)(2,1)S(1)}, u32[]{:S(2)}, u32[]{:S(2)}) collective-permute-start(bf16[128,2304]{1,0:T(8,128)(2,1)} %pad_maximum_fusion.12), channel_id=1, source_target_pairs={{0,2},{1,3},{2,0},{3,1},{4,6},{5,7},{6,4},{7,5},{8,10},{9,11},{10,... | collective-permute-start | bytes 1769480 | tf_op jit(solution)/shard_map/ppermute | solution.py:928
  491.7 24.8 %collective-permute-start.65 = (bf16[128,2304]{1,0:T(8,128)(2,1)S(1)}, bf16[128,2304]{1,0:T(8,128)(2,1)}, u32[]{:S(2)}, u32[]{:S(2)}) collective-permute-start(bf16[128,2304]{1,0:T(8,128)(2,1)S(1)} %pad_maximum_fusion.11), channel_id=1, source_target_pairs={{0,4},{1,5},{2,6},{3,7},{4,0},{5,1},{6,2},{7,3},{8,12},{9,13},{10,... | collective-permute-start | bytes 1769480 | tf_op jit(solution)/shard_map/ppermute | solution.py:928
  491.8 27.1 %collective-permute-start.63 = (bf16[128,2304]{1,0:T(8,128)(2,1)S(1)}, bf16[128,2304]{1,0:T(8,128)(2,1)}, u32[]{:S(2)}, u32[]{:S(2)}) collective-permute-start(bf16[128,2304]{1,0:T(8,128)(2,1)S(1)} %pad_maximum_fusion.10), channel_id=1, source_target_pairs={{0,2},{1,3},{2,0},{3,1},{4,6},{5,7},{6,4},{7,5},{8,10},{9,11},{10,... | collective-permute-start | bytes 1769480 | tf_op jit(solution)/shard_map/ppermute | solution.py:928
  494.7 35.7 %collective-permute-start.72 = (bf16[64,2304]{1,0:T(8,128)(2,1)}, bf16[64,2304]{1,0:T(8,128)(2,1)}, u32[]{:S(2)}, u32[]{:S(2)}) collective-permute-start(bf16[64,2304]{1,0:T(8,128)(2,1)} %get-tuple-element.350), channel_id=1, source_target_pairs={{0,4},{1,5},{2,6},{3,7},{4,0},{5,1},{6,2},{7,3},{8,12},{9,13},{10,... | collective-permute-start | bytes 884744 | tf_op jit(solution)/shard_map/ppermute | solution.py:928
  530.3 32.3 %collective-permute-start.89 = (bf16[128,2304]{1,0:T(8,128)(2,1)}, bf16[128,2304]{1,0:T(8,128)(2,1)S(1)}, u32[]{:S(2)}, u32[]{:S(2)}) collective-permute-start(bf16[128,2304]{1,0:T(8,128)(2,1)} %get-tuple-element.213.refs_10_), channel_id=1, source_target_pairs={{0,1},{1,0},{2,3},{3,2},{4,5},{5,4},{6,7},{7,6},{8,9},{9,8},{10,11... | collective-permute-start | bytes 1769480 | tf_op jit(solution)/shard_map/ppermute | solution.py:928
  530.3 27.0 %collective-permute-start.77 = (bf16[128,2304]{1,0:T(8,128)(2,1)}, bf16[128,2304]{1,0:T(8,128)(2,1)S(1)}, u32[]{:S(2)}, u32[]{:S(2)}) collective-permute-start(bf16[128,2304]{1,0:T(8,128)(2,1)} %get-tuple-element.212.refs_0_), channel_id=1, source_target_pairs={{0,4},{1,5},{2,6},{3,7},{4,0},{5,1},{6,2},{7,3},{8,12},{9,13},{10,... | collective-permute-start | bytes 1769480 | tf_op jit(solution)/shard_map/ppermute | solution.py:928
  531.8 30.2 %collective-permute-start.76 = (bf16[128,2304]{1,0:T(8,128)(2,1)}, bf16[128,2304]{1,0:T(8,128)(2,1)S(1)}, u32[]{:S(2)}, u32[]{:S(2)}) collective-permute-start(bf16[128,2304]{1,0:T(8,128)(2,1)} %get-tuple-element.212.refs_0_), channel_id=1, source_target_pairs={{0,2},{1,3},{2,0},{3,1},{4,6},{5,7},{6,4},{7,5},{8,10},{9,11},{10,... | collective-permute-start | bytes 1769480 | tf_op jit(solution)/shard_map/ppermute | solution.py:928
  546.0 24.0 %collective-permute-start.75 = (bf16[128,2304]{1,0:T(8,128)(2,1)S(1)}, bf16[128,2304]{1,0:T(8,128)(2,1)S(1)}, u32[]{:S(2)}, u32[]{:S(2)}) collective-permute-start(bf16[128,2304]{1,0:T(8,128)(2,1)S(1)} %pad_maximum_fusion.15), channel_id=1, source_target_pairs={{0,4},{1,5},{2,6},{3,7},{4,0},{5,1},{6,2},{7,3},{8,12},{9,13},{10,... | collective-permute-start | bytes 1769480 | tf_op jit(solution)/shard_map/ppermute | solution.py:928
  643.9 242.7 %reduce-scatter.10.cloned.1.call-start = ((), (), s32[]{:S(2)}) async-start(), calls=%async_computation.18 | async-start | bytes 6635520 | tf_op jit(solution)/shard_map/reduce_scatter | solution.py:990
  689.1 67.0 %collective-permute-start.103 = (bf16[512,2304]{1,0:T(8,128)(2,1)}, bf16[512,2304]{1,0:T(8,128)(2,1)}, u32[]{:S(2)}, u32[]{:S(2)}) collective-permute-start(bf16[512,2304]{1,0:T(8,128)(2,1)} %get-tuple-element.222), channel_id=1, source_target_pairs={{0,1},{1,0},{2,3},{3,2},{4,5},{5,4},{6,7},{7,6},{8,9},{9,8},{10,11... | collective-permute-start | bytes 7077896 | tf_op jit(solution)/shard_map/ppermute | solution.py:928
  722.2 38.7 %collective-permute-start.117 = (bf16[512,2304]{1,0:T(8,128)(2,1)}, bf16[512,2304]{1,0:T(8,128)(2,1)}, u32[]{:S(2)}, u32[]{:S(2)}) collective-permute-start(bf16[512,2304]{1,0:T(8,128)(2,1)} %get-tuple-element.233), channel_id=1, source_target_pairs={{0,1},{1,0},{2,3},{3,2},{4,5},{5,4},{6,7},{7,6},{8,9},{9,8},{10,11... | collective-permute-start | bytes 7077896 | tf_op jit(solution)/shard_map/ppermute | solution.py:928
  756.0 37.7 %collective-permute-start.131 = (bf16[512,2304]{1,0:T(8,128)(2,1)}, bf16[512,2304]{1,0:T(8,128)(2,1)}, u32[]{:S(2)}, u32[]{:S(2)}) collective-permute-start(bf16[512,2304]{1,0:T(8,128)(2,1)} %get-tuple-element.248), channel_id=1, source_target_pairs={{0,1},{1,0},{2,3},{3,2},{4,5},{5,4},{6,7},{7,6},{8,9},{9,8},{10,11... | collective-permute-start | bytes 7077896 | tf_op jit(solution)/shard_map/ppermute | solution.py:928
  759.3 37.7 %collective-permute-start.104 = (bf16[64,2304]{1,0:T(8,128)(2,1)}, bf16[64,2304]{1,0:T(8,128)(2,1)}, u32[]{:S(2)}, u32[]{:S(2)}) collective-permute-start(bf16[64,2304]{1,0:T(8,128)(2,1)} %get-tuple-element.332), channel_id=1, source_target_pairs={{0,4},{1,5},{2,6},{3,7},{4,0},{5,1},{6,2},{7,3},{8,12},{9,13},{10,... | collective-permute-start | bytes 884744 | tf_op jit(solution)/shard_map/ppermute | solution.py:928
  759.4 39.2 %collective-permute-start.106 = (bf16[64,2304]{1,0:T(8,128)(2,1)}, bf16[64,2304]{1,0:T(8,128)(2,1)}, u32[]{:S(2)}, u32[]{:S(2)}) collective-permute-start(bf16[64,2304]{1,0:T(8,128)(2,1)} %get-tuple-element.330), channel_id=1, source_target_pairs={{0,2},{1,3},{2,0},{3,1},{4,6},{5,7},{6,4},{7,5},{8,10},{9,11},{10,... | collective-permute-start | bytes 884744 | tf_op jit(solution)/shard_map/ppermute | solution.py:928
  764.2 36.7 %collective-permute-start.118 = (bf16[64,2304]{1,0:T(8,128)(2,1)}, bf16[64,2304]{1,0:T(8,128)(2,1)}, u32[]{:S(2)}, u32[]{:S(2)}) collective-permute-start(bf16[64,2304]{1,0:T(8,128)(2,1)} %get-tuple-element.338), channel_id=1, source_target_pairs={{0,4},{1,5},{2,6},{3,7},{4,0},{5,1},{6,2},{7,3},{8,12},{9,13},{10,... | collective-permute-start | bytes 884744 | tf_op jit(solution)/shard_map/ppermute | solution.py:928
  764.6 38.2 %collective-permute-start.120 = (bf16[64,2304]{1,0:T(8,128)(2,1)}, bf16[64,2304]{1,0:T(8,128)(2,1)}, u32[]{:S(2)}, u32[]{:S(2)}) collective-permute-start(bf16[64,2304]{1,0:T(8,128)(2,1)} %get-tuple-element.336), channel_id=1, source_target_pairs={{0,2},{1,3},{2,0},{3,1},{4,6},{5,7},{6,4},{7,5},{8,10},{9,11},{10,... | collective-permute-start | bytes 884744 | tf_op jit(solution)/shard_map/ppermute | solution.py:928
  792.4 289.7 %reduce-scatter.12.cloned.1.call-start = ((), (), s32[]{:S(2)}) async-start(), calls=%async_computation.19 | async-start | bytes 6635520 | tf_op jit(solution)/shard_map/reduce_scatter | solution.py:990
  804.0 28.0 %collective-permute-start.121 = (bf16[128,2304]{1,0:T(8,128)(2,1)S(1)}, bf16[128,2304]{1,0:T(8,128)(2,1)S(1)}, u32[]{:S(2)}, u32[]{:S(2)}) collective-permute-start(bf16[128,2304]{1,0:T(8,128)(2,1)S(1)} %pad_maximum_fusion.19), channel_id=1, source_target_pairs={{0,4},{1,5},{2,6},{3,7},{4,0},{5,1},{6,2},{7,3},{8,12},{9,13},{10,... | collective-permute-start | bytes 1769480 | tf_op jit(solution)/shard_map/ppermute | solution.py:928
  806.8 25.5 %collective-permute-start.119 = (bf16[128,2304]{1,0:T(8,128)(2,1)}, bf16[128,2304]{1,0:T(8,128)(2,1)S(1)}, u32[]{:S(2)}, u32[]{:S(2)}) collective-permute-start(bf16[128,2304]{1,0:T(8,128)(2,1)} %pad_maximum_fusion.18), channel_id=1, source_target_pairs={{0,2},{1,3},{2,0},{3,1},{4,6},{5,7},{6,4},{7,5},{8,10},{9,11},{10,... | collective-permute-start | bytes 1769480 | tf_op jit(solution)/shard_map/ppermute | solution.py:928
  807.9 36.8 %collective-permute-start.135 = (bf16[128,2304]{1,0:T(8,128)(2,1)}, bf16[128,2304]{1,0:T(8,128)(2,1)S(1)}, u32[]{:S(2)}, u32[]{:S(2)}) collective-permute-start(bf16[128,2304]{1,0:T(8,128)(2,1)} %pad_maximum_fusion.21), channel_id=1, source_target_pairs={{0,4},{1,5},{2,6},{3,7},{4,0},{5,1},{6,2},{7,3},{8,12},{9,13},{10,... | collective-permute-start | bytes 1769480 | tf_op jit(solution)/shard_map/ppermute | solution.py:928
  819.4 25.4 %collective-permute-start.133 = (bf16[128,2304]{1,0:T(8,128)(2,1)}, bf16[128,2304]{1,0:T(8,128)(2,1)S(1)}, u32[]{:S(2)}, u32[]{:S(2)}) collective-permute-start(bf16[128,2304]{1,0:T(8,128)(2,1)} %pad_maximum_fusion.20), channel_id=1, source_target_pairs={{0,2},{1,3},{2,0},{3,1},{4,6},{5,7},{6,4},{7,5},{8,10},{9,11},{10,... | collective-permute-start | bytes 1769480 | tf_op jit(solution)/shard_map/ppermute | solution.py:928
  826.5 61.8 %collective-permute-start.109 = (bf16[128,2304]{1,0:T(8,128)(2,1)}, bf16[128,2304]{1,0:T(8,128)(2,1)S(1)}, u32[]{:S(2)}, u32[]{:S(2)}) collective-permute-start(bf16[128,2304]{1,0:T(8,128)(2,1)} %get-tuple-element.224.refs_0_), channel_id=1, source_target_pairs={{0,4},{1,5},{2,6},{3,7},{4,0},{5,1},{6,2},{7,3},{8,12},{9,13},{10,... | collective-permute-start | bytes 1769480 | tf_op jit(solution)/shard_map/ppermute | solution.py:928
  832.0 56.2 %collective-permute-start.108 = (bf16[128,2304]{1,0:T(8,128)(2,1)}, bf16[128,2304]{1,0:T(8,128)(2,1)S(1)}, u32[]{:S(2)}, u32[]{:S(2)}) collective-permute-start(bf16[128,2304]{1,0:T(8,128)(2,1)} %get-tuple-element.224.refs_0_), channel_id=1, source_target_pairs={{0,2},{1,3},{2,0},{3,1},{4,6},{5,7},{6,4},{7,5},{8,10},{9,11},{10,... | collective-permute-start | bytes 1769480 | tf_op jit(solution)/shard_map/ppermute | solution.py:928
  838.2 50.5 %collective-permute-start.123 = (bf16[128,2304]{1,0:T(8,128)(2,1)}, bf16[128,2304]{1,0:T(8,128)(2,1)S(1)}, u32[]{:S(2)}, u32[]{:S(2)}) collective-permute-start(bf16[128,2304]{1,0:T(8,128)(2,1)} %get-tuple-element.237.refs_0_), channel_id=1, source_target_pairs={{0,4},{1,5},{2,6},{3,7},{4,0},{5,1},{6,2},{7,3},{8,12},{9,13},{10,... | collective-permute-start | bytes 1769480 | tf_op jit(solution)/shard_map/ppermute | solution.py:928
  844.7 45.6 %collective-permute-start.122 = (bf16[128,2304]{1,0:T(8,128)(2,1)}, bf16[128,2304]{1,0:T(8,128)(2,1)S(1)}, u32[]{:S(2)}, u32[]{:S(2)}) collective-permute-start(bf16[128,2304]{1,0:T(8,128)(2,1)} %get-tuple-element.237.refs_0_), channel_id=1, source_target_pairs={{0,2},{1,3},{2,0},{3,1},{4,6},{5,7},{6,4},{7,5},{8,10},{9,11},{10,... | collective-permute-start | bytes 1769480 | tf_op jit(solution)/shard_map/ppermute | solution.py:928
  886.7 231.8 %reduce-scatter.6.cloned.1.call-start = ((), (), s32[]{:S(2)}) async-start(), calls=%async_computation.16 | async-start | bytes 2949120 | tf_op jit(solution)/shard_map/reduce_scatter | solution.py:990
  932.2 22.0 %collective-permute-start.140 = (bf16[128,2304]{1,0:T(8,128)(2,1)}, bf16[128,2304]{1,0:T(8,128)(2,1)}, u32[]{:S(2)}, u32[]{:S(2)}) collective-permute-start(bf16[128,2304]{1,0:T(8,128)(2,1)} %get-tuple-element.252.refs_0_), channel_id=1, source_target_pairs={{0,1},{1,0},{2,3},{3,2},{4,5},{5,4},{6,7},{7,6},{8,9},{9,8},{10,11... | collective-permute-start | bytes 1769480 | tf_op jit(solution)/shard_map/ppermute | solution.py:928
  932.2 21.9 %collective-permute-start.141 = (bf16[128,2304]{1,0:T(8,128)(2,1)S(1)}, bf16[128,2304]{1,0:T(8,128)(2,1)}, u32[]{:S(2)}, u32[]{:S(2)}) collective-permute-start(bf16[128,2304]{1,0:T(8,128)(2,1)S(1)} %collective-permute-done.136.refs_1_), channel_id=1, source_target_pairs={{0,1},{1,0},{2,3},{3,2},{4,5},{5,4},{6,7},{7,6},{8,9},{9,8},{10,11... | collective-permute-start | bytes 1769480 | tf_op jit(solution)/shard_map/ppermute | solution.py:928
  990.1 30.6 %collective-permute-start.145 = (f32[3,1024,256]{2,1,0:T(8,128)S(1)}, f32[3,1024,256]{2,1,0:T(8,128)S(1)}, u32[]{:S(2)}, u32[]{:S(2)}) collective-permute-start(f32[3,1024,256]{2,1,0:T(8,128)S(1)} %pad_maximum_fusion.1), channel_id=1, source_target_pairs={{0,1},{1,0},{2,3},{3,2},{4,5},{5,4},{6,7},{7,6},{8,9},{9,8},{10,11... | collective-permute-start | bytes 9437192 | tf_op jit(solution)/shard_map/ppermute | solution.py:928
  1058.0 24.1 %all-to-all-start.3 = ((bf16[8,72,1152]{2,1,0:T(8,128)(2,1)}), bf16[8,72,1152]{2,1,0:T(8,128)(2,1)}, u32[]{:S(2)}, u32[]{:S(2)}) async-start(bf16[8,72,1152]{2,1,0:T(8,128)(2,1)} %bitcast.421), calls=%async_computation.6 | async-start | bytes 2654208 | tf_op jit(solution)/shard_map/all_to_all | solution.py:982
  1062.3 72.2 %reduce-scatter.14.cloned.1.call-start = ((), (), s32[]{:S(2)}) async-start(), calls=%async_computation.20 | async-start | bytes 1474560 | tf_op jit(solution)/shard_map/reduce_scatter | solution.py:990
  1082.1 24.0 %all-to-all-start.4 = ((bf16[8,72,1152]{2,1,0:T(8,128)(2,1)}), bf16[8,72,1152]{2,1,0:T(8,128)(2,1)}, u32[]{:S(2)}, u32[]{:S(2)}) async-start(bf16[8,72,1152]{2,1,0:T(8,128)(2,1)} %bitcast.422), calls=%async_computation.8 | async-start | bytes 2654208 | tf_op jit(solution)/shard_map/all_to_all | solution.py:982
  1087.2 31.2 %collective-permute-start.150 = (bf16[128,2304]{1,0:T(8,128)(2,1)}, bf16[128,2304]{1,0:T(8,128)(2,1)}, u32[]{:S(2)}, u32[]{:S(2)}) collective-permute-start(bf16[128,2304]{1,0:T(8,128)(2,1)} %pad_maximum_fusion.23), channel_id=1, source_target_pairs={{0,4},{1,5},{2,6},{3,7},{4,0},{5,1},{6,2},{7,3},{8,12},{9,13},{10,... | collective-permute-start | bytes 1769480 | tf_op jit(solution)/shard_map/ppermute | solution.py:928
  1090.0 28.5 %collective-permute-start.148 = (bf16[128,2304]{1,0:T(8,128)(2,1)}, bf16[128,2304]{1,0:T(8,128)(2,1)}, u32[]{:S(2)}, u32[]{:S(2)}) collective-permute-start(bf16[128,2304]{1,0:T(8,128)(2,1)} %pad_maximum_fusion.22), channel_id=1, source_target_pairs={{0,2},{1,3},{2,0},{3,1},{4,6},{5,7},{6,4},{7,5},{8,10},{9,11},{10,... | collective-permute-start | bytes 1769480 | tf_op jit(solution)/shard_map/ppermute | solution.py:928
  (277 other events, 3280.0 us)
Sparse Core Ops, SparseCore 0:
  25.1 52.1 all-gather.5
  78.9 29.1 all-gather.7
  109.7 98.2 all-gather.9
  209.4 97.4 all-gather.11
  308.4 97.4 all-gather.13
  644.1 94.2 reduce-scatter.7
  792.5 94.0 reduce-scatter.9
  888.9 95.3 reduce-scatter.11
  1030.3 46.6 reduce-scatter.5
  1079.9 28.6 reduce-scatter.13

commit v3 on v2

--- a/solution.py
+++ b/solution.py
@@ -1052,8 +1052,15 @@
         [by_head(query_codes), by_head(key_codes), by_head(value_codes)], axis=2
     )
     inputs = tokens.astype(F32)
-    qkv_codes = gather_rows(merged(tp_columns(qkv_blocks)))
-    normed = tp_gather(rms_norm(inputs, pre_attn_gain).astype(BF))
+    qkv_mine = merged(tp_columns(qkv_blocks))
+    qkv_codes = gather_rows(qkv_mine)
+    gate_mine = merged(tp_columns(by_ff(after(gate_codes, qkv_mine))))
+    up_mine = merged(tp_columns(by_ff(after(up_codes, gate_mine))))
+    gate_codes_t = gather_rows(gate_mine)
+    normed_own, up_mine = lax.optimization_barrier(
+        (rms_norm(inputs, pre_attn_gain).astype(BF), up_mine)
+    )
+    normed = after(tp_gather(normed_own), qkv_scale)
 
     whole_heads = group_count == 1 and 8 % planes == 0
     heads_per_plane = max(1, 8 // planes)
@@ -1083,9 +1090,6 @@
             result = lax.dynamic_update_index_in_dim(result, moved, (rank + step) % planes, 0)
         return result
 
-    gate_mine = merged(tp_columns(by_ff(after(gate_codes, normed, qkv_scale))))
-    normed, gate_mine = lax.optimization_barrier((normed, gate_mine))
-    gate_codes_t = gather_rows(gate_mine)
     output_pieces = gather_rows(output_codes)
 
     blocks_at = jnp.stack([t_index ^ (c + 2 * x + 4 * y) for c in (0, 1) for y in (0, 1) for x in (0, 1)])
@@ -1129,7 +1133,7 @@
     v_all = jnp.concatenate(v_parts, axis=1)
     attended = attend(qpos, kpos, q, k_all, v_all, tok_rows)
 
-    up_codes_t = gather_rows(merged(tp_columns(by_ff(after(up_codes, k_near)))))
+    up_codes_t = gather_rows(up_mine)
     down_codes_t = gather_rows(down_codes)
 
     slot_of, live_of, cot_of = [], [], []
@@ -1230,18 +1234,10 @@
 
     o_grad = jnp.stack([kept[w]["o_grad"] for w in widths])
     turns = (cosine, sine, jnp.cos(key_angles), jnp.sin(key_angles))
-    out_total = dot_tn(
-        attended.reshape(SLOTS * group_rows, HD),
-        jnp.concatenate([kept[w]["out_round"] for w in widths], axis=0),
-    )
-    out_total = (out_total / o_scale_all).astype(BF)
-    if whole_heads:
-        out_pieces = heads_to_pieces(out_total.reshape(planes, o_rows, model))
-        out_pieces = out_pieces.reshape(planes * o_rows, model)
-    else:
-        whole = jnp.zeros((HEADS * HD, model), BF)
-        out_pieces = lax.dynamic_update_slice_in_dim(whole, out_total, t_index * HD, 0)
+    gate_back = tp_columns(gate_sum.reshape(8, d_rows, ff_cols))
+    up_back = tp_columns(up_sum.reshape(8, d_rows, ff_cols))
     q_grad, dk, dv = attend_back(qpos, kpos, turns, q, k_all, v_all, o_grad, tok_rows)
+    q_grad, dk, dv, gate_back = lax.optimization_barrier((q_grad, dk, dv, gate_back))
     other = 1 - core
 
     def half_of(values, which):
@@ -1263,19 +1259,31 @@
     qkv_scale_acc = jnp.sum(qkv_raw.astype(F32) * qkv_grad, axis=(0, 1))
     qkv_rows = jnp.sum(qkv_round.astype(F32), axis=0).astype(BF)
     qkv_total = (dot_tn(normed, qkv_rows) / qkv_scale).astype(BF)
-    qkv_total, out_pieces = lax.optimization_barrier((qkv_total, out_pieces))
     qkv_sum = scatter_rows(qkv_total)
+    out_total = dot_tn(
+        after(attended, qkv_total).reshape(SLOTS * group_rows, HD),
+        jnp.concatenate([kept[w]["out_round"] for w in widths], axis=0),
+    )
+    out_total = (out_total / o_scale_all).astype(BF)
+    if whole_heads:
+        out_pieces = heads_to_pieces(out_total.reshape(planes, o_rows, model))
+        out_pieces = out_pieces.reshape(planes * o_rows, model)
+    else:
+        whole = jnp.zeros((HEADS * HD, model), BF)
+        out_pieces = lax.dynamic_update_slice_in_dim(whole, out_total, t_index * HD, 0)
+    low, high = project_back(qkv_round, qkv_w)
+    low, up_back = lax.optimization_barrier((low, up_back))
+    normed_parts = tp_scatter(low, high)
+    gate_grad = by_ff_back(gate_back).astype(F32)
+    up_grad = by_ff_back(up_back).astype(F32)
+    down_grad = down_sum.reshape(ff_rows, model).astype(F32)
+    out_pieces, qkv_sum, gate_grad, up_grad, down_grad = lax.optimization_barrier(
+        (out_pieces, qkv_sum, gate_grad, up_grad, down_grad)
+    )
     if whole_heads:
         out_sum = scatter_rows(out_pieces)
     else:
         out_sum = lax.psum_scatter(out_pieces, ALL, scatter_dimension=0, tiled=True)
-    normed_parts = tp_scatter(*project_back(qkv_round, qkv_w))
-    gate_grad = by_ff_back(tp_columns(gate_sum.reshape(8, d_rows, ff_cols))).astype(F32)
-    up_grad = by_ff_back(tp_columns(up_sum.reshape(8, d_rows, ff_cols))).astype(F32)
-    down_grad = down_sum.reshape(ff_rows, model).astype(F32)
-    normed_parts, qkv_sum, gate_grad, up_grad, down_grad = lax.optimization_barrier(
-        (normed_parts, qkv_sum, gate_grad, up_grad, down_grad)
-    )
     normed_grad = total(normed_parts)
     _, pull_one = jax.vjp(rms_norm, inputs, pre_attn_gain)
     input_part, gain_one = pull_one(normed_grad)

time: 1170 us -> 1170 us (level)
  blocking collectives: 59.4 us -> 37.1 us
    all_to_all x3 -> x2, blocking collectives: 59.4 us -> 37.1 us  [tp_columns(): lax.all_to_all(blocks, 'fsdp', 0, 0, tiled=True, axis_index_groups=groups)]
    all_to_all x3 -> x4, waiting for transfers between devices: 14.5 us -> 36.6 us  [tp_columns(): lax.all_to_all(blocks, 'fsdp', 0, 0, tiled=True, axis_index_groups=groups)]
    unnamed x340 -> x310, local copies, waits for them, and re-layouts: 29.5 us -> 20.1 us
  transfers between devices with their start and end apart: 173 -> 174, of which waited for: 71 -> 69; matrix products, arithmetic and copies ran while one was open for 19% -> 20% of each run, Pallas kernels for 28% -> 28%
where the time goes in v3:
time: 1170 us; the launch traced here: 1160 us
  Pallas kernels  402 us (34%)
  waiting for transfers between devices  301 us (26%)
  starting transfers between devices  140 us (12%)
  local copies, waits for them, and re-layouts  132 us (11%)
  matrix products  64.9 us (6%)
  other arithmetic  58.8 us (5%)
  blocking collectives  37.1 us (3%)
  between operations  23 us (2%)
    ppermute x142, waiting for transfers between devices, swap(): return lax.ppermute(values, 'fsdp', [(i, i ^ mask) for i in range(width)])  225 us
    pallas_call x3, Pallas kernels, ffn_back(): pl.pallas_call(ffn_back_kernel, grid=(rows // chunk,), in_specs=[wide, bl...  99.1 us
    ppermute x142, starting transfers between devices, swap(): return lax.ppermute(values, 'fsdp', [(i, i ^ mask) for i in range(width)])  92.5 us
    pallas_call x3, Pallas kernels, ffn_in(): pl.pallas_call(functools.partial(ffn_in_kernel, width, len(pieces)), grid...  65.3 us
    dot_general x4, matrix products, dot_tn(): lax.dot_general(left, right, (((0,), (0,)), ((), ())), preferred_element_...  64.9 us
    pallas_call x3, Pallas kernels, ffn_out(): pl.pallas_call(functools.partial(ffn_out_kernel, width), grid=(rows // ch...  40.6 us
    all_to_all x2, blocking collectives, tp_columns(): lax.all_to_all(blocks, 'fsdp', 0, 0, tiled=True, axis_index_groups=groups)  37.1 us
    all_to_all x4, waiting for transfers between devices, tp_columns(): lax.all_to_all(blocks, 'fsdp', 0, 0, tiled=True, axis_index_groups=groups)  36.6 us
  transfers between devices with their start and end apart: 174, of which 69 were waited for; matrix products, arithmetic and copies ran while one was open for 20% of the time, Pallas kernels for 28%

profile of v3, /device:TPU:0, one launch (start us, length us, event | category | flops | bytes accessed | tf_op | source)
XLA Modules:
  0.0 1158.6 jit_solution(10564077920446873408)
XLA Ops:
  9.4 15.5 %all_to_all.30 = bf16[8,72,512]{2,1,0:T(8,128)(2,1)} all-to-all(bf16[8,72,512]{2,1,0:T(8,128)(2,1)S(1)} %pad_maximum_fusion.3), channel_id=1, replica_groups=mesh['dp'=4,'fsdp'=8] {'fsdp'}, dimensions={0} | all-to-all | bytes 1179648 | tf_op jit(solution)/shard_map/all_to_all | solution.py:982
  30.4 21.6 %all_to_all.31 = bf16[8,72,1152]{2,1,0:T(8,128)(2,1)} all-to-all(bf16[8,72,1152]{2,1,0:T(8,128)(2,1)S(1)} %reshape.533), channel_id=1, replica_groups=mesh['dp'=4,'fsdp'=8] {'fsdp'}, dimensions={0} | all-to-all | bytes 2654208 | tf_op jit(solution)/shard_map/all_to_all | solution.py:982
  67.2 16.2 %all-to-all-done.2 = bf16[8,72,1152]{2,1,0:T(8,128)(2,1)S(1)} async-done(((bf16[8,72,1152]{2,1,0:T(8,128)(2,1)}), bf16[8,72,1152]{2,1,0:T(8,128)(2,1)S(1)}, u32[]{:S(2)}, u32[]{:S(2)}) %all-to-all-start.2) | async-done | bytes 1327136 | tf_op jit(solution)/shard_map/all_to_all | solution.py:982
  86.6 9.7 collective-permute-done.11
  118.1 6.2 join.1.a_ref
  124.3 17.6 %project.1 = (bf16[3,1024,512]{2,1,0:T(8,128)(2,1)}, bf16[3,1024,256]{2,1,0:T(8,128)(2,1)}, f32[3,1024,256]{2,1,0:T(8,128)}, bf16[3,2304,512]{2,1,0:T(8,128)(2,1)}) custom-call(bf16[1024,2304]{1,0:T(8,128)(2,1)} %join.1.a_ref, bf16[2304,512]{1,0:T(8,128)(2,1)} %all-gather.6.cloned.1.call-done.w_hbm, f32[1,512]{1,0:T(1,128)} %bitcast.443, ...), custom_call_target="tpu_custom_call" | custom-call | flops 7247757312 | bytes 19660800 | tf_op jit(solution)/shard_map/project/pallas_call | solution.py:196
  146.2 5.2 collective-permute-start.16
  161.8 7.0 heads.1
  168.8 14.6 %attend.1.o_ref = bf16[3,1024,256]{2,1,0:T(8,128)(2,1)} custom-call(s32[1024,1]{1,0:T(8,128)} %copy.61.qpos_ref, s32[1,1024]{1,0:T(1,128)} %compare_select_fusion.kpos_ref, bf16[3,1024,256]{2,1,0:T(8,128)(2,1)} %get-tuple-element.173.q_ref, bf16[3,1024,256]{2,1,0:T(8,128)(2,1)} %get-tuple-element.175.k_ref, bf16[3,1024,256]{2,1,0:T(8,128)(2,1)} %get-tuple-element.176.v_ref), custom_call_target="tpu_custom_call" | custom-call | flops 3221225472 | bytes 4718592 | tf_op jit(solution)/shard_map/attend/pallas_call | solution.py:136
  183.3 6.0 output_partial.3
  189.3 6.1 output_partial.4
  195.4 6.1 output_partial.5
  205.6 5.1 collective-permute-done.47
  241.5 7.4 collective-permute-done.51.from_y_ref
  255.3 6.4 collective-permute-done.37.from_y_ref
  268.0 6.3 collective-permute-done.23.from_y_ref
  279.7 7.3 collective-permute-done.53.refs_2_
  289.1 10.5 collective-permute-done.39.refs_2_
  307.2 5.0 collective-permute-done.25.refs_2_
  316.0 6.3 collective-permute-done.54.refs_3_
  335.3 22.2 %ffn_in.5 = (bf16[1024,1152]{1,0:T(8,128)(2,1)}, bf16[1024,1152]{1,0:T(8,128)(2,1)}, bf16[1024,1152]{1,0:T(8,128)(2,1)}, bf16[1024,2304]{1,0:T(8,128)(2,1)}, bf1...) custom-call(bf16[128,2304]{1,0:T(8,128)(2,1)} %get-tuple-element.190.refs_0_, ...), custom_call_target="tpu_custom_call" | custom-call | flops 10871635968 | bytes 22413312 | tf_op jit(solution)/shard_map/ffn_in/pallas_call | solution.py:624
  358.7 21.9 %ffn_in.4 = (bf16[1024,1152]{1,0:T(8,128)(2,1)}, bf16[1024,1152]{1,0:T(8,128)(2,1)}, bf16[1024,1152]{1,0:T(8,128)(2,1)}, bf16[1024,2304]{1,0:T(8,128)(2,1)}, bf1...) custom-call(bf16[128,2304]{1,0:T(8,128)(2,1)} %get-tuple-element.185.refs_0_, ...), custom_call_target="tpu_custom_call" | custom-call | flops 10871635968 | bytes 22413312 | tf_op jit(solution)/shard_map/ffn_in/pallas_call | solution.py:624
  381.6 21.3 %ffn_in.3 = (bf16[1024,1152]{1,0:T(8,128)(2,1)}, bf16[1024,1152]{1,0:T(8,128)(2,1)}, bf16[1024,1152]{1,0:T(8,128)(2,1)}, bf16[1024,2304]{1,0:T(8,128)(2,1)}, bf1...) custom-call(bf16[128,2304]{1,0:T(8,128)(2,1)} %get-tuple-element.179.refs_0_, bf16[128,2304]{1,0:T(8,128)(2,1)} %copy-done.73, ...), custom_call_target="tpu_custom_call" | custom-call | flops 10871635968 | bytes 22413312 | tf_op jit(solution)/shard_map/ffn_in/pallas_call | solution.py:624
  404.8 12.9 %ffn_out.3 = (bf16[512,2304]{1,0:T(8,128)(2,1)}, bf16[512,2304]{1,0:T(8,128)(2,1)}, bf16[1152,2304]{1,0:T(8,128)(2,1)}) custom-call(bf16[1024,1152]{1,0:T(8,128)(2,1)} %get-tuple-element.194.h_ref.refs_30_, bf16[1152,2304]{1,0:T(8,128)(2,1)} %all-gather.14.cloned.1.call-done.d_hbm), custom_call_target="tpu_custom_call" | custom-call | flops 5435817984 | bytes 17694720 | tf_op jit(solution)/shard_map/ffn_out/pallas_call | solution.py:728
  417.8 13.8 %ffn_out.4 = (bf16[512,2304]{1,0:T(8,128)(2,1)}, bf16[512,2304]{1,0:T(8,128)(2,1)}, bf16[1152,2304]{1,0:T(8,128)(2,1)}) custom-call(bf16[1024,1152]{1,0:T(8,128)(2,1)} %get-tuple-element.196.h_ref.refs_31_, bf16[1152,2304]{1,0:T(8,128)(2,1)} %all-gather.14.cloned.1.call-done.d_hbm), custom_call_target="tpu_custom_call" | custom-call | flops 5435817984 | bytes 17694720 | tf_op jit(solution)/shard_map/ffn_out/pallas_call | solution.py:728
  449.8 13.8 %ffn_out.5 = (bf16[512,2304]{1,0:T(8,128)(2,1)}, bf16[512,2304]{1,0:T(8,128)(2,1)}, bf16[1152,2304]{1,0:T(8,128)(2,1)}) custom-call(bf16[1024,1152]{1,0:T(8,128)(2,1)} %get-tuple-element.210.h_ref.refs_32_, bf16[1152,2304]{1,0:T(8,128)(2,1)} %all-gather.14.cloned.1.call-done.d_hbm), custom_call_target="tpu_custom_call" | custom-call | flops 5435817984 | bytes 17694720 | tf_op jit(solution)/shard_map/ffn_out/pallas_call | solution.py:728
  468.0 5.6 collective-permute-done.67
  486.7 19.6 %collective-permute-done.65.from_y_ref = bf16[128,2304]{1,0:T(8,128)(2,1)} collective-permute-done((bf16[128,2304]{1,0:T(8,128)(2,1)S(1)}, bf16[128,2304]{1,0:T(8,128)(2,1)}, u32[]{:S(2)}, u32[]{:S(2)}) %collective-permute-start.65) | collective-permute-done | bytes 589856 | tf_op jit(solution)/shard_map/ppermute | solution.py:928
  524.5 11.1 collective-permute-done.86.refs_12_
  537.7 10.5 collective-permute-done.77.refs_2_
  554.7 6.2 collective-permute-done.75.from_y_ref
  574.3 11.5 collective-permute-done.95.refs_22_
  598.0 5.0 copy-done.29
  605.0 33.2 %down_grad.1 = (bf16[1152,2304]{1,0:T(8,128)(2,1)}, bf16[1024,2304]{1,0:T(8,128)(2,1)}, bf16[1024,2304]{1,0:T(8,128)(2,1)}, bf16[1024,2304]{1,0:T(8,128)(2,1)}) custom-call(bf16[128,2304]{1,0:T(8,128)(2,1)} %get-tuple-element.217.refs_0_, bf16[128,2304]{1,0:T(8,128)(2,1)} %copy-done.70, bf16[128,2304]{1,0:T(8,128)(2,1)} %copy-done.67, ...), custom_call_target="tpu_custom_call" | custom-call | flops 16307453952 | bytes 40697856 | tf_op jit(solution)/shard_map/down_grad/pallas_call | solution.py:687
  638.3 5.2 constant_dynamic-update-slice_fusion
  643.5 32.8 %ffn_back.3 = (bf16[512,2304]{1,0:T(8,128)(2,1)}, bf16[512,2304]{1,0:T(8,128)(2,1)}, bf16[1024,1152]{1,0:T(8,128)(2,1)}, bf16[1024,1152]{1,0:T(8,128)(2,1)}, f32[1,1152]{1,0:T(1,128)}, /*index=5*/f32[1,1152]{1,0:T(1,128)}) custom-call(bf16[1024,2304]{1,0:T(8,128)(2,1)} %get-tuple-element.220.dr_ref, bf16[1024,1152]{1,0:T(8,128)(2,1)} %get-tuple-element.221.gate_ref, ...), custom_call_target="tpu_custom_call" | custom-call | flops 16307453952 | bytes 34799616 | tf_op jit(solution)/shard_map/ffn_back/pallas_call | solution.py:822
  676.5 32.9 %ffn_back.4 = (bf16[512,2304]{1,0:T(8,128)(2,1)}, bf16[512,2304]{1,0:T(8,128)(2,1)}, bf16[1024,1152]{1,0:T(8,128)(2,1)}, bf16[1024,1152]{1,0:T(8,128)(2,1)}, f32[1,1152]{1,0:T(1,128)}, /*index=5*/f32[1,1152]{1,0:T(1,128)}) custom-call(bf16[1024,2304]{1,0:T(8,128)(2,1)} %get-tuple-element.231.dr_ref, bf16[1024,1152]{1,0:T(8,128)(2,1)} %get-tuple-element.232.gate_ref, ...), custom_call_target="tpu_custom_call" | custom-call | flops 16307453952 | bytes 34799616 | tf_op jit(solution)/shard_map/ffn_back/pallas_call | solution.py:822
  709.7 33.5 %ffn_back.5 = (bf16[512,2304]{1,0:T(8,128)(2,1)}, bf16[512,2304]{1,0:T(8,128)(2,1)}, bf16[1024,1152]{1,0:T(8,128)(2,1)}, bf16[1024,1152]{1,0:T(8,128)(2,1)}, f32[1,1152]{1,0:T(1,128)}, /*index=5*/f32[1,1152]{1,0:T(1,128)}) custom-call(bf16[1024,2304]{1,0:T(8,128)(2,1)} %get-tuple-element.245.dr_ref, bf16[1024,1152]{1,0:T(8,128)(2,1)} %get-tuple-element.246.gate_ref, ...), custom_call_target="tpu_custom_call" | custom-call | flops 16307453952 | bytes 34799616 | tf_op jit(solution)/shard_map/ffn_back/pallas_call | solution.py:822
  756.5 24.8 %fusion.7 = bf16[2304,1152]{1,0:T(8,128)(2,1)} fusion(bf16[3072,2304]{1,0:T(8,128)(2,1)} %constant_dynamic-update-slice_fusion, bf16[1024,1152]{1,0:T(8,128)(2,1)} %get-tuple-element.278, bf16[1024,1152]{1,0:T(8,128)(2,1)} %get-tuple-element.277, bf16[1024,1152]{1,0:T(8,128)(2,1)} %get-tuple-element.276, f32[1152]{0:T(1024)S(1)} %div.91), kind=kOutput, calls=%fused_computation.11 | convolution fusion | flops 16333996032 | bytes 26546688 | tf_op jit(solution)/shard_map/dot_general | solution.py:57
  795.7 8.6 collective-permute-done.107.from_y_ref
  806.1 5.1 output_back.3
  812.6 4.4 collective-permute-done.121.from_y_ref
  818.0 5.1 output_back.4
  825.2 4.4 collective-permute-done.135.from_y_ref
  831.9 5.1 output_back.5
  837.1 5.1 collective-permute-done.109.refs_2_
  843.3 11.7 %collective-permute-done.123.refs_2_ = bf16[128,2304]{1,0:T(8,128)(2,1)} collective-permute-done((bf16[128,2304]{1,0:T(8,128)(2,1)}, bf16[128,2304]{1,0:T(8,128)(2,1)}, u32[]{:S(2)}, u32[]{:S(2)}) %collective-permute-start.123) | collective-permute-done | bytes 589856 | tf_op jit(solution)/shard_map/ppermute | solution.py:928
  859.1 8.4 collective-permute-done.137.refs_2_
  878.8 5.1 collective-permute-done.124.refs_3_
  892.2 25.0 %fusion.6 = bf16[2304,1152]{1,0:T(8,128)(2,1)} fusion(bf16[3072,2304]{1,0:T(8,128)(2,1)} %constant_dynamic-update-slice_fusion, bf16[1024,1152]{1,0:T(8,128)(2,1)} %get-tuple-element.272, bf16[1024,1152]{1,0:T(8,128)(2,1)} %get-tuple-element.271, bf16[1024,1152]{1,0:T(8,128)(2,1)} %get-tuple-element.270, f32[1152]{0:T(1024)S(1)} %div.88), kind=kOutput, calls=%fused_computation.10 | convolution fusion | flops 16333996032 | bytes 26546688 | tf_op jit(solution)/shard_map/dot_general | solution.py:57
  921.0 8.0 head_back.3
  928.9 7.7 head_back.4
  936.7 7.8 head_back.5
  946.8 22.6 %attend_back.1 = (f32[3,1024,256]{2,1,0:T(8,128)}, f32[3,1024,256]{2,1,0:T(8,128)}, f32[3,1024,256]{2,1,0:T(8,128)}) custom-call(s32[1024,1]{1,0:T(8,128)} %copy.61.qpos_ref, s32[1,1024]{1,0:T(1,128)} %compare_select_fusion.kpos_ref, f32[1024,128]{1,0:T(8,128)} %get-tuple-element.418.cos_ref.qcos_ref.kcos_ref, ...), custom_call_target="tpu_custom_call" | custom-call | flops 8053063680 | bytes 4718592 | tf_op jit(solution)/shard_map/attend_back/pallas_call | solution.py:150
  995.9 4.4 reshape.585
  1008.7 14.4 %project_back.1 = (bf16[512,2304]{1,0:T(8,128)(2,1)}, bf16[512,2304]{1,0:T(8,128)(2,1)}) custom-call(bf16[3,1024,512]{2,1,0:T(8,128)(2,1)} %get-tuple-element.323.round_ref, bf16[3,2304,512]{2,1,0:T(8,128)(2,1)} %get-tuple-element.283.w_hbm), custom_call_target="tpu_custom_call" | custom-call | flops 7247757312 | bytes 14942208 | tf_op jit(solution)/shard_map/project_back/pallas_call | solution.py:869
  1023.4 6.8 divide_convert_fusion
  1030.2 8.3 fusion.21
  1044.6 5.0 collective-permute-start.152
  1058.8 20.4 %all-to-all-done.4 = bf16[8,72,1152]{2,1,0:T(8,128)(2,1)S(1)} async-done(((bf16[8,72,1152]{2,1,0:T(8,128)(2,1)}), bf16[8,72,1152]{2,1,0:T(8,128)(2,1)S(1)}, u32[]{:S(2)}, u32[]{:S(2)}) %all-to-all-start.4) | async-done | bytes 1327136 | tf_op jit(solution)/shard_map/all_to_all | solution.py:982
  1084.0 5.5 collective-permute-done.147
  1103.6 4.6 reshape.586
  1108.2 4.3 all-to-all-start.5
  1142.2 7.5 reduce-scatter.14.cloned.1.call-done
  (860 shorter events, 396.2 us)
Async XLA Ops:
  7.2 117.1 %all-gather.6.cloned.1.call-start = ((), (), s32[]{:S(2)}) async-start(), calls=%async_computation.11 | async-start | bytes 2949120 | tf_op jit(solution)/shard_map/all_gather | solution.py:987
  24.9 117.5 %all-gather.8.cloned.1.call-start = ((), (), s32[]{:S(2)}) async-start(), calls=%async_computation.12 | async-start | bytes 1474560 | tf_op jit(solution)/shard_map/all_gather | solution.py:987
  25.7 309.6 %all-gather.10.cloned.1.call-start = ((), (), s32[]{:S(2)}) async-start(), calls=%async_computation.13 | async-start | bytes 6635520 | tf_op jit(solution)/shard_map/all_gather | solution.py:987
  64.9 270.3 %all-gather.12.cloned.1.call-start = ((), (), s32[]{:S(2)}) async-start(), calls=%async_computation.14 | async-start | bytes 6635520 | tf_op jit(solution)/shard_map/all_gather | solution.py:987
  83.9 23.5 %collective-permute-start = (bf16[128,2304]{1,0:T(8,128)(2,1)S(1)}, bf16[128,2304]{1,0:T(8,128)(2,1)}, u32[]{:S(2)}, u32[]{:S(2)}) collective-permute-start(bf16[128,2304]{1,0:T(8,128)(2,1)S(1)} %fusion.26.refs_0_), channel_id=1, source_target_pairs={{0,2},{1,3},{2,0},{3,1},{4,6},{5,7},{6,4},{7,5},{8,10},{9,11},{10,... | collective-permute-start | bytes 1769480 | tf_op jit(solution)/shard_map/ppermute | solution.py:928
  84.6 320.2 %all-gather.14.cloned.1.call-start = ((), (), s32[]{:S(2)}) async-start(), calls=%async_computation.15 | async-start | bytes 6635520 | tf_op jit(solution)/shard_map/all_gather | solution.py:987
  202.9 553.6 %reduce-scatter.6.cloned.1.call-start = ((), (), s32[]{:S(2)}) async-start(), calls=%async_computation.16 | async-start | bytes 6635520 | tf_op jit(solution)/shard_map/reduce_scatter | solution.py:990
  225.4 23.5 %collective-permute-start.51 = (bf16[128,2304]{1,0:T(8,128)(2,1)S(1)}, bf16[128,2304]{1,0:T(8,128)(2,1)S(1)}, u32[]{:S(2)}, u32[]{:S(2)}) collective-permute-start(bf16[128,2304]{1,0:T(8,128)(2,1)S(1)} %pad_maximum_fusion.9), channel_id=1, source_target_pairs={{0,4},{1,5},{2,6},{3,7},{4,0},{5,1},{6,2},{7,3},{8,12},{9,13},{10,... | collective-permute-start | bytes 1769480 | tf_op jit(solution)/shard_map/ppermute | solution.py:928
  232.6 29.2 %collective-permute-start.37 = (bf16[128,2304]{1,0:T(8,128)(2,1)}, bf16[128,2304]{1,0:T(8,128)(2,1)}, u32[]{:S(2)}, u32[]{:S(2)}) collective-permute-start(bf16[128,2304]{1,0:T(8,128)(2,1)} %pad_maximum_fusion.7), channel_id=1, source_target_pairs={{0,4},{1,5},{2,6},{3,7},{4,0},{5,1},{6,2},{7,3},{8,12},{9,13},{10,... | collective-permute-start | bytes 1769480 | tf_op jit(solution)/shard_map/ppermute | solution.py:928
  236.3 26.9 %collective-permute-start.35 = (bf16[128,2304]{1,0:T(8,128)(2,1)}, bf16[128,2304]{1,0:T(8,128)(2,1)}, u32[]{:S(2)}, u32[]{:S(2)}) collective-permute-start(bf16[128,2304]{1,0:T(8,128)(2,1)} %pad_maximum_fusion.6), channel_id=1, source_target_pairs={{0,2},{1,3},{2,0},{3,1},{4,6},{5,7},{6,4},{7,5},{8,10},{9,11},{10,... | collective-permute-start | bytes 1769480 | tf_op jit(solution)/shard_map/ppermute | solution.py:928
  238.9 35.5 %collective-permute-start.23 = (bf16[128,2304]{1,0:T(8,128)(2,1)}, bf16[128,2304]{1,0:T(8,128)(2,1)}, u32[]{:S(2)}, u32[]{:S(2)}) collective-permute-start(bf16[128,2304]{1,0:T(8,128)(2,1)} %pad_maximum_fusion.5), channel_id=1, source_target_pairs={{0,4},{1,5},{2,6},{3,7},{4,0},{5,1},{6,2},{7,3},{8,12},{9,13},{10,... | collective-permute-start | bytes 1769480 | tf_op jit(solution)/shard_map/ppermute | solution.py:928
  249.0 26.9 %collective-permute-start.21 = (bf16[128,2304]{1,0:T(8,128)(2,1)}, bf16[128,2304]{1,0:T(8,128)(2,1)}, u32[]{:S(2)}, u32[]{:S(2)}) collective-permute-start(bf16[128,2304]{1,0:T(8,128)(2,1)} %pad_maximum_fusion.4), channel_id=1, source_target_pairs={{0,2},{1,3},{2,0},{3,1},{4,6},{5,7},{6,4},{7,5},{8,10},{9,11},{10,... | collective-permute-start | bytes 1769480 | tf_op jit(solution)/shard_map/ppermute | solution.py:928
  254.5 32.6 %collective-permute-start.53 = (bf16[128,2304]{1,0:T(8,128)(2,1)}, bf16[128,2304]{1,0:T(8,128)(2,1)}, u32[]{:S(2)}, u32[]{:S(2)}) collective-permute-start(bf16[128,2304]{1,0:T(8,128)(2,1)} %get-tuple-element.190.refs_0_), channel_id=1, source_target_pairs={{0,4},{1,5},{2,6},{3,7},{4,0},{5,1},{6,2},{7,3},{8,12},{9,13},{10,... | collective-permute-start | bytes 1769480 | tf_op jit(solution)/shard_map/ppermute | solution.py:928
  261.7 26.8 %collective-permute-start.52 = (bf16[128,2304]{1,0:T(8,128)(2,1)}, bf16[128,2304]{1,0:T(8,128)(2,1)}, u32[]{:S(2)}, u32[]{:S(2)}) collective-permute-start(bf16[128,2304]{1,0:T(8,128)(2,1)} %get-tuple-element.190.refs_0_), channel_id=1, source_target_pairs={{0,2},{1,3},{2,0},{3,1},{4,6},{5,7},{6,4},{7,5},{8,10},{9,11},{10,... | collective-permute-start | bytes 1769480 | tf_op jit(solution)/shard_map/ppermute | solution.py:928
  267.1 32.4 %collective-permute-start.39 = (bf16[128,2304]{1,0:T(8,128)(2,1)}, bf16[128,2304]{1,0:T(8,128)(2,1)S(1)}, u32[]{:S(2)}, u32[]{:S(2)}) collective-permute-start(bf16[128,2304]{1,0:T(8,128)(2,1)} %get-tuple-element.185.refs_0_), channel_id=1, source_target_pairs={{0,4},{1,5},{2,6},{3,7},{4,0},{5,1},{6,2},{7,3},{8,12},{9,13},{10,... | collective-permute-start | bytes 1769480 | tf_op jit(solution)/shard_map/ppermute | solution.py:928
  274.4 26.8 %collective-permute-start.38 = (bf16[128,2304]{1,0:T(8,128)(2,1)}, bf16[128,2304]{1,0:T(8,128)(2,1)}, u32[]{:S(2)}, u32[]{:S(2)}) collective-permute-start(bf16[128,2304]{1,0:T(8,128)(2,1)} %get-tuple-element.185.refs_0_), channel_id=1, source_target_pairs={{0,2},{1,3},{2,0},{3,1},{4,6},{5,7},{6,4},{7,5},{8,10},{9,11},{10,... | collective-permute-start | bytes 1769480 | tf_op jit(solution)/shard_map/ppermute | solution.py:928
  275.9 28.7 %collective-permute-start.56 = (bf16[128,2304]{1,0:T(8,128)(2,1)}, bf16[128,2304]{1,0:T(8,128)(2,1)}, u32[]{:S(2)}, u32[]{:S(2)}) collective-permute-start(bf16[128,2304]{1,0:T(8,128)(2,1)} %get-tuple-element.190.refs_0_), channel_id=1, source_target_pairs={{0,1},{1,0},{2,3},{3,2},{4,5},{5,4},{6,7},{7,6},{8,9},{9,8},{10,11... | collective-permute-start | bytes 1769480 | tf_op jit(solution)/shard_map/ppermute | solution.py:928
  288.6 23.6 %collective-permute-start.25 = (bf16[128,2304]{1,0:T(8,128)(2,1)}, bf16[128,2304]{1,0:T(8,128)(2,1)S(1)}, u32[]{:S(2)}, u32[]{:S(2)}) collective-permute-start(bf16[128,2304]{1,0:T(8,128)(2,1)} %get-tuple-element.179.refs_0_), channel_id=1, source_target_pairs={{0,4},{1,5},{2,6},{3,7},{4,0},{5,1},{6,2},{7,3},{8,12},{9,13},{10,... | collective-permute-start | bytes 1769480 | tf_op jit(solution)/shard_map/ppermute | solution.py:928
  333.2 24.3 %collective-permute-start.27 = (bf16[64,2304]{1,0:T(8,128)(2,1)S(1)}, bf16[64,2304]{1,0:T(8,128)(2,1)S(1)}, u32[]{:S(2)}, u32[]{:S(2)}) collective-permute-start(bf16[64,2304]{1,0:T(8,128)(2,1)S(1)} %slice.581), channel_id=1, source_target_pairs={{0,4},{1,5},{2,6},{3,7},{4,0},{5,1},{6,2},{7,3},{8,12},{9,13},{10,... | collective-permute-start | bytes 884744 | tf_op jit(solution)/shard_map/ppermute | solution.py:928
  334.2 24.0 %collective-permute-start.43 = (bf16[128,2304]{1,0:T(8,128)(2,1)}, bf16[128,2304]{1,0:T(8,128)(2,1)}, u32[]{:S(2)}, u32[]{:S(2)}) collective-permute-start(bf16[128,2304]{1,0:T(8,128)(2,1)} %collective-permute-done.38.refs_1_), channel_id=1, source_target_pairs={{0,1},{1,0},{2,3},{3,2},{4,5},{5,4},{6,7},{7,6},{8,9},{9,8},{10,11... | collective-permute-start | bytes 1769480 | tf_op jit(solution)/shard_map/ppermute | solution.py:928
  334.2 24.4 %collective-permute-start.44 = (bf16[128,2304]{1,0:T(8,128)(2,1)S(1)}, bf16[128,2304]{1,0:T(8,128)(2,1)}, u32[]{:S(2)}, u32[]{:S(2)}) collective-permute-start(bf16[128,2304]{1,0:T(8,128)(2,1)S(1)} %collective-permute-done.39.refs_2_), channel_id=1, source_target_pairs={{0,1},{1,0},{2,3},{3,2},{4,5},{5,4},{6,7},{7,6},{8,9},{9,8},{10,11... | collective-permute-start | bytes 1769480 | tf_op jit(solution)/shard_map/ppermute | solution.py:928
  334.8 23.3 %collective-permute-start.46 = (bf16[64,2304]{1,0:T(8,128)(2,1)}, bf16[64,2304]{1,0:T(8,128)(2,1)}, u32[]{:S(2)}, u32[]{:S(2)}) collective-permute-start(bf16[64,2304]{1,0:T(8,128)(2,1)} %collective-permute-done.41.refs_4_), channel_id=1, source_target_pairs={{0,1},{1,0},{2,3},{3,2},{4,5},{5,4},{6,7},{7,6},{8,9},{9,8},{10,11... | collective-permute-start | bytes 884744 | tf_op jit(solution)/shard_map/ppermute | solution.py:928
  357.5 23.1 %collective-permute-start.28 = (bf16[128,2304]{1,0:T(8,128)(2,1)S(1)}, bf16[128,2304]{1,0:T(8,128)(2,1)S(1)}, u32[]{:S(2)}, u32[]{:S(2)}) collective-permute-start(bf16[128,2304]{1,0:T(8,128)(2,1)S(1)} %copy-done.131), channel_id=1, source_target_pairs={{0,1},{1,0},{2,3},{3,2},{4,5},{5,4},{6,7},{7,6},{8,9},{9,8},{10,11... | collective-permute-start | bytes 1769480 | tf_op jit(solution)/shard_map/ppermute | solution.py:928
  477.1 36.8 %collective-permute-start.70 = (bf16[128,2304]{1,0:T(8,128)(2,1)}, bf16[128,2304]{1,0:T(8,128)(2,1)S(1)}, u32[]{:S(2)}, u32[]{:S(2)}) collective-permute-start(bf16[128,2304]{1,0:T(8,128)(2,1)} %pad_maximum_fusion.13), channel_id=1, source_target_pairs={{0,4},{1,5},{2,6},{3,7},{4,0},{5,1},{6,2},{7,3},{8,12},{9,13},{10,... | collective-permute-start | bytes 1769480 | tf_op jit(solution)/shard_map/ppermute | solution.py:928
  478.6 35.3 %collective-permute-start.68 = (bf16[128,2304]{1,0:T(8,128)(2,1)}, bf16[128,2304]{1,0:T(8,128)(2,1)S(1)}, u32[]{:S(2)}, u32[]{:S(2)}) collective-permute-start(bf16[128,2304]{1,0:T(8,128)(2,1)} %pad_maximum_fusion.12), channel_id=1, source_target_pairs={{0,2},{1,3},{2,0},{3,1},{4,6},{5,7},{6,4},{7,5},{8,10},{9,11},{10,... | collective-permute-start | bytes 1769480 | tf_op jit(solution)/shard_map/ppermute | solution.py:928
  481.6 24.8 %collective-permute-start.65 = (bf16[128,2304]{1,0:T(8,128)(2,1)S(1)}, bf16[128,2304]{1,0:T(8,128)(2,1)}, u32[]{:S(2)}, u32[]{:S(2)}) collective-permute-start(bf16[128,2304]{1,0:T(8,128)(2,1)S(1)} %pad_maximum_fusion.11), channel_id=1, source_target_pairs={{0,4},{1,5},{2,6},{3,7},{4,0},{5,1},{6,2},{7,3},{8,12},{9,13},{10,... | collective-permute-start | bytes 1769480 | tf_op jit(solution)/shard_map/ppermute | solution.py:928
  481.9 27.9 %collective-permute-start.63 = (bf16[128,2304]{1,0:T(8,128)(2,1)S(1)}, bf16[128,2304]{1,0:T(8,128)(2,1)}, u32[]{:S(2)}, u32[]{:S(2)}) collective-permute-start(bf16[128,2304]{1,0:T(8,128)(2,1)S(1)} %pad_maximum_fusion.10), channel_id=1, source_target_pairs={{0,2},{1,3},{2,0},{3,1},{4,6},{5,7},{6,4},{7,5},{8,10},{9,11},{10,... | collective-permute-start | bytes 1769480 | tf_op jit(solution)/shard_map/ppermute | solution.py:928
  484.7 35.5 %collective-permute-start.72 = (bf16[64,2304]{1,0:T(8,128)(2,1)}, bf16[64,2304]{1,0:T(8,128)(2,1)}, u32[]{:S(2)}, u32[]{:S(2)}) collective-permute-start(bf16[64,2304]{1,0:T(8,128)(2,1)} %get-tuple-element.358), channel_id=1, source_target_pairs={{0,4},{1,5},{2,6},{3,7},{4,0},{5,1},{6,2},{7,3},{8,12},{9,13},{10,... | collective-permute-start | bytes 884744 | tf_op jit(solution)/shard_map/ppermute | solution.py:928
  520.2 33.3 %collective-permute-start.89 = (bf16[128,2304]{1,0:T(8,128)(2,1)}, bf16[128,2304]{1,0:T(8,128)(2,1)S(1)}, u32[]{:S(2)}, u32[]{:S(2)}) collective-permute-start(bf16[128,2304]{1,0:T(8,128)(2,1)} %get-tuple-element.218.refs_10_), channel_id=1, source_target_pairs={{0,1},{1,0},{2,3},{3,2},{4,5},{5,4},{6,7},{7,6},{8,9},{9,8},{10,11... | collective-permute-start | bytes 1769480 | tf_op jit(solution)/shard_map/ppermute | solution.py:928
  520.2 28.0 %collective-permute-start.77 = (bf16[128,2304]{1,0:T(8,128)(2,1)}, bf16[128,2304]{1,0:T(8,128)(2,1)S(1)}, u32[]{:S(2)}, u32[]{:S(2)}) collective-permute-start(bf16[128,2304]{1,0:T(8,128)(2,1)} %get-tuple-element.217.refs_0_), channel_id=1, source_target_pairs={{0,4},{1,5},{2,6},{3,7},{4,0},{5,1},{6,2},{7,3},{8,12},{9,13},{10,... | collective-permute-start | bytes 1769480 | tf_op jit(solution)/shard_map/ppermute | solution.py:928
  521.7 30.2 %collective-permute-start.76 = (bf16[128,2304]{1,0:T(8,128)(2,1)}, bf16[128,2304]{1,0:T(8,128)(2,1)S(1)}, u32[]{:S(2)}, u32[]{:S(2)}) collective-permute-start(bf16[128,2304]{1,0:T(8,128)(2,1)} %get-tuple-element.217.refs_0_), channel_id=1, source_target_pairs={{0,2},{1,3},{2,0},{3,1},{4,6},{5,7},{6,4},{7,5},{8,10},{9,11},{10,... | collective-permute-start | bytes 1769480 | tf_op jit(solution)/shard_map/ppermute | solution.py:928
  536.2 24.6 %collective-permute-start.75 = (bf16[128,2304]{1,0:T(8,128)(2,1)S(1)}, bf16[128,2304]{1,0:T(8,128)(2,1)S(1)}, u32[]{:S(2)}, u32[]{:S(2)}) collective-permute-start(bf16[128,2304]{1,0:T(8,128)(2,1)S(1)} %pad_maximum_fusion.15), channel_id=1, source_target_pairs={{0,4},{1,5},{2,6},{3,7},{4,0},{5,1},{6,2},{7,3},{8,12},{9,13},{10,... | collective-permute-start | bytes 1769480 | tf_op jit(solution)/shard_map/ppermute | solution.py:928
  638.3 279.0 %reduce-scatter.8.cloned.1.call-start = ((), (), s32[]{:S(2)}) async-start(), calls=%async_computation.17 | async-start | bytes 6635520 | tf_op jit(solution)/shard_map/reduce_scatter | solution.py:990
  676.3 67.2 %collective-permute-start.103 = (bf16[512,2304]{1,0:T(8,128)(2,1)}, bf16[512,2304]{1,0:T(8,128)(2,1)}, u32[]{:S(2)}, u32[]{:S(2)}) collective-permute-start(bf16[512,2304]{1,0:T(8,128)(2,1)} %get-tuple-element.227), channel_id=1, source_target_pairs={{0,1},{1,0},{2,3},{3,2},{4,5},{5,4},{6,7},{7,6},{8,9},{9,8},{10,11... | collective-permute-start | bytes 7077896 | tf_op jit(solution)/shard_map/ppermute | solution.py:928
  709.3 39.9 %collective-permute-start.117 = (bf16[512,2304]{1,0:T(8,128)(2,1)}, bf16[512,2304]{1,0:T(8,128)(2,1)}, u32[]{:S(2)}, u32[]{:S(2)}) collective-permute-start(bf16[512,2304]{1,0:T(8,128)(2,1)} %get-tuple-element.238), channel_id=1, source_target_pairs={{0,1},{1,0},{2,3},{3,2},{4,5},{5,4},{6,7},{7,6},{8,9},{9,8},{10,11... | collective-permute-start | bytes 7077896 | tf_op jit(solution)/shard_map/ppermute | solution.py:928
  746.6 36.1 %collective-permute-start.104 = (bf16[64,2304]{1,0:T(8,128)(2,1)}, bf16[64,2304]{1,0:T(8,128)(2,1)}, u32[]{:S(2)}, u32[]{:S(2)}) collective-permute-start(bf16[64,2304]{1,0:T(8,128)(2,1)} %get-tuple-element.340), channel_id=1, source_target_pairs={{0,4},{1,5},{2,6},{3,7},{4,0},{5,1},{6,2},{7,3},{8,12},{9,13},{10,... | collective-permute-start | bytes 884744 | tf_op jit(solution)/shard_map/ppermute | solution.py:928
  748.0 36.0 %collective-permute-start.106 = (bf16[64,2304]{1,0:T(8,128)(2,1)}, bf16[64,2304]{1,0:T(8,128)(2,1)}, u32[]{:S(2)}, u32[]{:S(2)}) collective-permute-start(bf16[64,2304]{1,0:T(8,128)(2,1)} %get-tuple-element.338), channel_id=1, source_target_pairs={{0,2},{1,3},{2,0},{3,1},{4,6},{5,7},{6,4},{7,5},{8,10},{9,11},{10,... | collective-permute-start | bytes 884744 | tf_op jit(solution)/shard_map/ppermute | solution.py:928
  752.4 33.8 %collective-permute-start.118 = (bf16[64,2304]{1,0:T(8,128)(2,1)}, bf16[64,2304]{1,0:T(8,128)(2,1)}, u32[]{:S(2)}, u32[]{:S(2)}) collective-permute-start(bf16[64,2304]{1,0:T(8,128)(2,1)} %get-tuple-element.346), channel_id=1, source_target_pairs={{0,4},{1,5},{2,6},{3,7},{4,0},{5,1},{6,2},{7,3},{8,12},{9,13},{10,... | collective-permute-start | bytes 884744 | tf_op jit(solution)/shard_map/ppermute | solution.py:928
  753.1 34.3 %collective-permute-start.120 = (bf16[64,2304]{1,0:T(8,128)(2,1)}, bf16[64,2304]{1,0:T(8,128)(2,1)}, u32[]{:S(2)}, u32[]{:S(2)}) collective-permute-start(bf16[64,2304]{1,0:T(8,128)(2,1)} %get-tuple-element.344), channel_id=1, source_target_pairs={{0,2},{1,3},{2,0},{3,1},{4,6},{5,7},{6,4},{7,5},{8,10},{9,11},{10,... | collective-permute-start | bytes 884744 | tf_op jit(solution)/shard_map/ppermute | solution.py:928
  781.3 271.0 %reduce-scatter.10.cloned.1.call-start = ((), (), s32[]{:S(2)}) async-start(), calls=%async_computation.18 | async-start | bytes 6635520 | tf_op jit(solution)/shard_map/reduce_scatter | solution.py:990
  789.6 27.4 %collective-permute-start.121 = (bf16[128,2304]{1,0:T(8,128)(2,1)}, bf16[128,2304]{1,0:T(8,128)(2,1)}, u32[]{:S(2)}, u32[]{:S(2)}) collective-permute-start(bf16[128,2304]{1,0:T(8,128)(2,1)} %pad_maximum_fusion.19), channel_id=1, source_target_pairs={{0,4},{1,5},{2,6},{3,7},{4,0},{5,1},{6,2},{7,3},{8,12},{9,13},{10,... | collective-permute-start | bytes 1769480 | tf_op jit(solution)/shard_map/ppermute | solution.py:928
  791.6 26.4 %collective-permute-start.119 = (bf16[128,2304]{1,0:T(8,128)(2,1)}, bf16[128,2304]{1,0:T(8,128)(2,1)}, u32[]{:S(2)}, u32[]{:S(2)}) collective-permute-start(bf16[128,2304]{1,0:T(8,128)(2,1)} %pad_maximum_fusion.18), channel_id=1, source_target_pairs={{0,2},{1,3},{2,0},{3,1},{4,6},{5,7},{6,4},{7,5},{8,10},{9,11},{10,... | collective-permute-start | bytes 1769480 | tf_op jit(solution)/shard_map/ppermute | solution.py:928
  793.8 35.9 %collective-permute-start.135 = (bf16[128,2304]{1,0:T(8,128)(2,1)}, bf16[128,2304]{1,0:T(8,128)(2,1)}, u32[]{:S(2)}, u32[]{:S(2)}) collective-permute-start(bf16[128,2304]{1,0:T(8,128)(2,1)} %pad_maximum_fusion.21), channel_id=1, source_target_pairs={{0,4},{1,5},{2,6},{3,7},{4,0},{5,1},{6,2},{7,3},{8,12},{9,13},{10,... | collective-permute-start | bytes 1769480 | tf_op jit(solution)/shard_map/ppermute | solution.py:928
  804.4 26.3 %collective-permute-start.133 = (bf16[128,2304]{1,0:T(8,128)(2,1)}, bf16[128,2304]{1,0:T(8,128)(2,1)}, u32[]{:S(2)}, u32[]{:S(2)}) collective-permute-start(bf16[128,2304]{1,0:T(8,128)(2,1)} %pad_maximum_fusion.20), channel_id=1, source_target_pairs={{0,2},{1,3},{2,0},{3,1},{4,6},{5,7},{6,4},{7,5},{8,10},{9,11},{10,... | collective-permute-start | bytes 1769480 | tf_op jit(solution)/shard_map/ppermute | solution.py:928
  811.2 30.9 %collective-permute-start.109 = (bf16[128,2304]{1,0:T(8,128)(2,1)}, bf16[128,2304]{1,0:T(8,128)(2,1)S(1)}, u32[]{:S(2)}, u32[]{:S(2)}) collective-permute-start(bf16[128,2304]{1,0:T(8,128)(2,1)} %get-tuple-element.229.refs_0_), channel_id=1, source_target_pairs={{0,4},{1,5},{2,6},{3,7},{4,0},{5,1},{6,2},{7,3},{8,12},{9,13},{10,... | collective-permute-start | bytes 1769480 | tf_op jit(solution)/shard_map/ppermute | solution.py:928
  817.0 26.2 %collective-permute-start.108 = (bf16[128,2304]{1,0:T(8,128)(2,1)}, bf16[128,2304]{1,0:T(8,128)(2,1)S(1)}, u32[]{:S(2)}, u32[]{:S(2)}) collective-permute-start(bf16[128,2304]{1,0:T(8,128)(2,1)} %get-tuple-element.229.refs_0_), channel_id=1, source_target_pairs={{0,2},{1,3},{2,0},{3,1},{4,6},{5,7},{6,4},{7,5},{8,10},{9,11},{10,... | collective-permute-start | bytes 1769480 | tf_op jit(solution)/shard_map/ppermute | solution.py:928
  823.1 31.8 %collective-permute-start.123 = (bf16[128,2304]{1,0:T(8,128)(2,1)}, bf16[128,2304]{1,0:T(8,128)(2,1)}, u32[]{:S(2)}, u32[]{:S(2)}) collective-permute-start(bf16[128,2304]{1,0:T(8,128)(2,1)} %get-tuple-element.242.refs_0_), channel_id=1, source_target_pairs={{0,4},{1,5},{2,6},{3,7},{4,0},{5,1},{6,2},{7,3},{8,12},{9,13},{10,... | collective-permute-start | bytes 1769480 | tf_op jit(solution)/shard_map/ppermute | solution.py:928
  829.7 27.2 %collective-permute-start.112 = (bf16[128,2304]{1,0:T(8,128)(2,1)}, bf16[128,2304]{1,0:T(8,128)(2,1)}, u32[]{:S(2)}, u32[]{:S(2)}) collective-permute-start(bf16[128,2304]{1,0:T(8,128)(2,1)} %get-tuple-element.229.refs_0_), channel_id=1, source_target_pairs={{0,1},{1,0},{2,3},{3,2},{4,5},{5,4},{6,7},{7,6},{8,9},{9,8},{10,11... | collective-permute-start | bytes 1769480 | tf_op jit(solution)/shard_map/ppermute | solution.py:928
  830.7 27.4 %collective-permute-start.122 = (bf16[128,2304]{1,0:T(8,128)(2,1)}, bf16[128,2304]{1,0:T(8,128)(2,1)S(1)}, u32[]{:S(2)}, u32[]{:S(2)}) collective-permute-start(bf16[128,2304]{1,0:T(8,128)(2,1)} %get-tuple-element.242.refs_0_), channel_id=1, source_target_pairs={{0,2},{1,3},{2,0},{3,1},{4,6},{5,7},{6,4},{7,5},{8,10},{9,11},{10,... | collective-permute-start | bytes 1769480 | tf_op jit(solution)/shard_map/ppermute | solution.py:928
  842.2 25.3 %collective-permute-start.137 = (bf16[128,2304]{1,0:T(8,128)(2,1)}, bf16[128,2304]{1,0:T(8,128)(2,1)S(1)}, u32[]{:S(2)}, u32[]{:S(2)}) collective-permute-start(bf16[128,2304]{1,0:T(8,128)(2,1)} %get-tuple-element.257.refs_0_), channel_id=1, source_target_pairs={{0,4},{1,5},{2,6},{3,7},{4,0},{5,1},{6,2},{7,3},{8,12},{9,13},{10,... | collective-permute-start | bytes 1769480 | tf_op jit(solution)/shard_map/ppermute | solution.py:928
  843.2 25.2 %collective-permute-start.126 = (bf16[128,2304]{1,0:T(8,128)(2,1)S(1)}, bf16[128,2304]{1,0:T(8,128)(2,1)S(1)}, u32[]{:S(2)}, u32[]{:S(2)}) collective-permute-start(bf16[128,2304]{1,0:T(8,128)(2,1)S(1)} %copy-done.41), channel_id=1, source_target_pairs={{0,1},{1,0},{2,3},{3,2},{4,5},{5,4},{6,7},{7,6},{8,9},{9,8},{10,11... | collective-permute-start | bytes 1769480 | tf_op jit(solution)/shard_map/ppermute | solution.py:928
  889.6 47.0 %collective-permute-start.140 = (bf16[128,2304]{1,0:T(8,128)(2,1)}, bf16[128,2304]{1,0:T(8,128)(2,1)}, u32[]{:S(2)}, u32[]{:S(2)}) collective-permute-start(bf16[128,2304]{1,0:T(8,128)(2,1)} %get-tuple-element.257.refs_0_), channel_id=1, source_target_pairs={{0,1},{1,0},{2,3},{3,2},{4,5},{5,4},{6,7},{7,6},{8,9},{9,8},{10,11... | collective-permute-start | bytes 1769480 | tf_op jit(solution)/shard_map/ppermute | solution.py:928
  891.1 45.5 %collective-permute-start.141 = (bf16[128,2304]{1,0:T(8,128)(2,1)}, bf16[128,2304]{1,0:T(8,128)(2,1)}, u32[]{:S(2)}, u32[]{:S(2)}) collective-permute-start(bf16[128,2304]{1,0:T(8,128)(2,1)} %collective-permute-done.136.refs_1_), channel_id=1, source_target_pairs={{0,1},{1,0},{2,3},{3,2},{4,5},{5,4},{6,7},{7,6},{8,9},{9,8},{10,11... | collective-permute-start | bytes 1769480 | tf_op jit(solution)/shard_map/ppermute | solution.py:928
  891.6 45.1 %collective-permute-start.142 = (bf16[128,2304]{1,0:T(8,128)(2,1)S(1)}, bf16[128,2304]{1,0:T(8,128)(2,1)}, u32[]{:S(2)}, u32[]{:S(2)}) collective-permute-start(bf16[128,2304]{1,0:T(8,128)(2,1)S(1)} %collective-permute-done.137.refs_2_), channel_id=1, source_target_pairs={{0,1},{1,0},{2,3},{3,2},{4,5},{5,4},{6,7},{7,6},{8,9},{9,8},{10,11... | collective-permute-start | bytes 1769480 | tf_op jit(solution)/shard_map/ppermute | solution.py:928
  891.7 44.9 %collective-permute-start.143 = (bf16[64,2304]{1,0:T(8,128)(2,1)}, bf16[64,2304]{1,0:T(8,128)(2,1)}, u32[]{:S(2)}, u32[]{:S(2)}) collective-permute-start(bf16[64,2304]{1,0:T(8,128)(2,1)} %collective-permute-done.138.refs_3_), channel_id=1, source_target_pairs={{0,1},{1,0},{2,3},{3,2},{4,5},{5,4},{6,7},{7,6},{8,9},{9,8},{10,11... | collective-permute-start | bytes 884744 | tf_op jit(solution)/shard_map/ppermute | solution.py:928
  892.1 44.6 %collective-permute-start.144 = (bf16[64,2304]{1,0:T(8,128)(2,1)}, bf16[64,2304]{1,0:T(8,128)(2,1)}, u32[]{:S(2)}, u32[]{:S(2)}) collective-permute-start(bf16[64,2304]{1,0:T(8,128)(2,1)} %copy-done.59), channel_id=1, source_target_pairs={{0,1},{1,0},{2,3},{3,2},{4,5},{5,4},{6,7},{7,6},{8,9},{9,8},{10,11... | collective-permute-start | bytes 884744 | tf_op jit(solution)/shard_map/ppermute | solution.py:928
  917.3 52.2 %all-to-all-start.3 = ((bf16[8,72,1152]{2,1,0:T(8,128)(2,1)}), bf16[8,72,1152]{2,1,0:T(8,128)(2,1)S(1)}, u32[]{:S(2)}, u32[]{:S(2)}) async-start(bf16[8,72,1152]{2,1,0:T(8,128)(2,1)} %bitcast.118), calls=%async_computation.5 | async-start | bytes 2654208 | tf_op jit(solution)/shard_map/all_to_all | solution.py:982
  920.9 187.3 %reduce-scatter.12.cloned.1.call-start = ((), (), s32[]{:S(2)}) async-start(), calls=%async_computation.19 | async-start | bytes 2949120 | tf_op jit(solution)/shard_map/reduce_scatter | solution.py:990
  976.7 23.7 %collective-permute-start.145 = (f32[3,1024,256]{2,1,0:T(8,128)}, f32[3,1024,256]{2,1,0:T(8,128)}, u32[]{:S(2)}, u32[]{:S(2)}) collective-permute-start(f32[3,1024,256]{2,1,0:T(8,128)} %pad_maximum_fusion.1), channel_id=1, source_target_pairs={{0,1},{1,0},{2,3},{3,2},{4,5},{5,4},{6,7},{7,6},{8,9},{9,8},{10,11... | collective-permute-start | bytes 9437192 | tf_op jit(solution)/shard_map/ppermute | solution.py:928
  1023.1 56.1 %collective-permute-start.146 = (bf16[512,2304]{1,0:T(8,128)(2,1)}, bf16[512,2304]{1,0:T(8,128)(2,1)}, u32[]{:S(2)}, u32[]{:S(2)}) collective-permute-start(bf16[512,2304]{1,0:T(8,128)(2,1)} %get-tuple-element.287), channel_id=1, source_target_pairs={{0,1},{1,0},{2,3},{3,2},{4,5},{5,4},{6,7},{7,6},{8,9},{9,8},{10,11... | collective-permute-start | bytes 7077896 | tf_op jit(solution)/shard_map/ppermute | solution.py:928
  1049.6 33.4 %collective-permute-start.153 = (bf16[64,2304]{1,0:T(8,128)(2,1)}, bf16[64,2304]{1,0:T(8,128)(2,1)S(1)}, u32[]{:S(2)}, u32[]{:S(2)}) collective-permute-start(bf16[64,2304]{1,0:T(8,128)(2,1)} %get-tuple-element.394), channel_id=1, source_target_pairs={{4,0},{6,1},{0,2},{2,3},{5,4},{7,5},{1,6},{3,7},{12,8},{14,9},{8,1... | collective-permute-start | bytes 884744 | tf_op jit(solution)/shard_map/ppermute | solution.py:1089
  1049.7 45.5 %collective-permute-start.154 = (bf16[64,2304]{1,0:T(8,128)(2,1)}, bf16[64,2304]{1,0:T(8,128)(2,1)S(1)}, u32[]{:S(2)}, u32[]{:S(2)}) collective-permute-start(bf16[64,2304]{1,0:T(8,128)(2,1)} %get-tuple-element.393), channel_id=1, source_target_pairs={{6,0},{0,1},{2,2},{4,3},{7,4},{1,5},{3,6},{5,7},{14,8},{8,9},{10,1... | collective-permute-start | bytes 884744 | tf_op jit(solution)/shard_map/ppermute | solution.py:1089
  1052.3 26.9 %all-to-all-start.4 = ((bf16[8,72,1152]{2,1,0:T(8,128)(2,1)}), bf16[8,72,1152]{2,1,0:T(8,128)(2,1)S(1)}, u32[]{:S(2)}, u32[]{:S(2)}) async-start(bf16[8,72,1152]{2,1,0:T(8,128)(2,1)} %bitcast.428), calls=%async_computation.7 | async-start | bytes 2654208 | tf_op jit(solution)/shard_map/all_to_all | solution.py:982
  1112.6 37.1 %reduce-scatter.14.cloned.1.call-start = ((), (), s32[]{:S(2)}) async-start(), calls=%async_computation.20 | async-start | bytes 1474560 | tf_op jit(solution)/shard_map/reduce_scatter | solution.py:990
  (263 other events, 3223.5 us)
Sparse Core Ops, SparseCore 0:
  25.1 49.8 all-gather.5
  76.5 30.5 all-gather.7
  108.7 98.1 all-gather.9
  208.3 97.4 all-gather.11
  307.3 97.4 all-gather.13
  638.4 92.8 reduce-scatter.5
  781.5 92.8 reduce-scatter.7
  917.4 92.5 reduce-scatter.9
  1052.4 47.5 reduce-scatter.11
  1120.3 29.4 reduce-scatter.13

commit v4 on v3

--- a/solution.py
+++ b/solution.py
@@ -1237,7 +1237,6 @@
     gate_back = tp_columns(gate_sum.reshape(8, d_rows, ff_cols))
     up_back = tp_columns(up_sum.reshape(8, d_rows, ff_cols))
     q_grad, dk, dv = attend_back(qpos, kpos, turns, q, k_all, v_all, o_grad, tok_rows)
-    q_grad, dk, dv, gate_back = lax.optimization_barrier((q_grad, dk, dv, gate_back))
     other = 1 - core
 
     def half_of(values, which):
@@ -1260,8 +1259,10 @@
     qkv_rows = jnp.sum(qkv_round.astype(F32), axis=0).astype(BF)
     qkv_total = (dot_tn(normed, qkv_rows) / qkv_scale).astype(BF)
     qkv_sum = scatter_rows(qkv_total)
+    low, high = project_back(after(qkv_round, qkv_total), qkv_w)
+    normed_parts = tp_scatter(low, high)
     out_total = dot_tn(
-        after(attended, qkv_total).reshape(SLOTS * group_rows, HD),
+        after(attended, low).reshape(SLOTS * group_rows, HD),
         jnp.concatenate([kept[w]["out_round"] for w in widths], axis=0),
     )
     out_total = (out_total / o_scale_all).astype(BF)
@@ -1271,15 +1272,11 @@
     else:
         whole = jnp.zeros((HEADS * HD, model), BF)
         out_pieces = lax.dynamic_update_slice_in_dim(whole, out_total, t_index * HD, 0)
-    low, high = project_back(qkv_round, qkv_w)
-    low, up_back = lax.optimization_barrier((low, up_back))
-    normed_parts = tp_scatter(low, high)
     gate_grad = by_ff_back(gate_back).astype(F32)
     up_grad = by_ff_back(up_back).astype(F32)
     down_grad = down_sum.reshape(ff_rows, model).astype(F32)
-    out_pieces, qkv_sum, gate_grad, up_grad, down_grad = lax.optimization_barrier(
-        (out_pieces, qkv_sum, gate_grad, up_grad, down_grad)
-    )
+    normed_parts, qkv_sum, gate_grad = lax.optimization_barrier((normed_parts, qkv_sum, gate_grad))
+    out_pieces, up_grad, down_grad = lax.optimization_barrier((out_pieces, up_grad, down_grad))
     if whole_heads:
         out_sum = scatter_rows(out_pieces)
     else:

time: 1170 us -> 1180 us (level)
  waiting for transfers between devices: 301 us -> 314 us
    ppermute x10, waiting for transfers between devices: 22.3 us -> 36 us  [swap_all(): return lax.ppermute(values, ALL, [(i, i ^ mask) for i in range(devices)])]
    reduce_scatter x5, waiting for transfers between devices: 7.61 us -> 19.9 us  [scatter_rows(): rows = lax.psum_scatter(grad, 'dp', scatter_dimension=0, tiled=True)]
  transfers between devices with their start and end apart: 174 -> 174, of which waited for: 69 -> 69; matrix products, arithmetic and copies ran while one was open for 20% -> 19% of each run, Pallas kernels for 28% -> 28%
where the time goes in v4:
time: 1180 us; the launch traced here: 1170 us
  Pallas kernels  402 us (34%)
  waiting for transfers between devices  314 us (27%)
  starting transfers between devices  144 us (12%)
  local copies, waits for them, and re-layouts  127 us (11%)
  matrix products  62.4 us (5%)
  other arithmetic  57.9 us (5%)
  blocking collectives  37.1 us (3%)
  between operations  23 us (2%)
    ppermute x142, waiting for transfers between devices, swap(): return lax.ppermute(values, 'fsdp', [(i, i ^ mask) for i in range(width)])  219 us
    pallas_call x3, Pallas kernels, ffn_back(): pl.pallas_call(ffn_back_kernel, grid=(rows // chunk,), in_specs=[wide, bl...  100 us
    ppermute x142, starting transfers between devices, swap(): return lax.ppermute(values, 'fsdp', [(i, i ^ mask) for i in range(width)])  96.8 us
    pallas_call x3, Pallas kernels, ffn_in(): pl.pallas_call(functools.partial(ffn_in_kernel, width, len(pieces)), grid...  65.2 us
    dot_general x4, matrix products, dot_tn(): lax.dot_general(left, right, (((0,), (0,)), ((), ())), preferred_element_...  62.4 us
    pallas_call x3, Pallas kernels, ffn_out(): pl.pallas_call(functools.partial(ffn_out_kernel, width), grid=(rows // ch...  40.6 us
    all_to_all x2, blocking collectives, tp_columns(): lax.all_to_all(blocks, 'fsdp', 0, 0, tiled=True, axis_index_groups=groups)  37.1 us
    ppermute x10, waiting for transfers between devices, swap_all(): return lax.ppermute(values, ALL, [(i, i ^ mask) for i in range(devices)])  36 us
  transfers between devices with their start and end apart: 174, of which 69 were waited for; matrix products, arithmetic and copies ran while one was open for 19% of the time, Pallas kernels for 28%

profile of v4, /device:TPU:0, one launch (start us, length us, event | category | flops | bytes accessed | tf_op | source)
XLA Modules:
  0.0 1167.7 jit_solution(3385465881116753692)
XLA Ops:
  9.4 15.5 %all_to_all.30 = bf16[8,72,512]{2,1,0:T(8,128)(2,1)} all-to-all(bf16[8,72,512]{2,1,0:T(8,128)(2,1)S(1)} %pad_maximum_fusion.3), channel_id=1, replica_groups=mesh['dp'=4,'fsdp'=8] {'fsdp'}, dimensions={0} | all-to-all | bytes 1179648 | tf_op jit(solution)/shard_map/all_to_all | solution.py:982
  30.4 21.6 %all_to_all.31 = bf16[8,72,1152]{2,1,0:T(8,128)(2,1)} all-to-all(bf16[8,72,1152]{2,1,0:T(8,128)(2,1)S(1)} %reshape.531), channel_id=1, replica_groups=mesh['dp'=4,'fsdp'=8] {'fsdp'}, dimensions={0} | all-to-all | bytes 2654208 | tf_op jit(solution)/shard_map/all_to_all | solution.py:982
  67.2 16.2 %all-to-all-done.2 = bf16[8,72,1152]{2,1,0:T(8,128)(2,1)S(1)} async-done(((bf16[8,72,1152]{2,1,0:T(8,128)(2,1)}), bf16[8,72,1152]{2,1,0:T(8,128)(2,1)S(1)}, u32[]{:S(2)}, u32[]{:S(2)}) %all-to-all-start.2) | async-done | bytes 1327136 | tf_op jit(solution)/shard_map/all_to_all | solution.py:982
  86.6 9.7 collective-permute-done.11
  118.2 6.2 join.1.a_ref
  124.4 17.6 %project.1 = (bf16[3,1024,512]{2,1,0:T(8,128)(2,1)}, bf16[3,1024,256]{2,1,0:T(8,128)(2,1)}, f32[3,1024,256]{2,1,0:T(8,128)}, bf16[3,2304,512]{2,1,0:T(8,128)(2,1)}) custom-call(bf16[1024,2304]{1,0:T(8,128)(2,1)} %join.1.a_ref, bf16[2304,512]{1,0:T(8,128)(2,1)} %all-gather.6.cloned.1.call-done.w_hbm, f32[1,512]{1,0:T(1,128)} %bitcast.438, ...), custom_call_target="tpu_custom_call" | custom-call | flops 7247757312 | bytes 19660800 | tf_op jit(solution)/shard_map/project/pallas_call | solution.py:196
  146.2 5.3 collective-permute-start.16
  161.8 7.0 heads.1
  168.8 14.6 %attend.1.o_ref = bf16[3,1024,256]{2,1,0:T(8,128)(2,1)} custom-call(s32[1024,1]{1,0:T(8,128)} %copy.61.qpos_ref, s32[1,1024]{1,0:T(1,128)} %compare_select_fusion.kpos_ref, bf16[3,1024,256]{2,1,0:T(8,128)(2,1)} %get-tuple-element.171.q_ref, bf16[3,1024,256]{2,1,0:T(8,128)(2,1)} %get-tuple-element.173.k_ref, bf16[3,1024,256]{2,1,0:T(8,128)(2,1)} %get-tuple-element.174.v_ref), custom_call_target="tpu_custom_call" | custom-call | flops 3221225472 | bytes 4718592 | tf_op jit(solution)/shard_map/attend/pallas_call | solution.py:136
  183.3 6.0 output_partial.3
  189.3 6.1 output_partial.4
  195.4 6.2 output_partial.5
  205.6 5.1 collective-permute-done.47
  241.5 7.5 collective-permute-done.51.from_y_ref
  255.4 6.4 collective-permute-done.37.from_y_ref
  268.0 6.4 collective-permute-done.23.from_y_ref
  279.7 7.3 collective-permute-done.53.refs_2_
  289.1 10.5 collective-permute-done.39.refs_2_
  307.2 5.0 collective-permute-done.25.refs_2_
  316.0 6.3 collective-permute-done.54.refs_3_
  335.3 22.1 %ffn_in.5 = (bf16[1024,1152]{1,0:T(8,128)(2,1)}, bf16[1024,1152]{1,0:T(8,128)(2,1)}, bf16[1024,1152]{1,0:T(8,128)(2,1)}, bf16[1024,2304]{1,0:T(8,128)(2,1)}, bf1...) custom-call(bf16[128,2304]{1,0:T(8,128)(2,1)} %get-tuple-element.188.refs_0_, ...), custom_call_target="tpu_custom_call" | custom-call | flops 10871635968 | bytes 22413312 | tf_op jit(solution)/shard_map/ffn_in/pallas_call | solution.py:624
  358.6 21.8 %ffn_in.4 = (bf16[1024,1152]{1,0:T(8,128)(2,1)}, bf16[1024,1152]{1,0:T(8,128)(2,1)}, bf16[1024,1152]{1,0:T(8,128)(2,1)}, bf16[1024,2304]{1,0:T(8,128)(2,1)}, bf1...) custom-call(bf16[128,2304]{1,0:T(8,128)(2,1)} %get-tuple-element.183.refs_0_, ...), custom_call_target="tpu_custom_call" | custom-call | flops 10871635968 | bytes 22413312 | tf_op jit(solution)/shard_map/ffn_in/pallas_call | solution.py:624
  381.5 21.3 %ffn_in.3 = (bf16[1024,1152]{1,0:T(8,128)(2,1)}, bf16[1024,1152]{1,0:T(8,128)(2,1)}, bf16[1024,1152]{1,0:T(8,128)(2,1)}, bf16[1024,2304]{1,0:T(8,128)(2,1)}, bf1...) custom-call(bf16[128,2304]{1,0:T(8,128)(2,1)} %get-tuple-element.177.refs_0_, bf16[128,2304]{1,0:T(8,128)(2,1)} %copy-done.70, ...), custom_call_target="tpu_custom_call" | custom-call | flops 10871635968 | bytes 22413312 | tf_op jit(solution)/shard_map/ffn_in/pallas_call | solution.py:624
  404.8 12.9 %ffn_out.3 = (bf16[512,2304]{1,0:T(8,128)(2,1)}, bf16[512,2304]{1,0:T(8,128)(2,1)}, bf16[1152,2304]{1,0:T(8,128)(2,1)}) custom-call(bf16[1024,1152]{1,0:T(8,128)(2,1)} %get-tuple-element.192.h_ref.refs_30_, bf16[1152,2304]{1,0:T(8,128)(2,1)} %all-gather.14.cloned.1.call-done.d_hbm), custom_call_target="tpu_custom_call" | custom-call | flops 5435817984 | bytes 17694720 | tf_op jit(solution)/shard_map/ffn_out/pallas_call | solution.py:728
  417.8 13.8 %ffn_out.4 = (bf16[512,2304]{1,0:T(8,128)(2,1)}, bf16[512,2304]{1,0:T(8,128)(2,1)}, bf16[1152,2304]{1,0:T(8,128)(2,1)}) custom-call(bf16[1024,1152]{1,0:T(8,128)(2,1)} %get-tuple-element.194.h_ref.refs_31_, bf16[1152,2304]{1,0:T(8,128)(2,1)} %all-gather.14.cloned.1.call-done.d_hbm), custom_call_target="tpu_custom_call" | custom-call | flops 5435817984 | bytes 17694720 | tf_op jit(solution)/shard_map/ffn_out/pallas_call | solution.py:728
  449.8 13.9 %ffn_out.5 = (bf16[512,2304]{1,0:T(8,128)(2,1)}, bf16[512,2304]{1,0:T(8,128)(2,1)}, bf16[1152,2304]{1,0:T(8,128)(2,1)}) custom-call(bf16[1024,1152]{1,0:T(8,128)(2,1)} %get-tuple-element.208.h_ref.refs_32_, bf16[1152,2304]{1,0:T(8,128)(2,1)} %all-gather.14.cloned.1.call-done.d_hbm), custom_call_target="tpu_custom_call" | custom-call | flops 5435817984 | bytes 17694720 | tf_op jit(solution)/shard_map/ffn_out/pallas_call | solution.py:728
  468.0 5.6 collective-permute-done.67
  486.8 19.7 %collective-permute-done.65.from_y_ref = bf16[128,2304]{1,0:T(8,128)(2,1)} collective-permute-done((bf16[128,2304]{1,0:T(8,128)(2,1)S(1)}, bf16[128,2304]{1,0:T(8,128)(2,1)}, u32[]{:S(2)}, u32[]{:S(2)}) %collective-permute-start.65) | collective-permute-done | bytes 589856 | tf_op jit(solution)/shard_map/ppermute | solution.py:928
  524.5 11.1 collective-permute-done.86.refs_12_
  537.8 10.5 collective-permute-done.77.refs_2_
  554.7 6.2 collective-permute-done.75.from_y_ref
  565.6 4.3 loss_step.5
  575.3 10.4 collective-permute-done.95.refs_22_
  592.4 6.3 collective-permute-done.96.refs_23_
  599.6 5.0 copy-done.25
  607.1 33.1 %down_grad.1 = (bf16[1152,2304]{1,0:T(8,128)(2,1)}, bf16[1024,2304]{1,0:T(8,128)(2,1)}, bf16[1024,2304]{1,0:T(8,128)(2,1)}, bf16[1024,2304]{1,0:T(8,128)(2,1)}) custom-call(bf16[128,2304]{1,0:T(8,128)(2,1)} %get-tuple-element.215.refs_0_, bf16[128,2304]{1,0:T(8,128)(2,1)} %copy-done.66, bf16[128,2304]{1,0:T(8,128)(2,1)} %copy-done.64, ...), custom_call_target="tpu_custom_call" | custom-call | flops 16307453952 | bytes 40697856 | tf_op jit(solution)/shard_map/down_grad/pallas_call | solution.py:687
  640.3 33.9 %ffn_back.3 = (bf16[512,2304]{1,0:T(8,128)(2,1)}, bf16[512,2304]{1,0:T(8,128)(2,1)}, bf16[1024,1152]{1,0:T(8,128)(2,1)}, bf16[1024,1152]{1,0:T(8,128)(2,1)}, f32[1,1152]{1,0:T(1,128)}, /*index=5*/f32[1,1152]{1,0:T(1,128)}) custom-call(bf16[1024,2304]{1,0:T(8,128)(2,1)} %get-tuple-element.218.dr_ref, bf16[1024,1152]{1,0:T(8,128)(2,1)} %get-tuple-element.219.gate_ref, ...), custom_call_target="tpu_custom_call" | custom-call | flops 16307453952 | bytes 34799616 | tf_op jit(solution)/shard_map/ffn_back/pallas_call | solution.py:822
  674.5 32.9 %ffn_back.4 = (bf16[512,2304]{1,0:T(8,128)(2,1)}, bf16[512,2304]{1,0:T(8,128)(2,1)}, bf16[1024,1152]{1,0:T(8,128)(2,1)}, bf16[1024,1152]{1,0:T(8,128)(2,1)}, f32[1,1152]{1,0:T(1,128)}, /*index=5*/f32[1,1152]{1,0:T(1,128)}) custom-call(bf16[1024,2304]{1,0:T(8,128)(2,1)} %get-tuple-element.229.dr_ref, bf16[1024,1152]{1,0:T(8,128)(2,1)} %get-tuple-element.230.gate_ref, ...), custom_call_target="tpu_custom_call" | custom-call | flops 16307453952 | bytes 34799616 | tf_op jit(solution)/shard_map/ffn_back/pallas_call | solution.py:822
  707.7 33.3 %ffn_back.5 = (bf16[512,2304]{1,0:T(8,128)(2,1)}, bf16[512,2304]{1,0:T(8,128)(2,1)}, bf16[1024,1152]{1,0:T(8,128)(2,1)}, bf16[1024,1152]{1,0:T(8,128)(2,1)}, f32[1,1152]{1,0:T(1,128)}, /*index=5*/f32[1,1152]{1,0:T(1,128)}) custom-call(bf16[1024,2304]{1,0:T(8,128)(2,1)} %get-tuple-element.243.dr_ref, bf16[1024,1152]{1,0:T(8,128)(2,1)} %get-tuple-element.244.gate_ref, ...), custom_call_target="tpu_custom_call" | custom-call | flops 16307453952 | bytes 34799616 | tf_op jit(solution)/shard_map/ffn_back/pallas_call | solution.py:822
  767.8 25.2 %fusion.7 = bf16[2304,1152]{1,0:T(8,128)(2,1)} fusion(bf16[3072,2304]{1,0:T(8,128)(2,1)} %copy-done.25, bf16[1024,1152]{1,0:T(8,128)(2,1)} %get-tuple-element.280, bf16[1024,1152]{1,0:T(8,128)(2,1)} %get-tuple-element.279, bf16[1024,1152]{1,0:T(8,128)(2,1)} %get-tuple-element.278, f32[1152]{0:T(1024)S(1)} %div.93), kind=kOutput, calls=%fused_computation.11 | convolution fusion | flops 16333996032 | bytes 26546688 | tf_op jit(solution)/shard_map/dot_general | solution.py:57
  798.9 5.1 output_back.3
  806.2 5.2 output_back.4
  814.8 5.2 output_back.5
  822.4 4.9 collective-permute-done.108.refs_1_
  827.3 7.8 collective-permute-done.123.refs_2_
  853.1 5.5 collective-permute-done.110.refs_3_
  860.0 4.9 collective-permute-done.124.refs_3_
  873.9 7.8 head_back.3
  881.7 7.6 head_back.4
  889.3 7.7 head_back.5
  899.4 22.6 %attend_back.1 = (f32[3,1024,256]{2,1,0:T(8,128)}, f32[3,1024,256]{2,1,0:T(8,128)}, f32[3,1024,256]{2,1,0:T(8,128)}) custom-call(s32[1024,1]{1,0:T(8,128)} %copy.61.qpos_ref, s32[1,1024]{1,0:T(1,128)} %compare_select_fusion.kpos_ref, f32[1024,128]{1,0:T(8,128)} %get-tuple-element.414.cos_ref.qcos_ref.kcos_ref, ...), custom_call_target="tpu_custom_call" | custom-call | flops 8053063680 | bytes 4718592 | tf_op jit(solution)/shard_map/attend_back/pallas_call | solution.py:150
  951.1 25.3 %fusion.6 = bf16[2304,1152]{1,0:T(8,128)(2,1)} fusion(bf16[3072,2304]{1,0:T(8,128)(2,1)} %copy-done.25, bf16[1024,1152]{1,0:T(8,128)(2,1)} %get-tuple-element.274, bf16[1024,1152]{1,0:T(8,128)(2,1)} %get-tuple-element.273, bf16[1024,1152]{1,0:T(8,128)(2,1)} %get-tuple-element.272, f32[1152]{0:T(1024)S(1)} %div.90), kind=kOutput, calls=%fused_computation.10 | convolution fusion | flops 16333996032 | bytes 26546688 | tf_op jit(solution)/shard_map/dot_general | solution.py:57
  980.8 14.5 %project_back.1 = (bf16[512,2304]{1,0:T(8,128)(2,1)}, bf16[512,2304]{1,0:T(8,128)(2,1)}) custom-call(bf16[3,1024,512]{2,1,0:T(8,128)(2,1)} %get-tuple-element.261.round_ref, bf16[3,2304,512]{2,1,0:T(8,128)(2,1)} %get-tuple-element.262.w_hbm), custom_call_target="tpu_custom_call" | custom-call | flops 7247757312 | bytes 14942208 | tf_op jit(solution)/shard_map/project_back/pallas_call | solution.py:869
  997.3 8.0 fusion.21
  1007.1 5.6 collective-permute-start.152
  1023.0 11.1 collective-permute-done.147
  1034.3 4.3 all-to-all-start.3
  1044.5 13.0 %all-to-all-done.3 = bf16[8,72,1152]{2,1,0:T(8,128)(2,1)} async-done(((bf16[8,72,1152]{2,1,0:T(8,128)(2,1)}), bf16[8,72,1152]{2,1,0:T(8,128)(2,1)}, u32[]{:S(2)}, u32[]{:S(2)}) %all-to-all-start.3) | async-done | bytes 1327136 | tf_op jit(solution)/shard_map/all_to_all | solution.py:982
  1065.1 4.5 reshape.582
  1076.5 9.1 collective-permute-done.155
  1101.1 10.8 collective-permute-done.158
  1120.2 5.9 copy.87
  1126.0 4.5 reshape.586
  1138.9 19.8 %reduce-scatter.14.cloned.1.call-done = bf16[64,2304]{1,0:T(8,128)(2,1)} async-done(((bf16[256,2304]{1,0:T(8,128)(2,1)}), bf16[64,2304]{1,0:T(8,128)(2,1)}) %reduce-scatter.14.cloned.1.call-update) | async-done | bytes 294928 | tf_op jit(solution)/shard_map/reduce_scatter | solution.py:990
  (865 shorter events, 394.4 us)
Async XLA Ops:
  7.2 117.2 %all-gather.6.cloned.1.call-start = ((), (), s32[]{:S(2)}) async-start(), calls=%async_computation.11 | async-start | bytes 2949120 | tf_op jit(solution)/shard_map/all_gather | solution.py:987
  24.9 117.5 %all-gather.8.cloned.1.call-start = ((), (), s32[]{:S(2)}) async-start(), calls=%async_computation.12 | async-start | bytes 1474560 | tf_op jit(solution)/shard_map/all_gather | solution.py:987
  25.7 309.6 %all-gather.10.cloned.1.call-start = ((), (), s32[]{:S(2)}) async-start(), calls=%async_computation.13 | async-start | bytes 6635520 | tf_op jit(solution)/shard_map/all_gather | solution.py:987
  61.4 22.1 %all-to-all-start.2 = ((bf16[8,72,1152]{2,1,0:T(8,128)(2,1)}), bf16[8,72,1152]{2,1,0:T(8,128)(2,1)S(1)}, u32[]{:S(2)}, u32[]{:S(2)}) async-start(bf16[8,72,1152]{2,1,0:T(8,128)(2,1)} %reshape.534), calls=%async_computation.2 | async-start | bytes 2654208 | tf_op jit(solution)/shard_map/all_to_all | solution.py:982
  64.9 270.3 %all-gather.12.cloned.1.call-start = ((), (), s32[]{:S(2)}) async-start(), calls=%async_computation.14 | async-start | bytes 6635520 | tf_op jit(solution)/shard_map/all_gather | solution.py:987
  83.9 23.5 %collective-permute-start = (bf16[128,2304]{1,0:T(8,128)(2,1)S(1)}, bf16[128,2304]{1,0:T(8,128)(2,1)}, u32[]{:S(2)}, u32[]{:S(2)}) collective-permute-start(bf16[128,2304]{1,0:T(8,128)(2,1)S(1)} %fusion.26.refs_0_), channel_id=1, source_target_pairs={{0,2},{1,3},{2,0},{3,1},{4,6},{5,7},{6,4},{7,5},{8,10},{9,11},{10,... | collective-permute-start | bytes 1769480 | tf_op jit(solution)/shard_map/ppermute | solution.py:928
  84.6 320.2 %all-gather.14.cloned.1.call-start = ((), (), s32[]{:S(2)}) async-start(), calls=%async_computation.15 | async-start | bytes 6635520 | tf_op jit(solution)/shard_map/all_gather | solution.py:987
  202.9 564.8 %reduce-scatter.8.cloned.1.call-start = ((), (), s32[]{:S(2)}) async-start(), calls=%async_computation.17 | async-start | bytes 6635520 | tf_op jit(solution)/shard_map/reduce_scatter | solution.py:990
  225.5 23.5 %collective-permute-start.51 = (bf16[128,2304]{1,0:T(8,128)(2,1)S(1)}, bf16[128,2304]{1,0:T(8,128)(2,1)S(1)}, u32[]{:S(2)}, u32[]{:S(2)}) collective-permute-start(bf16[128,2304]{1,0:T(8,128)(2,1)S(1)} %pad_maximum_fusion.9), channel_id=1, source_target_pairs={{0,4},{1,5},{2,6},{3,7},{4,0},{5,1},{6,2},{7,3},{8,12},{9,13},{10,... | collective-permute-start | bytes 1769480 | tf_op jit(solution)/shard_map/ppermute | solution.py:928
  232.6 29.2 %collective-permute-start.37 = (bf16[128,2304]{1,0:T(8,128)(2,1)}, bf16[128,2304]{1,0:T(8,128)(2,1)}, u32[]{:S(2)}, u32[]{:S(2)}) collective-permute-start(bf16[128,2304]{1,0:T(8,128)(2,1)} %pad_maximum_fusion.7), channel_id=1, source_target_pairs={{0,4},{1,5},{2,6},{3,7},{4,0},{5,1},{6,2},{7,3},{8,12},{9,13},{10,... | collective-permute-start | bytes 1769480 | tf_op jit(solution)/shard_map/ppermute | solution.py:928
  236.4 26.9 %collective-permute-start.35 = (bf16[128,2304]{1,0:T(8,128)(2,1)}, bf16[128,2304]{1,0:T(8,128)(2,1)}, u32[]{:S(2)}, u32[]{:S(2)}) collective-permute-start(bf16[128,2304]{1,0:T(8,128)(2,1)} %pad_maximum_fusion.6), channel_id=1, source_target_pairs={{0,2},{1,3},{2,0},{3,1},{4,6},{5,7},{6,4},{7,5},{8,10},{9,11},{10,... | collective-permute-start | bytes 1769480 | tf_op jit(solution)/shard_map/ppermute | solution.py:928
  238.9 35.5 %collective-permute-start.23 = (bf16[128,2304]{1,0:T(8,128)(2,1)}, bf16[128,2304]{1,0:T(8,128)(2,1)}, u32[]{:S(2)}, u32[]{:S(2)}) collective-permute-start(bf16[128,2304]{1,0:T(8,128)(2,1)} %pad_maximum_fusion.5), channel_id=1, source_target_pairs={{0,4},{1,5},{2,6},{3,7},{4,0},{5,1},{6,2},{7,3},{8,12},{9,13},{10,... | collective-permute-start | bytes 1769480 | tf_op jit(solution)/shard_map/ppermute | solution.py:928
  249.0 26.9 %collective-permute-start.21 = (bf16[128,2304]{1,0:T(8,128)(2,1)}, bf16[128,2304]{1,0:T(8,128)(2,1)}, u32[]{:S(2)}, u32[]{:S(2)}) collective-permute-start(bf16[128,2304]{1,0:T(8,128)(2,1)} %pad_maximum_fusion.4), channel_id=1, source_target_pairs={{0,2},{1,3},{2,0},{3,1},{4,6},{5,7},{6,4},{7,5},{8,10},{9,11},{10,... | collective-permute-start | bytes 1769480 | tf_op jit(solution)/shard_map/ppermute | solution.py:928
  254.5 32.5 %collective-permute-start.53 = (bf16[128,2304]{1,0:T(8,128)(2,1)}, bf16[128,2304]{1,0:T(8,128)(2,1)}, u32[]{:S(2)}, u32[]{:S(2)}) collective-permute-start(bf16[128,2304]{1,0:T(8,128)(2,1)} %get-tuple-element.188.refs_0_), channel_id=1, source_target_pairs={{0,4},{1,5},{2,6},{3,7},{4,0},{5,1},{6,2},{7,3},{8,12},{9,13},{10,... | collective-permute-start | bytes 1769480 | tf_op jit(solution)/shard_map/ppermute | solution.py:928
  261.8 26.8 %collective-permute-start.52 = (bf16[128,2304]{1,0:T(8,128)(2,1)}, bf16[128,2304]{1,0:T(8,128)(2,1)}, u32[]{:S(2)}, u32[]{:S(2)}) collective-permute-start(bf16[128,2304]{1,0:T(8,128)(2,1)} %get-tuple-element.188.refs_0_), channel_id=1, source_target_pairs={{0,2},{1,3},{2,0},{3,1},{4,6},{5,7},{6,4},{7,5},{8,10},{9,11},{10,... | collective-permute-start | bytes 1769480 | tf_op jit(solution)/shard_map/ppermute | solution.py:928
  267.1 32.5 %collective-permute-start.39 = (bf16[128,2304]{1,0:T(8,128)(2,1)}, bf16[128,2304]{1,0:T(8,128)(2,1)S(1)}, u32[]{:S(2)}, u32[]{:S(2)}) collective-permute-start(bf16[128,2304]{1,0:T(8,128)(2,1)} %get-tuple-element.183.refs_0_), channel_id=1, source_target_pairs={{0,4},{1,5},{2,6},{3,7},{4,0},{5,1},{6,2},{7,3},{8,12},{9,13},{10,... | collective-permute-start | bytes 1769480 | tf_op jit(solution)/shard_map/ppermute | solution.py:928
  274.4 26.8 %collective-permute-start.38 = (bf16[128,2304]{1,0:T(8,128)(2,1)}, bf16[128,2304]{1,0:T(8,128)(2,1)}, u32[]{:S(2)}, u32[]{:S(2)}) collective-permute-start(bf16[128,2304]{1,0:T(8,128)(2,1)} %get-tuple-element.183.refs_0_), channel_id=1, source_target_pairs={{0,2},{1,3},{2,0},{3,1},{4,6},{5,7},{6,4},{7,5},{8,10},{9,11},{10,... | collective-permute-start | bytes 1769480 | tf_op jit(solution)/shard_map/ppermute | solution.py:928
  275.9 28.7 %collective-permute-start.56 = (bf16[128,2304]{1,0:T(8,128)(2,1)}, bf16[128,2304]{1,0:T(8,128)(2,1)}, u32[]{:S(2)}, u32[]{:S(2)}) collective-permute-start(bf16[128,2304]{1,0:T(8,128)(2,1)} %get-tuple-element.188.refs_0_), channel_id=1, source_target_pairs={{0,1},{1,0},{2,3},{3,2},{4,5},{5,4},{6,7},{7,6},{8,9},{9,8},{10,11... | collective-permute-start | bytes 1769480 | tf_op jit(solution)/shard_map/ppermute | solution.py:928
  288.6 23.6 %collective-permute-start.25 = (bf16[128,2304]{1,0:T(8,128)(2,1)}, bf16[128,2304]{1,0:T(8,128)(2,1)S(1)}, u32[]{:S(2)}, u32[]{:S(2)}) collective-permute-start(bf16[128,2304]{1,0:T(8,128)(2,1)} %get-tuple-element.177.refs_0_), channel_id=1, source_target_pairs={{0,4},{1,5},{2,6},{3,7},{4,0},{5,1},{6,2},{7,3},{8,12},{9,13},{10,... | collective-permute-start | bytes 1769480 | tf_op jit(solution)/shard_map/ppermute | solution.py:928
  301.2 21.2 %collective-permute-start.54 = (bf16[64,2304]{1,0:T(8,128)(2,1)S(1)}, bf16[64,2304]{1,0:T(8,128)(2,1)S(1)}, u32[]{:S(2)}, u32[]{:S(2)}) collective-permute-start(bf16[64,2304]{1,0:T(8,128)(2,1)S(1)} %slice.600), channel_id=1, source_target_pairs={{0,2},{1,3},{2,0},{3,1},{4,6},{5,7},{6,4},{7,5},{8,10},{9,11},{10,... | collective-permute-start | bytes 884744 | tf_op jit(solution)/shard_map/ppermute | solution.py:928
  306.2 20.9 %collective-permute-start.40 = (bf16[64,2304]{1,0:T(8,128)(2,1)S(1)}, bf16[64,2304]{1,0:T(8,128)(2,1)S(1)}, u32[]{:S(2)}, u32[]{:S(2)}) collective-permute-start(bf16[64,2304]{1,0:T(8,128)(2,1)S(1)} %slice.591), channel_id=1, source_target_pairs={{0,2},{1,3},{2,0},{3,1},{4,6},{5,7},{6,4},{7,5},{8,10},{9,11},{10,... | collective-permute-start | bytes 884744 | tf_op jit(solution)/shard_map/ppermute | solution.py:928
  333.2 24.2 %collective-permute-start.27 = (bf16[64,2304]{1,0:T(8,128)(2,1)S(1)}, bf16[64,2304]{1,0:T(8,128)(2,1)S(1)}, u32[]{:S(2)}, u32[]{:S(2)}) collective-permute-start(bf16[64,2304]{1,0:T(8,128)(2,1)S(1)} %slice.581), channel_id=1, source_target_pairs={{0,4},{1,5},{2,6},{3,7},{4,0},{5,1},{6,2},{7,3},{8,12},{9,13},{10,... | collective-permute-start | bytes 884744 | tf_op jit(solution)/shard_map/ppermute | solution.py:928
  334.2 23.9 %collective-permute-start.43 = (bf16[128,2304]{1,0:T(8,128)(2,1)}, bf16[128,2304]{1,0:T(8,128)(2,1)}, u32[]{:S(2)}, u32[]{:S(2)}) collective-permute-start(bf16[128,2304]{1,0:T(8,128)(2,1)} %collective-permute-done.38.refs_1_), channel_id=1, source_target_pairs={{0,1},{1,0},{2,3},{3,2},{4,5},{5,4},{6,7},{7,6},{8,9},{9,8},{10,11... | collective-permute-start | bytes 1769480 | tf_op jit(solution)/shard_map/ppermute | solution.py:928
  334.2 24.3 %collective-permute-start.44 = (bf16[128,2304]{1,0:T(8,128)(2,1)S(1)}, bf16[128,2304]{1,0:T(8,128)(2,1)}, u32[]{:S(2)}, u32[]{:S(2)}) collective-permute-start(bf16[128,2304]{1,0:T(8,128)(2,1)S(1)} %collective-permute-done.39.refs_2_), channel_id=1, source_target_pairs={{0,1},{1,0},{2,3},{3,2},{4,5},{5,4},{6,7},{7,6},{8,9},{9,8},{10,11... | collective-permute-start | bytes 1769480 | tf_op jit(solution)/shard_map/ppermute | solution.py:928
  334.7 22.8 %collective-permute-start.45 = (bf16[64,2304]{1,0:T(8,128)(2,1)S(1)}, bf16[64,2304]{1,0:T(8,128)(2,1)}, u32[]{:S(2)}, u32[]{:S(2)}) collective-permute-start(bf16[64,2304]{1,0:T(8,128)(2,1)S(1)} %collective-permute-done.40.refs_3_), channel_id=1, source_target_pairs={{0,1},{1,0},{2,3},{3,2},{4,5},{5,4},{6,7},{7,6},{8,9},{9,8},{10,11... | collective-permute-start | bytes 884744 | tf_op jit(solution)/shard_map/ppermute | solution.py:928
  334.8 23.2 %collective-permute-start.46 = (bf16[64,2304]{1,0:T(8,128)(2,1)}, bf16[64,2304]{1,0:T(8,128)(2,1)}, u32[]{:S(2)}, u32[]{:S(2)}) collective-permute-start(bf16[64,2304]{1,0:T(8,128)(2,1)} %collective-permute-done.41.refs_4_), channel_id=1, source_target_pairs={{0,1},{1,0},{2,3},{3,2},{4,5},{5,4},{6,7},{7,6},{8,9},{9,8},{10,11... | collective-permute-start | bytes 884744 | tf_op jit(solution)/shard_map/ppermute | solution.py:928
  357.4 23.1 %collective-permute-start.28 = (bf16[128,2304]{1,0:T(8,128)(2,1)S(1)}, bf16[128,2304]{1,0:T(8,128)(2,1)S(1)}, u32[]{:S(2)}, u32[]{:S(2)}) collective-permute-start(bf16[128,2304]{1,0:T(8,128)(2,1)S(1)} %copy-done.128), channel_id=1, source_target_pairs={{0,1},{1,0},{2,3},{3,2},{4,5},{5,4},{6,7},{7,6},{8,9},{9,8},{10,11... | collective-permute-start | bytes 1769480 | tf_op jit(solution)/shard_map/ppermute | solution.py:928
  357.6 23.0 %collective-permute-start.29 = (bf16[128,2304]{1,0:T(8,128)(2,1)S(1)}, bf16[128,2304]{1,0:T(8,128)(2,1)}, u32[]{:S(2)}, u32[]{:S(2)}) collective-permute-start(bf16[128,2304]{1,0:T(8,128)(2,1)S(1)} %collective-permute-done.24.refs_1_), channel_id=1, source_target_pairs={{0,1},{1,0},{2,3},{3,2},{4,5},{5,4},{6,7},{7,6},{8,9},{9,8},{10,11... | collective-permute-start | bytes 1769480 | tf_op jit(solution)/shard_map/ppermute | solution.py:928
  358.0 22.5 %collective-permute-start.30 = (bf16[128,2304]{1,0:T(8,128)(2,1)S(1)}, bf16[128,2304]{1,0:T(8,128)(2,1)}, u32[]{:S(2)}, u32[]{:S(2)}) collective-permute-start(bf16[128,2304]{1,0:T(8,128)(2,1)S(1)} %collective-permute-done.25.refs_2_), channel_id=1, source_target_pairs={{0,1},{1,0},{2,3},{3,2},{4,5},{5,4},{6,7},{7,6},{8,9},{9,8},{10,11... | collective-permute-start | bytes 1769480 | tf_op jit(solution)/shard_map/ppermute | solution.py:928
  358.1 22.4 %collective-permute-start.31 = (bf16[64,2304]{1,0:T(8,128)(2,1)}, bf16[64,2304]{1,0:T(8,128)(2,1)S(1)}, u32[]{:S(2)}, u32[]{:S(2)}) collective-permute-start(bf16[64,2304]{1,0:T(8,128)(2,1)} %collective-permute-done.26.refs_3_), channel_id=1, source_target_pairs={{0,1},{1,0},{2,3},{3,2},{4,5},{5,4},{6,7},{7,6},{8,9},{9,8},{10,11... | collective-permute-start | bytes 884744 | tf_op jit(solution)/shard_map/ppermute | solution.py:928
  358.6 22.0 %collective-permute-start.32 = (bf16[64,2304]{1,0:T(8,128)(2,1)S(1)}, bf16[64,2304]{1,0:T(8,128)(2,1)S(1)}, u32[]{:S(2)}, u32[]{:S(2)}) collective-permute-start(bf16[64,2304]{1,0:T(8,128)(2,1)S(1)} %collective-permute-done.27.refs_4_), channel_id=1, source_target_pairs={{0,1},{1,0},{2,3},{3,2},{4,5},{5,4},{6,7},{7,6},{8,9},{9,8},{10,11... | collective-permute-start | bytes 884744 | tf_op jit(solution)/shard_map/ppermute | solution.py:928
  477.2 36.8 %collective-permute-start.70 = (bf16[128,2304]{1,0:T(8,128)(2,1)}, bf16[128,2304]{1,0:T(8,128)(2,1)S(1)}, u32[]{:S(2)}, u32[]{:S(2)}) collective-permute-start(bf16[128,2304]{1,0:T(8,128)(2,1)} %pad_maximum_fusion.13), channel_id=1, source_target_pairs={{0,4},{1,5},{2,6},{3,7},{4,0},{5,1},{6,2},{7,3},{8,12},{9,13},{10,... | collective-permute-start | bytes 1769480 | tf_op jit(solution)/shard_map/ppermute | solution.py:928
  478.6 35.3 %collective-permute-start.68 = (bf16[128,2304]{1,0:T(8,128)(2,1)}, bf16[128,2304]{1,0:T(8,128)(2,1)S(1)}, u32[]{:S(2)}, u32[]{:S(2)}) collective-permute-start(bf16[128,2304]{1,0:T(8,128)(2,1)} %pad_maximum_fusion.12), channel_id=1, source_target_pairs={{0,2},{1,3},{2,0},{3,1},{4,6},{5,7},{6,4},{7,5},{8,10},{9,11},{10,... | collective-permute-start | bytes 1769480 | tf_op jit(solution)/shard_map/ppermute | solution.py:928
  481.7 24.8 %collective-permute-start.65 = (bf16[128,2304]{1,0:T(8,128)(2,1)S(1)}, bf16[128,2304]{1,0:T(8,128)(2,1)}, u32[]{:S(2)}, u32[]{:S(2)}) collective-permute-start(bf16[128,2304]{1,0:T(8,128)(2,1)S(1)} %pad_maximum_fusion.11), channel_id=1, source_target_pairs={{0,4},{1,5},{2,6},{3,7},{4,0},{5,1},{6,2},{7,3},{8,12},{9,13},{10,... | collective-permute-start | bytes 1769480 | tf_op jit(solution)/shard_map/ppermute | solution.py:928
  481.9 27.9 %collective-permute-start.63 = (bf16[128,2304]{1,0:T(8,128)(2,1)S(1)}, bf16[128,2304]{1,0:T(8,128)(2,1)}, u32[]{:S(2)}, u32[]{:S(2)}) collective-permute-start(bf16[128,2304]{1,0:T(8,128)(2,1)S(1)} %pad_maximum_fusion.10), channel_id=1, source_target_pairs={{0,2},{1,3},{2,0},{3,1},{4,6},{5,7},{6,4},{7,5},{8,10},{9,11},{10,... | collective-permute-start | bytes 1769480 | tf_op jit(solution)/shard_map/ppermute | solution.py:928
  484.8 35.5 %collective-permute-start.72 = (bf16[64,2304]{1,0:T(8,128)(2,1)}, bf16[64,2304]{1,0:T(8,128)(2,1)}, u32[]{:S(2)}, u32[]{:S(2)}) collective-permute-start(bf16[64,2304]{1,0:T(8,128)(2,1)} %get-tuple-element.354), channel_id=1, source_target_pairs={{0,4},{1,5},{2,6},{3,7},{4,0},{5,1},{6,2},{7,3},{8,12},{9,13},{10,... | collective-permute-start | bytes 884744 | tf_op jit(solution)/shard_map/ppermute | solution.py:928
  520.3 33.2 %collective-permute-start.89 = (bf16[128,2304]{1,0:T(8,128)(2,1)}, bf16[128,2304]{1,0:T(8,128)(2,1)S(1)}, u32[]{:S(2)}, u32[]{:S(2)}) collective-permute-start(bf16[128,2304]{1,0:T(8,128)(2,1)} %get-tuple-element.216.refs_10_), channel_id=1, source_target_pairs={{0,1},{1,0},{2,3},{3,2},{4,5},{5,4},{6,7},{7,6},{8,9},{9,8},{10,11... | collective-permute-start | bytes 1769480 | tf_op jit(solution)/shard_map/ppermute | solution.py:928
  520.3 28.0 %collective-permute-start.77 = (bf16[128,2304]{1,0:T(8,128)(2,1)}, bf16[128,2304]{1,0:T(8,128)(2,1)S(1)}, u32[]{:S(2)}, u32[]{:S(2)}) collective-permute-start(bf16[128,2304]{1,0:T(8,128)(2,1)} %get-tuple-element.215.refs_0_), channel_id=1, source_target_pairs={{0,4},{1,5},{2,6},{3,7},{4,0},{5,1},{6,2},{7,3},{8,12},{9,13},{10,... | collective-permute-start | bytes 1769480 | tf_op jit(solution)/shard_map/ppermute | solution.py:928
  521.7 30.2 %collective-permute-start.76 = (bf16[128,2304]{1,0:T(8,128)(2,1)}, bf16[128,2304]{1,0:T(8,128)(2,1)S(1)}, u32[]{:S(2)}, u32[]{:S(2)}) collective-permute-start(bf16[128,2304]{1,0:T(8,128)(2,1)} %get-tuple-element.215.refs_0_), channel_id=1, source_target_pairs={{0,2},{1,3},{2,0},{3,1},{4,6},{5,7},{6,4},{7,5},{8,10},{9,11},{10,... | collective-permute-start | bytes 1769480 | tf_op jit(solution)/shard_map/ppermute | solution.py:928
  536.3 24.6 %collective-permute-start.75 = (bf16[128,2304]{1,0:T(8,128)(2,1)S(1)}, bf16[128,2304]{1,0:T(8,128)(2,1)S(1)}, u32[]{:S(2)}, u32[]{:S(2)}) collective-permute-start(bf16[128,2304]{1,0:T(8,128)(2,1)S(1)} %pad_maximum_fusion.15), channel_id=1, source_target_pairs={{0,4},{1,5},{2,6},{3,7},{4,0},{5,1},{6,2},{7,3},{8,12},{9,13},{10,... | collective-permute-start | bytes 1769480 | tf_op jit(solution)/shard_map/ppermute | solution.py:928
  640.2 336.2 %reduce-scatter.10.cloned.1.call-start = ((), (), s32[]{:S(2)}) async-start(), calls=%async_computation.18 | async-start | bytes 6635520 | tf_op jit(solution)/shard_map/reduce_scatter | solution.py:990
  674.2 67.1 %collective-permute-start.103 = (bf16[512,2304]{1,0:T(8,128)(2,1)}, bf16[512,2304]{1,0:T(8,128)(2,1)}, u32[]{:S(2)}, u32[]{:S(2)}) collective-permute-start(bf16[512,2304]{1,0:T(8,128)(2,1)} %get-tuple-element.225), channel_id=1, source_target_pairs={{0,1},{1,0},{2,3},{3,2},{4,5},{5,4},{6,7},{7,6},{8,9},{9,8},{10,11... | collective-permute-start | bytes 7077896 | tf_op jit(solution)/shard_map/ppermute | solution.py:928
  707.4 39.1 %collective-permute-start.117 = (bf16[512,2304]{1,0:T(8,128)(2,1)}, bf16[512,2304]{1,0:T(8,128)(2,1)}, u32[]{:S(2)}, u32[]{:S(2)}) collective-permute-start(bf16[512,2304]{1,0:T(8,128)(2,1)} %get-tuple-element.236), channel_id=1, source_target_pairs={{0,1},{1,0},{2,3},{3,2},{4,5},{5,4},{6,7},{7,6},{8,9},{9,8},{10,11... | collective-permute-start | bytes 7077896 | tf_op jit(solution)/shard_map/ppermute | solution.py:928
  756.0 42.2 %collective-permute-start.107 = (bf16[128,2304]{1,0:T(8,128)(2,1)}, bf16[128,2304]{1,0:T(8,128)(2,1)}, u32[]{:S(2)}, u32[]{:S(2)}) collective-permute-start(bf16[128,2304]{1,0:T(8,128)(2,1)} %pad_maximum_fusion.17), channel_id=1, source_target_pairs={{0,4},{1,5},{2,6},{3,7},{4,0},{5,1},{6,2},{7,3},{8,12},{9,13},{10,... | collective-permute-start | bytes 1769480 | tf_op jit(solution)/shard_map/ppermute | solution.py:928
  759.8 39.1 %collective-permute-start.105 = (bf16[128,2304]{1,0:T(8,128)(2,1)}, bf16[128,2304]{1,0:T(8,128)(2,1)}, u32[]{:S(2)}, u32[]{:S(2)}) collective-permute-start(bf16[128,2304]{1,0:T(8,128)(2,1)} %pad_maximum_fusion.16), channel_id=1, source_target_pairs={{0,2},{1,3},{2,0},{3,1},{4,6},{5,7},{6,4},{7,5},{8,10},{9,11},{10,... | collective-permute-start | bytes 1769480 | tf_op jit(solution)/shard_map/ppermute | solution.py:928
  762.3 43.0 %collective-permute-start.121 = (bf16[128,2304]{1,0:T(8,128)(2,1)}, bf16[128,2304]{1,0:T(8,128)(2,1)}, u32[]{:S(2)}, u32[]{:S(2)}) collective-permute-start(bf16[128,2304]{1,0:T(8,128)(2,1)} %pad_maximum_fusion.19), channel_id=1, source_target_pairs={{0,4},{1,5},{2,6},{3,7},{4,0},{5,1},{6,2},{7,3},{8,12},{9,13},{10,... | collective-permute-start | bytes 1769480 | tf_op jit(solution)/shard_map/ppermute | solution.py:928
  766.1 40.0 %collective-permute-start.119 = (bf16[128,2304]{1,0:T(8,128)(2,1)}, bf16[128,2304]{1,0:T(8,128)(2,1)}, u32[]{:S(2)}, u32[]{:S(2)}) collective-permute-start(bf16[128,2304]{1,0:T(8,128)(2,1)} %pad_maximum_fusion.18), channel_id=1, source_target_pairs={{0,2},{1,3},{2,0},{3,1},{4,6},{5,7},{6,4},{7,5},{8,10},{9,11},{10,... | collective-permute-start | bytes 1769480 | tf_op jit(solution)/shard_map/ppermute | solution.py:928
  793.0 276.8 %reduce-scatter.6.cloned.1.call-start = ((), (), s32[]{:S(2)}) async-start(), calls=%async_computation.16 | async-start | bytes 2949120 | tf_op jit(solution)/shard_map/reduce_scatter | solution.py:990
  805.3 22.0 %collective-permute-start.108 = (bf16[128,2304]{1,0:T(8,128)(2,1)}, bf16[128,2304]{1,0:T(8,128)(2,1)S(1)}, u32[]{:S(2)}, u32[]{:S(2)}) collective-permute-start(bf16[128,2304]{1,0:T(8,128)(2,1)} %get-tuple-element.227.refs_0_), channel_id=1, source_target_pairs={{0,2},{1,3},{2,0},{3,1},{4,6},{5,7},{6,4},{7,5},{8,10},{9,11},{10,... | collective-permute-start | bytes 1769480 | tf_op jit(solution)/shard_map/ppermute | solution.py:928
  811.3 23.8 %collective-permute-start.123 = (bf16[128,2304]{1,0:T(8,128)(2,1)}, bf16[128,2304]{1,0:T(8,128)(2,1)}, u32[]{:S(2)}, u32[]{:S(2)}) collective-permute-start(bf16[128,2304]{1,0:T(8,128)(2,1)} %get-tuple-element.240.refs_0_), channel_id=1, source_target_pairs={{0,4},{1,5},{2,6},{3,7},{4,0},{5,1},{6,2},{7,3},{8,12},{9,13},{10,... | collective-permute-start | bytes 1769480 | tf_op jit(solution)/shard_map/ppermute | solution.py:928
  812.5 27.3 %collective-permute-start.122 = (bf16[128,2304]{1,0:T(8,128)(2,1)}, bf16[128,2304]{1,0:T(8,128)(2,1)}, u32[]{:S(2)}, u32[]{:S(2)}) collective-permute-start(bf16[128,2304]{1,0:T(8,128)(2,1)} %get-tuple-element.240.refs_0_), channel_id=1, source_target_pairs={{0,2},{1,3},{2,0},{3,1},{4,6},{5,7},{6,4},{7,5},{8,10},{9,11},{10,... | collective-permute-start | bytes 1769480 | tf_op jit(solution)/shard_map/ppermute | solution.py:928
  820.0 25.5 %collective-permute-start.137 = (bf16[128,2304]{1,0:T(8,128)(2,1)}, bf16[128,2304]{1,0:T(8,128)(2,1)S(1)}, u32[]{:S(2)}, u32[]{:S(2)}) collective-permute-start(bf16[128,2304]{1,0:T(8,128)(2,1)} %get-tuple-element.255.refs_0_), channel_id=1, source_target_pairs={{0,4},{1,5},{2,6},{3,7},{4,0},{5,1},{6,2},{7,3},{8,12},{9,13},{10,... | collective-permute-start | bytes 1769480 | tf_op jit(solution)/shard_map/ppermute | solution.py:928
  822.4 24.5 %collective-permute-start.112 = (bf16[128,2304]{1,0:T(8,128)(2,1)S(1)}, bf16[128,2304]{1,0:T(8,128)(2,1)S(1)}, u32[]{:S(2)}, u32[]{:S(2)}) collective-permute-start(bf16[128,2304]{1,0:T(8,128)(2,1)S(1)} %copy-done.34), channel_id=1, source_target_pairs={{0,1},{1,0},{2,3},{3,2},{4,5},{5,4},{6,7},{7,6},{8,9},{9,8},{10,11... | collective-permute-start | bytes 1769480 | tf_op jit(solution)/shard_map/ppermute | solution.py:928
  943.2 147.5 %reduce-scatter.12.cloned.1.call-start = ((), (), s32[]{:S(2)}) async-start(), calls=%async_computation.19 | async-start | bytes 6635520 | tf_op jit(solution)/shard_map/reduce_scatter | solution.py:990
  1007.1 67.7 %collective-permute-start.152 = (bf16[64,2304]{1,0:T(8,128)(2,1)}, bf16[64,2304]{1,0:T(8,128)(2,1)}, u32[]{:S(2)}, u32[]{:S(2)}) collective-permute-start(bf16[64,2304]{1,0:T(8,128)(2,1)} %get-tuple-element.391), channel_id=1, source_target_pairs={{2,0},{4,1},{6,2},{0,3},{3,4},{5,5},{7,6},{1,7},{10,8},{12,9},{14,... | collective-permute-start | bytes 884744 | tf_op jit(solution)/shard_map/ppermute | solution.py:1089
  1012.7 73.1 %collective-permute-start.153 = (bf16[64,2304]{1,0:T(8,128)(2,1)}, bf16[64,2304]{1,0:T(8,128)(2,1)}, u32[]{:S(2)}, u32[]{:S(2)}) collective-permute-start(bf16[64,2304]{1,0:T(8,128)(2,1)} %get-tuple-element.390), channel_id=1, source_target_pairs={{4,0},{6,1},{0,2},{2,3},{5,4},{7,5},{1,6},{3,7},{12,8},{14,9},{8,1... | collective-permute-start | bytes 884744 | tf_op jit(solution)/shard_map/ppermute | solution.py:1089
  1012.7 81.6 %collective-permute-start.154 = (bf16[64,2304]{1,0:T(8,128)(2,1)}, bf16[64,2304]{1,0:T(8,128)(2,1)}, u32[]{:S(2)}, u32[]{:S(2)}) collective-permute-start(bf16[64,2304]{1,0:T(8,128)(2,1)} %get-tuple-element.389), channel_id=1, source_target_pairs={{6,0},{0,1},{2,2},{4,3},{7,4},{1,5},{3,6},{5,7},{14,8},{8,9},{10,1... | collective-permute-start | bytes 884744 | tf_op jit(solution)/shard_map/ppermute | solution.py:1089
  1034.3 23.2 %all-to-all-start.3 = ((bf16[8,72,1152]{2,1,0:T(8,128)(2,1)}), bf16[8,72,1152]{2,1,0:T(8,128)(2,1)}, u32[]{:S(2)}, u32[]{:S(2)}) async-start(bf16[8,72,1152]{2,1,0:T(8,128)(2,1)} %bitcast.422), calls=%async_computation.6 | async-start | bytes 2654208 | tf_op jit(solution)/shard_map/all_to_all | solution.py:982
  1039.4 30.3 %collective-permute-start.150 = (bf16[128,2304]{1,0:T(8,128)(2,1)}, bf16[128,2304]{1,0:T(8,128)(2,1)}, u32[]{:S(2)}, u32[]{:S(2)}) collective-permute-start(bf16[128,2304]{1,0:T(8,128)(2,1)} %pad_maximum_fusion.23), channel_id=1, source_target_pairs={{0,4},{1,5},{2,6},{3,7},{4,0},{5,1},{6,2},{7,3},{8,12},{9,13},{10,... | collective-permute-start | bytes 1769480 | tf_op jit(solution)/shard_map/ppermute | solution.py:928
  1042.2 27.5 %collective-permute-start.148 = (bf16[128,2304]{1,0:T(8,128)(2,1)}, bf16[128,2304]{1,0:T(8,128)(2,1)}, u32[]{:S(2)}, u32[]{:S(2)}) collective-permute-start(bf16[128,2304]{1,0:T(8,128)(2,1)} %pad_maximum_fusion.22), channel_id=1, source_target_pairs={{0,2},{1,3},{2,0},{3,1},{4,6},{5,7},{6,4},{7,5},{8,10},{9,11},{10,... | collective-permute-start | bytes 1769480 | tf_op jit(solution)/shard_map/ppermute | solution.py:928
  1090.7 22.0 %all-to-all-start.5 = ((bf16[8,72,1152]{2,1,0:T(8,128)(2,1)}), bf16[8,72,1152]{2,1,0:T(8,128)(2,1)S(1)}, u32[]{:S(2)}, u32[]{:S(2)}) async-start(bf16[8,72,1152]{2,1,0:T(8,128)(2,1)} %bitcast.423), calls=%async_computation.9 | async-start | bytes 2654208 | tf_op jit(solution)/shard_map/all_to_all | solution.py:982
  1111.9 22.2 %collective-permute-start.159 = (f32[1,1136]{1,0:T(1,128)S(1)}, f32[1,1136]{1,0:T(1,128)S(1)}, u32[]{:S(2)}, u32[]{:S(2)}) collective-permute-start(f32[1,1136]{1,0:T(1,128)S(1)} %slice.678), channel_id=1, source_target_pairs={{0,1},{1,0},{2,3},{3,2},{4,5},{5,4},{6,7},{7,6},{8,9},{9,8},{10,11... | collective-permute-start | bytes 13640 | tf_op jit(solution)/shard_map/ppermute | solution.py:931
  1112.7 23.8 %all-to-all-start.4 = ((bf16[8,72,512]{2,1,0:T(8,128)(2,1)}), bf16[8,72,512]{2,1,0:T(8,128)(2,1)S(1)}, u32[]{:S(2)}, u32[]{:S(2)}) async-start(bf16[8,72,512]{2,1,0:T(8,128)(2,1)} %bitcast.427), calls=%async_computation.7 | async-start | bytes 1179648 | tf_op jit(solution)/shard_map/all_to_all | solution.py:982
  1116.3 42.5 %reduce-scatter.14.cloned.1.call-start = ((), (), s32[]{:S(2)}) async-start(), calls=%async_computation.20 | async-start | bytes 1474560 | tf_op jit(solution)/shard_map/reduce_scatter | solution.py:990
  (264 other events, 2932.6 us)
Sparse Core Ops, SparseCore 0:
  25.1 49.8 all-gather.5
  76.5 30.5 all-gather.7
  108.7 98.1 all-gather.9
  208.3 97.4 all-gather.11
  307.3 97.4 all-gather.13
  640.4 92.9 reduce-scatter.7
  793.1 92.7 reduce-scatter.9
  943.4 45.9 reduce-scatter.5
  991.7 96.2 reduce-scatter.11
  1130.7 28.0 reduce-scatter.13
